TPU v7x, 128 devices: a whole 4x4x4 slice. The times are simulated.
128 devices in a mesh: dp: 16 (over x, y_hi, core), tensor: 8 (over y_lo, z).
Axes of the slice: x: 4, y: 4 (y_hi: 2, y_lo: 2; y = y_hi * 2 + y_lo), z: 4, core: 2. Of those that a mesh axis runs over, the one named last changes fastest.
Arguments:
- tokens: bfloat16 [20480, 1024], P(('dp', 'tensor')), may hold values from -6 to 6
- kept: int32 [64], P('dp'), may hold values from 0 to 256
- w_qkv: bfloat16 [2, 1024, 3, 1024], P(None, 'dp', None, 'tensor'), may hold values from -0.1875 to 0.1875
- w_out: bfloat16 [2, 1024, 1024], P(None, 'tensor', 'dp'), may hold values from -1.75 to 1.75
- w_up: bfloat16 [2, 1024, 4096], P(None, 'dp', 'tensor'), may hold values from -0.1875 to 0.1875
- w_down: bfloat16 [2, 4096, 1024], P(None, 'tensor', 'dp'), may hold values from -0.09375 to 0.09375
- ln_gains: float32 [2, 2, 1024], P(None, None, ('dp', 'tensor')), may hold values from 0.5 to 1.5
- biases: float32 [2, 10, 1024], P(None, None, ('dp', 'tensor')), may hold values from -3 to 3
- grad_out: float32 [20480, 1024], P(('dp', 'tensor')), may hold values from -6 to 6
Outputs:
- activations: float32 [20480, 1024], P(('dp', 'tensor'))
- input_grad: float32 [20480, 1024], P(('dp', 'tensor'))
- qkv_grad: float32 [2, 1024, 3, 1024], P(None, 'dp', None, 'tensor')
- proj_grad: float32 [2, 1024, 1024], P(None, 'tensor', 'dp')
- up_grad: float32 [2, 1024, 4096], P(None, 'dp', 'tensor')
- down_grad: float32 [2, 4096, 1024], P(None, 'tensor', 'dp')
- gain_grad: float32 [2, 2, 1024], P(None, None, ('dp', 'tensor'))
- bias_grad: float32 [2, 10, 1024], P(None, None, ('dp', 'tensor'))
All inputs are finite; a program needn't handle non-finite values.
Results may differ from a plain program's by a relative error of at most 0.022.
Values may be sent and summed in bfloat16 or wider, within the bound.
No kernel may reach another device: no remote copies, remote signals or barrier semaphores. Data moves between devices by JAX's collectives and lax.ppermute only.
A program may use at most 192 MiB of HBM per device.

v0:
```python
import math

import jax
import jax.numpy as jnp
from jax import lax
from jax.sharding import PartitionSpec as P

HEAD = 64
BUFFER = 64


EPS = 1e-06
NEG = -1e30


def sent_to_all(array, axis):
    copies = jnp.broadcast_to(array, (lax.axis_size(axis), *array.shape))
    return lax.all_to_all(copies, axis, split_axis=0, concat_axis=0, tiled=True)


def laid_out(parts, dim):
    shape = list(parts.shape[1:])
    shape[dim] *= parts.shape[0]
    return jnp.moveaxis(parts, 0, dim).reshape(shape)


def gather_directly(array, axis, dim):
    parts = sent_to_all(array, axis)
    return laid_out(parts, dim)


def split_up(array, dim, peers):
    before, after = (array.shape[:dim], array.shape[dim + 1 :])
    return jnp.moveaxis(array.reshape(*before, peers, -1, *after), dim, 0)


def sent_and_summed(array, axis, dim):
    peers = lax.axis_size(axis)
    parts = lax.all_to_all(split_up(array, dim, peers), axis, 0, 0, tiled=True)
    return jnp.sum(parts.astype(jnp.float32), axis=0)


def gather_turned(arrays, axis, dims):
    turned = [jnp.moveaxis(a, dim, 0) for a, dim in zip(arrays, dims)]
    widths = [t[0].size for t in turned]
    both = jnp.concatenate([t.reshape(-1, w) for t, w in zip(turned, widths)], axis=1)
    whole = lax.all_gather(both, axis, axis=0, tiled=True)
    parts = jnp.split(whole, [sum(widths[:k]) for k in range(1, len(widths))], axis=1)
    return tuple(
        (
            jnp.moveaxis(b.reshape(-1, *t.shape[1:]), 0, dim)
            for b, t, dim in zip(parts, turned, dims)
        )
    )


def sum_together(arrays, axis, dims):
    peers = lax.axis_size(axis)
    parts = [split_up(a, dim, peers) for a, dim in zip(arrays, dims)]
    lines = jnp.concatenate([b.reshape(peers, -1) for b in parts], axis=1)
    extent = max(16, -(-lines.shape[1] // 1024) * 8)
    lines = jnp.pad(lines, ((0, 0), (0, extent * 128 - lines.shape[1]))).reshape(-1, 128)
    vector, at, outs = (lax.psum_scatter(lines, axis, tiled=True).reshape(-1), 0, [])
    for b in parts:
        part = b[0]
        outs.append(vector[at : at + part.size].reshape(part.shape))
        at += part.size
    return tuple(outs)


def side_by_side(arrays, axis, dim, along):
    widths = [a.shape[along] for a in arrays]
    both = jnp.concatenate(arrays, axis=along)
    whole = lax.psum_scatter(both, axis, scatter_dimension=dim, tiled=True)
    return tuple(jnp.split(whole, [sum(widths[:k]) for k in range(1, len(widths))], axis=along))


def layer_norm(rows, gain, shift):
    centre = rows - jnp.mean(rows, axis=-1, keepdims=True)
    spread = jnp.mean(centre * centre, axis=-1, keepdims=True)
    return centre * lax.rsqrt(spread + EPS) * gain + shift


def gelu_exact(values):
    return jax.nn.gelu(values, approximate=False)


def gather_rows(normed):
    return gather_directly(normed, "tensor", 0)


def gather_back(cotangent):
    return gather_directly(cotangent, "tensor", 0)


def forward_sum(left, right):
    return lax.psum_scatter(
        jnp.dot(left, right, preferred_element_type=jnp.float32).astype(jnp.bfloat16),
        "tensor",
        scatter_dimension=0,
        tiled=True,
    ).astype(jnp.float32)


def backward_sum(left, right):
    return sent_and_summed(
        lax.dot_general(
            left, right, (((1,), (1,)), ((), ())), preferred_element_type=jnp.float32
        ).astype(jnp.bfloat16),
        "tensor",
        0,
    )


def outer_sum(left, right):
    return lax.dot_general(
        left, right, (((0,), (0,)), ((), ())), preferred_element_type=jnp.float32
    )


def per_device(tokens, kept, w_qkv, w_out, w_up, w_down, ln_gains, biases, grad_out):
    tensor_count = lax.axis_size("tensor")
    tensor_place = lax.axis_index("tensor")
    rows = tokens.shape[0]
    width = tokens.shape[1]
    images = kept.shape[0]
    group = rows * tensor_count
    seq = group // images
    layers = w_qkv.shape[0]
    width_dev = w_qkv.shape[3]
    hidden_dev = w_up.shape[2]
    heads_dev = width_dev // HEAD
    factor = 1.0 / math.sqrt(HEAD)
    gains_all, shifts_all = gather_turned((ln_gains, biases), ("dp", "tensor"), (2, 2))
    position = jnp.arange(seq, dtype=jnp.int32)
    allowed = (position[None, :] < (BUFFER + kept)[:, None])[:, None, None, :]
    head_shape = (images, seq, heads_dev, HEAD)

    def scores_of(query, keys):
        raw = (
            jnp.einsum("ishd,ithd->ihst", query, keys, preferred_element_type=jnp.float32) * factor
        )
        return jnp.where(allowed, raw, NEG)

    state = tokens.astype(jnp.float32)
    saved = []
    for index in range(layers):
        weights = gather_turned(
            (w_qkv[index], w_out[index], w_up[index], w_down[index]), "dp", (0, 1, 0, 1)
        )
        w_q, w_o, w_u, w_d = weights
        shift = shifts_all[index]
        gain = gains_all[index]
        bias_q = lax.dynamic_slice_in_dim(shift[4], tensor_place * width_dev, width_dev)
        bias_v = lax.dynamic_slice_in_dim(shift[5], tensor_place * width_dev, width_dev)
        bias_up = lax.dynamic_slice_in_dim(
            shift[6:10].reshape(-1), tensor_place * hidden_dev, hidden_dev
        )
        first = gather_rows(layer_norm(state, gain[0], shift[0]).astype(jnp.bfloat16))
        stacked = jnp.einsum("gd,dce->gce", first, w_q, preferred_element_type=jnp.float32)
        query = (stacked[:, 0] + bias_q).astype(jnp.bfloat16).reshape(head_shape)
        keys = stacked[:, 1].astype(jnp.bfloat16).reshape(head_shape)
        values = (stacked[:, 2] + bias_v).astype(jnp.bfloat16).reshape(head_shape)
        scores = scores_of(query, keys)
        top = jnp.max(scores, axis=-1, keepdims=True)
        total = top + jnp.log(jnp.sum(jnp.exp(scores - top), axis=-1, keepdims=True))
        probs = jnp.exp(scores - total).astype(jnp.bfloat16)
        mixed = jnp.einsum("ihst,ithd->ishd", probs, values, preferred_element_type=jnp.float32)
        mixed = mixed.reshape(group, width_dev).astype(jnp.bfloat16)
        middle = state + (forward_sum(mixed, w_o) + shift[2])
        second = gather_rows(layer_norm(middle, gain[1], shift[1]).astype(jnp.bfloat16))
        hidden = jnp.dot(second, w_u, preferred_element_type=jnp.float32) + bias_up
        active = gelu_exact(hidden).astype(jnp.bfloat16)
        saved.append(
            (
                state,
                first,
                query,
                keys,
                values,
                total,
                mixed,
                middle,
                second,
                hidden,
                active,
                weights,
            )
        )
        state = middle + (forward_sum(active, w_d) + shift[3])
    grad = grad_out
    qkv_parts = [None] * layers
    proj_parts = [None] * layers
    up_parts = [None] * layers
    down_parts = [None] * layers
    gain_parts = [None] * layers
    bias_parts = [None] * layers
    for index in reversed(range(layers)):
        (
            state_in,
            first,
            query,
            keys,
            values,
            total,
            mixed,
            middle,
            second,
            hidden,
            active,
            kept_weights,
        ) = saved[index]
        w_q, w_o, w_u, w_d = kept_weights
        shift = shifts_all[index]
        gain = gains_all[index]
        grad_down_bias = jnp.sum(grad, axis=0)
        branch_grad = gather_back(grad.astype(jnp.bfloat16))
        down_grad = outer_sum(active, branch_grad)
        active_grad = lax.dot_general(
            branch_grad, w_d, (((1,), (1,)), ((), ())), preferred_element_type=jnp.float32
        )
        hidden_pull = jax.vjp(gelu_exact, hidden)[1]
        hidden_grad = hidden_pull(active_grad)[0].astype(jnp.bfloat16)
        grad_up_bias = jnp.sum(hidden_grad.astype(jnp.float32), axis=0)
        up_grad = outer_sum(second, hidden_grad)
        second_grad = backward_sum(hidden_grad, w_u)
        norm_pull = jax.vjp(layer_norm, middle, gain[1], shift[1])[1]
        middle_part, gain_two, shift_two = norm_pull(second_grad)
        grad_mid = grad + middle_part
        grad_out_bias = jnp.sum(grad_mid, axis=0)
        mix_grad_all = gather_back(grad_mid.astype(jnp.bfloat16))
        proj_grad = outer_sum(mixed, mix_grad_all)
        mixed_grad = lax.dot_general(
            mix_grad_all, w_o, (((1,), (1,)), ((), ())), preferred_element_type=jnp.float32
        )
        mixed_grad = mixed_grad.astype(jnp.bfloat16).reshape(head_shape)
        scores = scores_of(query, keys)
        probs_full = jnp.exp(scores - total)
        probs = probs_full.astype(jnp.bfloat16)
        value_grad = jnp.einsum(
            "ihst,ishd->ithd", probs, mixed_grad, preferred_element_type=jnp.float32
        ).astype(jnp.bfloat16)
        prob_grad = jnp.einsum(
            "ishd,ithd->ihst", mixed_grad, values, preferred_element_type=jnp.float32
        )
        row_dot = jnp.sum(probs_full * prob_grad, axis=-1, keepdims=True)
        score_grad = (probs_full * (prob_grad - row_dot)).astype(jnp.bfloat16)
        query_grad = (
            jnp.einsum("ihst,ithd->ishd", score_grad, keys, preferred_element_type=jnp.float32)
            * factor
        ).astype(jnp.bfloat16)
        key_grad = (
            jnp.einsum("ihst,ishd->ithd", score_grad, query, preferred_element_type=jnp.float32)
            * factor
        ).astype(jnp.bfloat16)
        query_grad = query_grad.reshape(group, width_dev)
        key_grad = key_grad.reshape(group, width_dev)
        value_grad = value_grad.reshape(group, width_dev)
        triple_grad = jnp.stack([query_grad, key_grad, value_grad], axis=1)
        grad_q_bias = jnp.sum(query_grad.astype(jnp.float32), axis=0)
        grad_v_bias = jnp.sum(value_grad.astype(jnp.float32), axis=0)
        qkv_grad = jnp.einsum("gd,gce->dce", first, triple_grad, preferred_element_type=jnp.float32)
        first_grad = backward_sum(
            triple_grad.reshape(group, 3 * width_dev), w_q.reshape(width, 3 * width_dev)
        )
        first_pull = jax.vjp(layer_norm, state_in, gain[0], shift[0])[1]
        state_part, gain_one, shift_one = first_pull(first_grad)
        grad = grad_mid + state_part
        shards = tuple(
            (
                part.astype(jnp.float32)
                for part in sum_together(
                    (
                        qkv_grad.astype(jnp.bfloat16),
                        proj_grad.astype(jnp.bfloat16),
                        up_grad.astype(jnp.bfloat16),
                        down_grad.astype(jnp.bfloat16),
                    ),
                    "dp",
                    (0, 1, 0, 1),
                )
            )
        )
        qkv_parts[index], proj_parts[index], up_parts[index], down_parts[index] = shards
        placed_q = lax.dynamic_update_slice_in_dim(
            jnp.zeros((width,), jnp.float32), grad_q_bias, tensor_place * width_dev, 0
        )
        placed_v = lax.dynamic_update_slice_in_dim(
            jnp.zeros((width,), jnp.float32), grad_v_bias, tensor_place * width_dev, 0
        )
        placed_up = lax.dynamic_update_slice_in_dim(
            jnp.zeros((hidden_dev * tensor_count,), jnp.float32),
            grad_up_bias,
            tensor_place * hidden_dev,
            0,
        )
        gain_parts[index] = jnp.stack([gain_one, gain_two])
        bias_parts[index] = jnp.concatenate(
            [
                jnp.stack(
                    [shift_one, shift_two, grad_out_bias, grad_down_bias, placed_q, placed_v]
                ),
                placed_up.reshape(-1, width),
            ],
            axis=0,
        )
    gain_grad, bias_grad = side_by_side(
        (jnp.stack(gain_parts), jnp.stack(bias_parts)), ("dp", "tensor"), 2, 1
    )
    return (
        state,
        grad,
        jnp.stack(qkv_parts),
        jnp.stack(proj_parts),
        jnp.stack(up_parts),
        jnp.stack(down_parts),
        gain_grad,
        bias_grad,
    )


def solution(mesh):
    in_specs = (
        P(("dp", "tensor"), None),
        P("dp"),
        P(None, "dp", None, "tensor"),
        P(None, "tensor", "dp"),
        P(None, "dp", "tensor"),
        P(None, "tensor", "dp"),
        P(None, None, ("dp", "tensor")),
        P(None, None, ("dp", "tensor")),
        P(("dp", "tensor"), None),
    )
    out_specs = (
        P(("dp", "tensor"), None),
        P(("dp", "tensor"), None),
        P(None, "dp", None, "tensor"),
        P(None, "tensor", "dp"),
        P(None, "dp", "tensor"),
        P(None, "tensor", "dp"),
        P(None, None, ("dp", "tensor")),
        P(None, None, ("dp", "tensor")),
    )
    return jax.shard_map(
        per_device, mesh=mesh, in_specs=in_specs, out_specs=out_specs, check_vma=False
    )
```

profile of v0, /device:TPU:0, one launch (start us, length us, event | category | flops | bytes accessed | tf_op | source)
XLA Modules:
  0.0 1296.3 jit_solution(7533668736872293640)
XLA Ops:
  13.0 323.1 %all_gather.9 = f32[1024,24]{1,0:T(8,128)S(1)} all-gather(f32[8,24]{1,0:T(8,128)S(1)} %pad_maximum_fusion.4), channel_id=1, replica_groups=mesh['dp'=16,'tensor'=8] {'dp','tensor'}, dimensions={0}, use_global_device_ids=true | all-gather | bytes 99072 | tf_op jit(solution)/shard_map/all_gather | solution.py:47
  340.6 4.4 all-to-all-start
  346.9 17.2 %all-to-all-done = bf16[8,160,1024]{2,1,0:T(8,128)(2,1)} async-done(((bf16[8,160,1024]{2,1,0:T(8,128)(2,1)}), bf16[8,160,1024]{2,1,0:T(8,128)(2,1)}, u32[]{:S(2)}, u32[]{:S(2)}) %all-to-all-start) | async-done | bytes 2621472 | tf_op jit(solution)/shard_map/all_to_all | solution.py:18
  364.0 3.3 fusion.109
  374.3 3.5 convolution_convert_fusion.7
  377.9 40.4 %reduce-scatter.7.cloned.1.call-done = bf16[160,1024]{1,0:T(8,128)(2,1)} async-done(((bf16[1280,1024]{1,0:T(8,128)(2,1)}), bf16[160,1024]{1,0:T(8,128)(2,1)}) %reduce-scatter.7.cloned.1.call-update) | async-done | bytes 327696 | tf_op jit(solution)/shard_map/reduce_scatter | solution.py:97
  423.8 3.6 all-to-all-start.1
  427.5 10.9 reduce-scatter.9.cloned.1.call-start
  438.5 16.7 %all-to-all-done.1 = bf16[8,160,1024]{2,1,0:T(8,128)(2,1)S(1)} async-done(((bf16[8,160,1024]{2,1,0:T(8,128)(2,1)}), bf16[8,160,1024]{2,1,0:T(8,128)(2,1)S(1)}, u32[]{:S(2)}, u32[]{:S(2)}) %all-to-all-start.1) | async-done | bytes 2621472 | tf_op jit(solution)/shard_map/all_to_all | solution.py:18
  455.2 9.9 multiply_convert_fusion.3
  466.2 4.3 convolution_convert_fusion.6
  471.4 43.5 %reduce-scatter.9.cloned.1.call-done = bf16[160,1024]{1,0:T(8,128)(2,1)} async-done(((bf16[1280,1024]{1,0:T(8,128)(2,1)}), bf16[160,1024]{1,0:T(8,128)(2,1)}) %reduce-scatter.9.cloned.1.call-update) | async-done | bytes 327696 | tf_op jit(solution)/shard_map/reduce_scatter | solution.py:97
  518.4 4.4 all-to-all-start.2
  524.4 45.8 %all-gather.5.cloned.1.call-done = bf16[1024,1536]{1,0:T(8,128)(2,1)} async-done(((bf16[64,1536]{1,0:T(8,128)(2,1)}), bf16[1024,1536]{1,0:T(8,128)(2,1)}) %all-gather.5.cloned.1.call-update) | async-done | bytes 3145744 | tf_op jit(solution)/shard_map/all_gather | solution.py:47
  571.7 3.3 fusion.110
  579.3 2.2 copy.228
  581.4 2.5 squeeze.50
  589.5 3.5 convolution_convert_fusion.5
  593.1 43.4 %reduce-scatter.11.cloned.1.call-done = bf16[160,1024]{1,0:T(8,128)(2,1)} async-done(((bf16[1280,1024]{1,0:T(8,128)(2,1)}), bf16[160,1024]{1,0:T(8,128)(2,1)}) %reduce-scatter.11.cloned.1.call-update) | async-done | bytes 327696 | tf_op jit(solution)/shard_map/reduce_scatter | solution.py:97
  640.6 4.6 all-to-all-start.3
  645.2 27.4 %all-to-all-done.3 = bf16[8,160,1024]{2,1,0:T(8,128)(2,1)} async-done(((bf16[8,160,1024]{2,1,0:T(8,128)(2,1)}), bf16[8,160,1024]{2,1,0:T(8,128)(2,1)}, u32[]{:S(2)}, u32[]{:S(2)}) %all-to-all-start.3) | async-done | bytes 2621472 | tf_op jit(solution)/shard_map/all_to_all | solution.py:18
  674.4 4.4 all-to-all-start.4
  679.3 10.1 multiply_convert_fusion.2
  690.4 4.3 convolution_convert_fusion.4
  694.7 18.2 %all-to-all-done.4 = bf16[8,160,1024]{2,1,0:T(8,128)(2,1)} async-done(((bf16[8,160,1024]{2,1,0:T(8,128)(2,1)}), bf16[8,160,1024]{2,1,0:T(8,128)(2,1)}, u32[]{:S(2)}, u32[]{:S(2)}) %all-to-all-start.4) | async-done | bytes 2621472 | tf_op jit(solution)/shard_map/all_to_all | solution.py:18
  712.9 6.7 convert_reduce_fusion.8
  719.6 3.3 convolution_convert_fusion.3
  722.9 42.5 %all_to_all.60 = bf16[8,160,1024]{2,1,0:T(8,128)(2,1)S(1)} all-to-all(bf16[8,160,1024]{2,1,0:T(8,128)(2,1)S(1)} %bitcast.213), channel_id=1, replica_groups=mesh['dp'=16,'tensor'=8] {'tensor'}, dimensions={0} | all-to-all | bytes 5242880 | tf_op jit(solution)/shard_map/all_to_all | solution.py:39
  767.6 2.1 fusion.96
  770.9 36.1 %all_to_all.61 = bf16[8,160,1024]{2,1,0:T(8,128)(2,1)S(1)} all-to-all(bf16[8,160,1024]{2,1,0:T(8,128)(2,1)S(1)} %broadcast_in_dim.112), channel_id=1, replica_groups=mesh['dp'=16,'tensor'=8] {'tensor'}, dimensions={0} | all-to-all | bytes 5242880 | tf_op jit(solution)/shard_map/all_to_all | solution.py:18
  808.4 2.5 convolution_convert_fusion.9
  813.3 4.9 convert_reduce_fusion.11
  833.0 3.0 convolution_convert_fusion.1
  836.0 33.4 %all_to_all.62 = bf16[8,160,1024]{2,1,0:T(8,128)(2,1)S(1)} all-to-all(bf16[8,160,1024]{2,1,0:T(8,128)(2,1)S(1)} %bitcast.212), channel_id=1, replica_groups=mesh['dp'=16,'tensor'=8] {'tensor'}, dimensions={0} | all-to-all | bytes 5242880 | tf_op jit(solution)/shard_map/all_to_all | solution.py:39
  873.8 32.9 %all_to_all.63 = bf16[8,160,1024]{2,1,0:T(8,128)(2,1)S(1)} all-to-all(bf16[8,160,1024]{2,1,0:T(8,128)(2,1)S(1)} %broadcast_in_dim.115), channel_id=1, replica_groups=mesh['dp'=16,'tensor'=8] {'tensor'}, dimensions={0} | all-to-all | bytes 5242880 | tf_op jit(solution)/shard_map/all_to_all | solution.py:18
  906.7 3.1 convert_reduce_fusion.9
  909.8 3.1 convolution_convert_fusion.2
  912.9 4.6 all-to-all-start.9
  917.5 3.8 convolution_convert_fusion.11
  922.6 3.3 convolution_convert_fusion.10
  927.2 2.9 copy.280
  930.2 3.7 reshape.561
  937.0 3.5 convolution_convert_fusion.14
  942.8 2.2 all-to-all-done.9
  945.0 3.7 convert_reduce_fusion.2
  953.6 4.4 all-to-all-start.10
  960.4 2.6 reshape.562
  963.1 25.9 %all-to-all-done.10 = bf16[8,160,1024]{2,1,0:T(8,128)(2,1)} async-done(((bf16[8,160,1024]{2,1,0:T(8,128)(2,1)}), bf16[8,160,1024]{2,1,0:T(8,128)(2,1)}, u32[]{:S(2)}, u32[]{:S(2)}) %all-to-all-start.10) | async-done | bytes 2621472 | tf_op jit(solution)/shard_map/all_to_all | solution.py:18
  989.0 2.6 convolution_convert_fusion.8
  992.4 4.8 convert_reduce_fusion.13
  1009.5 4.2 convolution_convert_fusion
  1013.8 4.6 all-to-all-start.11
  1020.2 4.8 convolution_convert_fusion.13
  1025.0 2.3 reshape_reshape.13
  1027.4 3.8 convolution_convert_fusion.12
  1033.8 2.5 reshape.556
  1036.3 2.4 convolution_convert_fusion.21
  1040.5 3.3 convolution_convert_fusion.15
  1046.1 4.9 all-to-all-done.11
  1051.0 3.1 convert_reduce_fusion
  1057.1 2.0 pad_maximum_fusion
  1059.1 2.6 reshape.557
  1065.7 138.9 %all-reduce.3.cloned.1.call-done = f32[2,12,1024]{1,0,2:T(2,128)} async-done(((f32[2,12,1024]{1,0,2:T(2,128)}), f32[2,12,1024]{1,0,2:T(2,128)}) %all-reduce.3.cloned.1.call-update) | async-done | bytes 98320
  1207.4 76.3 %reduce-scatter.15.cloned.1.call-done = bf16[768,128]{1,0:T(8,128)(2,1)} async-done(((bf16[12288,128]{1,0:T(8,128)(2,1)}), bf16[768,128]{1,0:T(8,128)(2,1)}) %reduce-scatter.15.cloned.1.call-update) | async-done | bytes 196624 | tf_op jit(solution)/shard_map/reduce_scatter | solution.py:63
  (406 shorter events, 128.5 us)
Async XLA Ops:
  7.2 329.6 %copy-start.4 = (bf16[160,1024]{1,0:T(8,128)(2,1)S(1)}, bf16[160,1024]{1,0:T(8,128)(2,1)}, u32[]{:S(2)}) copy-start(bf16[160,1024]{1,0:T(8,128)(2,1)} %param.9) | copy-start | bytes 983044
  7.2 338.2 %all-gather.3.cloned.1.call-start = ((), (), s32[]{:S(2)}) async-start(), calls=%async_computation.18 | async-start | bytes 3342336 | tf_op jit(solution)/shard_map/all_gather | solution.py:47
  337.7 83.0 %copy-start.45 = (f32[1,1,1024]{2,1,0:T(1,128)}, f32[1,1,1024]{2,1,0:T(1,128)S(1)}, u32[]{:S(2)}) copy-start(f32[1,1,1024]{2,1,0:T(1,128)S(1)} %get-tuple-element.109) | copy-start | bytes 12292
  340.6 4.7 copy-start.76
  340.6 23.4 %all-to-all-start = ((bf16[8,160,1024]{2,1,0:T(8,128)(2,1)}), bf16[8,160,1024]{2,1,0:T(8,128)(2,1)}, u32[]{:S(2)}, u32[]{:S(2)}) async-start(bf16[8,160,1024]{2,1,0:T(8,128)(2,1)} %broadcast_in_dim.103), calls=%async_computation | async-start | bytes 5242880 | tf_op jit(solution)/shard_map/all_to_all | solution.py:18
  345.0 73.3 %reduce-scatter.7.cloned.1.call-start = ((), (), s32[]{:S(2)}) async-start(), calls=%async_computation.19 | async-start | bytes 2949120 | tf_op jit(solution)/shard_map/reduce_scatter | solution.py:97
  419.5 4.4 copy-start.48
  423.8 31.3 %all-to-all-start.1 = ((bf16[8,160,1024]{2,1,0:T(8,128)(2,1)}), bf16[8,160,1024]{2,1,0:T(8,128)(2,1)S(1)}, u32[]{:S(2)}, u32[]{:S(2)}) async-start(bf16[8,160,1024]{2,1,0:T(8,128)(2,1)} %broadcast_in_dim.106), calls=%async_computation.2 | async-start | bytes 5242880 | tf_op jit(solution)/shard_map/all_to_all | solution.py:18
  427.5 87.4 %reduce-scatter.9.cloned.1.call-start = ((), (), s32[]{:S(2)}) async-start(), calls=%async_computation.20 | async-start | bytes 2949120 | tf_op jit(solution)/shard_map/reduce_scatter | solution.py:97
  455.2 9.9 copy-start.23
  470.6 44.3 %copy-start.5 = (bf16[160,1024]{1,0:T(8,128)(2,1)S(1)}, bf16[160,1024]{1,0:T(8,128)(2,1)}, u32[]{:S(2)}) copy-start(bf16[160,1024]{1,0:T(8,128)(2,1)} %reduce-scatter.7.cloned.1.call-done) | copy-start | bytes 983044
  470.6 99.6 %all-gather.5.cloned.1.call-start = ((), (), s32[]{:S(2)}) async-start(), calls=%async_computation.21 | async-start | bytes 3342336 | tf_op jit(solution)/shard_map/all_gather | solution.py:47
  518.4 53.3 %all-to-all-start.2 = ((bf16[8,160,1024]{2,1,0:T(8,128)(2,1)}), bf16[8,160,1024]{2,1,0:T(8,128)(2,1)}, u32[]{:S(2)}, u32[]{:S(2)}) async-start(bf16[8,160,1024]{2,1,0:T(8,128)(2,1)} %broadcast_in_dim.107), calls=%async_computation.4 | async-start | bytes 5242880 | tf_op jit(solution)/shard_map/all_to_all | solution.py:18
  522.8 113.6 %reduce-scatter.11.cloned.1.call-start = ((), (), s32[]{:S(2)}) async-start(), calls=%async_computation.22 | async-start | bytes 2949120 | tf_op jit(solution)/shard_map/reduce_scatter | solution.py:97
  589.5 46.9 %copy-start.24 = (f32[160,1024]{1,0:T(8,128)S(1)}, f32[160,1024]{1,0:T(8,128)}, u32[]{:S(2)}) copy-start(f32[160,1024]{1,0:T(8,128)} %param.17) | copy-start | bytes 1966084
  640.6 32.1 %copy-start.39 = (bf16[160,1024]{1,0:T(8,128)(2,1)S(1)}, bf16[160,1024]{1,0:T(8,128)(2,1)}, u32[]{:S(2)}) copy-start(bf16[160,1024]{1,0:T(8,128)(2,1)} %get-tuple-element.133) | copy-start | bytes 983044
  640.6 32.1 %all-to-all-start.3 = ((bf16[8,160,1024]{2,1,0:T(8,128)(2,1)}), bf16[8,160,1024]{2,1,0:T(8,128)(2,1)}, u32[]{:S(2)}, u32[]{:S(2)}) async-start(bf16[8,160,1024]{2,1,0:T(8,128)(2,1)} %broadcast_in_dim.108), calls=%async_computation.6 | async-start | bytes 5242880 | tf_op jit(solution)/shard_map/all_to_all | solution.py:18
  674.4 38.5 %all-to-all-start.4 = ((bf16[8,160,1024]{2,1,0:T(8,128)(2,1)}), bf16[8,160,1024]{2,1,0:T(8,128)(2,1)}, u32[]{:S(2)}, u32[]{:S(2)}) async-start(bf16[8,160,1024]{2,1,0:T(8,128)(2,1)} %broadcast_in_dim.109), calls=%async_computation.8 | async-start | bytes 5242880 | tf_op jit(solution)/shard_map/all_to_all | solution.py:18
  678.9 88.8 %reduce-scatter.13.cloned.1.call-start = ((), (), s32[]{:S(2)}) async-start(), calls=%async_computation.23 | async-start | bytes 2949120 | tf_op jit(solution)/shard_map/reduce_scatter | solution.py:97
  813.3 4.9 copy-start.3
  813.3 5.0 copy-start.32
  813.3 5.0 copy-start.33
  831.6 4.4 copy-start.26
  873.4 33.3 %copy-start.12 = (f32[160,1024]{1,0:T(8,128)}, f32[160,1024]{1,0:T(8,128)S(1)}, u32[]{:S(2)}) copy-start(f32[160,1024]{1,0:T(8,128)S(1)} %get-tuple-element.57) | copy-start | bytes 1966084
  873.4 33.3 %copy-start.82 = (f32[1280,512]{1,0:T(8,128)S(1)}, f32[1280,512]{1,0:T(8,128)}, u32[]{:S(2)}) copy-start(f32[1280,512]{1,0:T(8,128)} %get-tuple-element.113) | copy-start | bytes 7864324
  873.5 33.3 %copy-start.81 = (f32[1280,512]{1,0:T(8,128)S(1)}, f32[1280,512]{1,0:T(8,128)}, u32[]{:S(2)}) copy-start(f32[1280,512]{1,0:T(8,128)} %get-tuple-element.73) | copy-start | bytes 7864324
  873.8 32.9 %copy-start.40 = (bf16[1024,1536]{1,0:T(8,128)(2,1)S(1)}, bf16[1024,1536]{1,0:T(8,128)(2,1)}, u32[]{:S(2)}) copy-start(bf16[1024,1536]{1,0:T(8,128)(2,1)} %all-gather.3.cloned.1.call-done) | copy-start | bytes 9437188
  912.9 32.1 %all-to-all-start.9 = ((bf16[8,160,1024]{2,1,0:T(8,128)(2,1)}), bf16[8,160,1024]{2,1,0:T(8,128)(2,1)}, u32[]{:S(2)}, u32[]{:S(2)}) async-start(bf16[8,160,1024]{2,1,0:T(8,128)(2,1)} %bitcast.47), calls=%async_computation.13 | async-start | bytes 5242880 | tf_op jit(solution)/shard_map/all_to_all | solution.py:39
  917.5 5.1 copy-start.38
  927.2 6.6 copy-start.9
  941.2 7.5 copy-start.46
  941.2 7.5 copy-start.49
  942.8 6.2 copy-start.68
  942.8 6.2 copy-start.53
  942.8 7.2 copy-start.13
  953.6 35.4 %all-to-all-start.10 = ((bf16[8,160,1024]{2,1,0:T(8,128)(2,1)}), bf16[8,160,1024]{2,1,0:T(8,128)(2,1)}, u32[]{:S(2)}, u32[]{:S(2)}) async-start(bf16[8,160,1024]{2,1,0:T(8,128)(2,1)} %broadcast_in_dim.118), calls=%async_computation.14 | async-start | bytes 5242880 | tf_op jit(solution)/shard_map/all_to_all | solution.py:18
  958.0 103.7 %reduce-scatter.17.cloned.1.call-start = ((), (), s32[]{:S(2)}) async-start(), calls=%async_computation.25 | async-start | bytes 3342336 | tf_op jit(solution)/shard_map/reduce_scatter | solution.py:63
  992.4 4.9 copy-start.1
  992.4 4.8 copy-start.30
  1001.7 4.9 copy-start.17
  1008.9 4.8 copy-start.27
  1013.7 4.9 copy-start.72
  1013.7 5.2 copy-start.77
  1013.7 5.3 copy-start.74
  1013.7 5.4 copy-start.56
  1013.7 5.4 copy-start.58
  1013.7 5.5 copy-start.54
  1013.7 5.5 copy-start.55
  1013.8 5.6 copy-start.73
  1013.8 37.3 %all-to-all-start.11 = ((bf16[8,160,1024]{2,1,0:T(8,128)(2,1)}), bf16[8,160,1024]{2,1,0:T(8,128)(2,1)}, u32[]{:S(2)}, u32[]{:S(2)}) async-start(bf16[8,160,1024]{2,1,0:T(8,128)(2,1)} %bitcast.53), calls=%async_computation.15 | async-start | bytes 5242880 | tf_op jit(solution)/shard_map/all_to_all | solution.py:39
  1018.3 186.3 %all-reduce.3.cloned.1.call-start = ((), (), s32[]{:S(2)}) async-start(), calls=%async_computation.26 | async-start | bytes 2097152
  1020.2 7.1 copy-start.7
  1036.3 4.1 copy-start.75
  1036.3 4.2 copy-start.28
  1044.5 9.7 copy-start.47
  1044.5 9.7 copy-start.57
  1044.5 9.7 copy-start.59
  1044.5 9.7 copy-start.60
  1044.5 9.9 copy-start.44
  1044.5 9.9 copy-start.51
  1046.0 8.6 copy-start.66
  1046.0 8.6 copy-start.63
  1046.1 9.6 copy-start.61
  1057.1 226.6 %reduce-scatter.15.cloned.1.call-start = ((), (), s32[]{:S(2)}) async-start(), calls=%async_computation.24 | async-start | bytes 3342336 | tf_op jit(solution)/shard_map/reduce_scatter | solution.py:63
  (36 other events, 85.9 us)
Sparse Core Ops, SparseCore 0:
  11.5 54.8 all-gather.2
  378.0 40.2 reduce-scatter.6
  470.7 44.1 reduce-scatter.8
  517.7 52.4 all-gather.4
  593.2 43.2 reduce-scatter.10
  694.9 63.4 reduce-scatter.12
  963.2 78.1 reduce-scatter.16
  1057.2 147.4 all-reduce.2
  1209.2 74.4 reduce-scatter.14
where the time goes:
time: 1310 us; the launch traced here: 1300 us
  waiting for transfers between devices  501 us (38%)
  blocking collectives  468 us (36%)
  matrix products  120 us (9%)
  local copies, waits for them, and re-layouts  103 us (8%)
  starting transfers between devices  47.2 us (4%)
  other arithmetic  41.6 us (3%)
  between operations  15.7 us (1%)
    all_gather x1, blocking collectives, gather_turned(): whole = lax.all_gather(both, axis, axis=0, tiled=True)  323 us
    unnamed x10, waiting for transfers between devices  139 us
    reduce_scatter x4, waiting for transfers between devices, forward_sum(): lax.psum_scatter(jnp.dot(left, right, preferred_element_type=jnp.float32)...  127 us
    all_to_all x6, waiting for transfers between devices, sent_to_all(): return lax.all_to_all(copies, axis, split_axis=0, concat_axis=0, tiled=True)  105 us
    reduce_scatter x2, waiting for transfers between devices, sum_together(): lax.psum_scatter(lines, axis, tiled=True).reshape(-1)  76.4 us
    all_to_all x2, blocking collectives, sent_and_summed(): parts = lax.all_to_all(split_up(array, dim, peers), axis, 0, 0, tiled=True)  75.9 us
    all_to_all x2, blocking collectives, sent_to_all(): return lax.all_to_all(copies, axis, split_axis=0, concat_axis=0, tiled=True)  69 us
    all_gather x2, waiting for transfers between devices, gather_turned(): whole = lax.all_gather(both, axis, axis=0, tiled=True)  45.8 us
  transfers between devices with their start and end apart: 17, of which 13 were waited for; matrix products, arithmetic and copies ran while one was open for 11% of the time, Pallas kernels for 0%

commit v1 on v0

v1 whole, which is shorter than its diff:
```python
import functools
import math

import jax
import jax.numpy as jnp
from jax import lax
from jax.experimental import pallas as pl
from jax.experimental.pallas import tpu as pltpu
from jax.sharding import PartitionSpec as P

HEAD = 64
BUFFER = 64
EPS = 1e-06
NEG = -1e30
BF = jnp.bfloat16
F32 = jnp.float32
LANES = 128
ROWS = 12
FLOPS_PER_US = 1.15e9

PLACES = ("dp", "tensor")
DEVICES = 128
X_MASKS = (32, 64, 96)
YH, CORE, YL, ZH, ZL = 16, 8, 4, 2, 1
Y_MASKS = (YL, YH, YH | YL)
Z_MASK = ZH | ZL

ANY = pl.BlockSpec(memory_space=pl.ANY)
HBM = pl.BlockSpec(memory_space=pltpu.HBM)
VMEM = pl.BlockSpec(memory_space=pltpu.VMEM)
SMEM = pl.BlockSpec(memory_space=pltpu.SMEM)
WINDOW = pl.BlockSpec()


def swapped(array, mask):
    return lax.ppermute(array, PLACES, [(i, i ^ mask) for i in range(DEVICES)])


def sent_by(array, mask, sends):
    return lax.ppermute(array, PLACES, [(i, i ^ mask) for i in range(DEVICES) if sends(i)])


def zl_is_core(place):
    return place & ZL == (place & CORE) // CORE


def zl_is_not_core(place):
    return not zl_is_core(place)


def dot(left, right):
    return jnp.dot(left, right, preferred_element_type=F32)


def dot_turned(left, right):
    return lax.dot_general(left, right, (((1,), (1,)), ((), ())), preferred_element_type=F32)


def outer(left, right):
    return lax.dot_general(left, right, (((0,), (0,)), ((), ())), preferred_element_type=F32)


def call(body, outs, in_specs, args, scratch=(), out_specs=None, limit=12, deps=(), cost=0.5):
    out_specs = tuple(out_specs or [VMEM] * len(outs))
    outs = [
        pltpu.HBM(o.shape, o.dtype) if spec is WINDOW else o
        for o, spec in zip(outs, out_specs)
    ]
    args = [
        pltpu.with_memory_space_constraint(a, pltpu.HBM) if spec is WINDOW else a
        for a, spec in zip(args, in_specs)
    ]
    inputs = len(args)

    def kernel(*refs):
        body(*refs[:inputs], *refs[inputs + len(deps) :])

    windowed = any(spec.block_shape is not None for spec in in_specs)
    return pl.pallas_call(
        kernel,
        grid=(1,) if windowed else (),
        out_shape=tuple(outs),
        in_specs=[*in_specs, *[ANY] * len(deps)],
        out_specs=out_specs,
        scratch_shapes=list(scratch),
        compiler_params=pltpu.CompilerParams(vmem_limit_bytes=limit << 20),
        cost_estimate=pl.CostEstimate(
            flops=int(cost * FLOPS_PER_US), bytes_accessed=1, transcendentals=0
        ),
    )(*args, *deps)


def shape(dims, dtype):
    return jax.ShapeDtypeStruct(tuple(dims), dtype)


def bundle_scratch(wide):
    return pltpu.VMEM((4, 2, LANES, 2 * wide), BF)


def line_piece(lines, last, first):
    if last == 2:
        return lines[2 + first // 2].at[first % 2]
    return lines[(0, 1, None, 4)[last]].at[first]


def bundle_copies(core, wide, lines, whole, sems, inward):
    made = []
    for last in range(4):
        for first in range(4):
            x = last + core * (first - last)
            y = first + core * (last - first)
            at = pl.multiple_of((y % 2) * wide, LANES)
            ends = (line_piece(lines, last, first), whole.at[x, y // 2, :, pl.ds(at, wide)])
            made.append(
                pltpu.make_async_copy(*(ends if inward else ends[::-1]), sems.at[4 * last + first])
            )
    return made


def along(array, number, last):
    masks = (X_MASKS, Y_MASKS) if last else (Y_MASKS, X_MASKS)
    pairs = [
        (i, i ^ masks[1 if i & CORE else 0][number - 1]) for i in range(DEVICES)
    ]
    return lax.ppermute(array, PLACES, pairs)


def shard_kernel(w_qkv, w_out, w_up, w_down, out):
    wide, hidden = w_qkv.shape[3], w_up.shape[2]
    for layer in range(2):
        at = 4 * wide * layer
        for k in range(3):
            out[:, at + k * wide : at + (k + 1) * wide] = w_qkv[layer, k]
        out[:, at + 3 * wide : at + 4 * wide] = w_out[layer]
        at = 8 * wide + 2 * hidden * layer
        out[:, at : at + hidden] = w_up[layer]
        out[:, at + hidden : at + 2 * hidden] = w_down[layer]


def both_kernel(scal, mine, other, out):
    rows = mine.shape[0]
    out[pl.ds(pl.multiple_of(scal[2] * rows, rows), rows), :] = mine[...]
    out[pl.ds(pl.multiple_of((1 - scal[2]) * rows, rows), rows), :] = other[...]


def begin_kernel(layer, scal, both, by_zl, by_zh, by_both, out):
    mine = scal[1] != 0
    attn = by_zh.shape[1] // 2
    feed = by_zl.shape[1] - attn
    cols = slice(attn * layer, attn * (layer + 1))
    rest = slice(2 * attn + feed * layer, 2 * attn + feed * (layer + 1))
    out[:, :attn] = jnp.where(mine, both[:, cols], by_zl[:, :attn])
    out[:, attn : 2 * attn] = jnp.where(mine, by_zh[:, cols], by_both[:, cols])
    out[:, 2 * attn :] = jnp.where(mine, both[:, rest], by_zl[:, attn:])


def cores_joined(shard, scal, deps):
    return call(
        both_kernel,
        [shape((2 * shard.shape[0], shard.shape[1]), BF)],
        [SMEM, VMEM, VMEM],
        [scal, shard, swapped(shard, CORE)],
        deps=deps,
    )[0]


def begun(both, scal, attn, deps=()):
    feed = both.shape[1] // 2 - attn
    part = both[:, : 2 * attn]
    far = [sent_by(part, m, zl_is_core) for m in (ZH, Z_MASK)]
    outs = []
    for layer in range(2):
        first = 2 * attn + feed * layer
        cols = (both[:, attn * layer : attn * (layer + 1)], both[:, first : first + feed])
        near = sent_by(jnp.concatenate(cols, axis=1), ZL, zl_is_core)
        outs.append(
            call(
                functools.partial(begin_kernel, layer),
                [shape((both.shape[0], 2 * attn + feed), BF)],
                [SMEM] + [VMEM] * 4,
                [scal, both, near, *far],
                deps=() if layer else deps,
            )[0]
        )
    return outs


def block(array, axis, at, parts):
    dims = tuple(n // parts if k == axis else n for k, n in enumerate(array.shape))
    place = tuple(at if k == axis else 0 for k in range(array.ndim))
    return pl.BlockSpec(dims, lambda *_: place), dims


def copies_kernel(*refs):
    half = len(refs) // 2
    for source, out in zip(refs[:half], refs[half:]):
        out[...] = source[...]


def halves_of(near, far, deps=(), axis=0):
    specs = [block(near, axis, 0, 2), block(far, axis, 1, 2)]
    return call(
        copies_kernel,
        [shape(dims, BF) for _, dims in specs],
        [spec for spec, _ in specs],
        [near, far],
        deps=deps,
    )


def line_kernel(*refs):
    for k in range(4):
        refs[4][k] = refs[k][...]


class Light:
    def __init__(self, begin, deps=()):
        self.begin = begin
        self.near, self.far = along(begin, 1, False), along(begin, 3, False)
        self.halves = halves_of(self.near, self.far, deps, 1)
        one, two = self.halves
        self.across = [along(one, 3, False), along(two, 1, False)]

    def line(self, k, deps=()):
        specs = [block(a, 1, k, 2) for a in (self.begin, self.near, self.far)]
        across = self.across[k]
        specs.insert(2, (VMEM, across.shape))
        return call(
            line_kernel,
            [shape((4, *across.shape), BF)],
            [spec for spec, _ in specs],
            [self.begin, self.near, across, self.far],
            deps=deps,
        )[0]


def tie_kernel(*refs):
    refs[-1][...] = refs[0][...]


def tied(array, deps):
    return call(tie_kernel, [shape(array.shape, array.dtype)], [VMEM], [array], deps=deps)[0]


class Heavy:
    def __init__(self, line, deps=()):
        self.line = line
        self.near, self.far = along(line, 1, True), along(line, 3, True)
        self.halves = halves_of(self.near, self.far, deps)
        one, two = self.halves
        self.across = [along(one, 3, True), along(two, 1, True)]

    def lines(self):
        return [self.line, self.near, *self.across, self.far]


def sum_kernel(count, *refs):
    total = refs[0][...].astype(F32)
    for ref in refs[1:count]:
        total = total + ref[...].astype(F32)
    total = total.astype(BF)
    outs = refs[count:]
    if len(outs) == 1:
        outs[0][...] = total
        return
    if len(outs) == 4:
        for k, out in enumerate(outs):
            out[...] = total[k]
        return
    keep, send = outs
    for k in range(2):
        keep[k] = total[k]
        send[k] = total[3 - k]


def halves_kernel(keep, moved, mine, send):
    total = (keep[...].astype(F32) + moved[...].astype(F32)).astype(BF)
    mine[...] = total[0]
    send[...] = total[1]


def summed(arrays, outs, deps=()):
    return call(
        functools.partial(sum_kernel, len(arrays)),
        outs,
        [VMEM] * len(arrays),
        arrays,
        deps=deps,
    )


def pass_on_kernel(near, far, to_far, to_near, near_out, far_out):
    half = near.shape[0] // 2
    near_out[:half] = near[:half]
    near_out[half:] = (near[half:].astype(F32) + to_near[...].astype(F32)).astype(BF)
    far_out[:half] = (far[:half].astype(F32) + to_far[...].astype(F32)).astype(BF)
    far_out[half:] = far[half:]


class Reduction:
    def __init__(self, lines):
        self.lines = lines

    def a(self, deps=()):
        mine, near, across_one, across_two, far = self.lines
        moved = [along(across_one, 1, True), along(across_two, 3, True)]
        self.passed = call(
            pass_on_kernel,
            [shape(near.shape, BF)] * 2,
            [VMEM] * 4,
            [near, far, *moved],
            deps=deps,
        )
        return self.passed[:1]

    def b(self, deps=(), direct=False):
        near, far = self.passed
        mine = self.lines[0]
        outs = [shape((2, *mine.shape[1:]), BF)] * 2
        if direct:
            outs = [shape(mine.shape[1:], BF)] * 4
        self.parts = summed([mine, along(near, 1, True), along(far, 3, True)], outs, deps)
        return self.parts[:1]

    def c(self, deps=()):
        keep, send = self.parts
        outs = [shape(keep.shape[1:], BF)] * 2
        self.pair = call(
            halves_kernel, outs, [VMEM] * 2, [keep, along(send, 3, False)], deps=deps
        )
        return self.pair[:1]

    def spread(self):
        return [along(self.parts[k], k, False) for k in (1, 2, 3)]

    def direct(self, moved, deps=()):
        outs = [shape(moved[0].shape, BF)]
        self.total = summed([self.parts[0], *moved], outs, deps)[0]

    def d(self, deps=()):
        mine, send = self.pair
        outs = [shape(mine.shape, BF)]
        self.total = summed([mine, along(send, 1, False)], outs, deps)[0]
        return [self.total]


class Bundle:
    def __init__(self, lines, blocks, places):
        self.lines = lines
        self.blocks = blocks
        self.wide = lines[0].shape[2]
        self.step = 2 * self.wide // blocks
        self.places = places

    def scratch(self):
        return [bundle_scratch(self.wide), pltpu.SemaphoreType.DMA((16,))]

    def out_shapes(self):
        return [shape(l.shape, BF) for l in self.lines]

    def copies(self, core, refs, scratch, inward):
        return bundle_copies(core, self.wide, refs, scratch[0], scratch[1], inward)

    def columns(self, scratch, name, blocks=None):
        first, wide = self.places[name]
        blocks = tuple(range(self.blocks)) if blocks is None else blocks
        cuts = [
            scratch[0][:, :, :, b * self.step + first : b * self.step + first + wide]
            for b in blocks
        ]
        whole = jnp.concatenate(cuts, axis=-1) if len(cuts) > 1 else cuts[0]
        return whole.reshape(-1, wide * len(blocks))

    def store(self, scratch, name, value, x):
        first, wide = self.places[name]
        value = value.reshape(2, LANES, -1)
        for b in range(self.blocks):
            scratch[0][x, :, :, b * self.step + first : b * self.step + first + wide] = value[
                :, :, b * wide : (b + 1) * wide
            ]


def start(copies):
    for copy in copies:
        copy.start()


def finish(copies):
    for copy in copies:
        copy.wait()


def both_rows(own, other):
    return jnp.concatenate([own[...], other[...]])


def lane_halves(value):
    lane = lax.broadcasted_iota(jnp.int32, value.shape, 1)
    zero = jnp.zeros_like(value)
    return jnp.where(lane < HEAD, value, zero), jnp.where(lane < HEAD, zero, value)


def attention_kernel(weights, layer, scal, own, other, small, *refs):
    pieces, refs = refs[:5], refs[5:]
    mine, theirs, qkv, probs, mixed = refs[:5]
    scratch = refs[5:]
    core, valid = scal[2], scal[3]
    copies = weights.copies(core, pieces, scratch, True)
    start(copies)
    rows = own.shape[0]
    seq = 2 * rows
    a = both_rows(own, other)
    finish(copies)
    wide = qkv.shape[1] // 3
    places = [
        pl.multiple_of(
            (((scal[4] ^ ylr) * 4 + (scal[5] ^ zhr) * 2 + core) ^ scal[0]) * LANES, LANES
        )
        for ylr in range(2)
        for zhr in range(2)
    ]
    for k, name in enumerate("qkv"):
        part = dot(a, weights.columns(scratch, name))
        if name != "k":
            at = layer * ROWS + (6 if name == "q" else 7)
            bias = [small[at : at + 1, pl.ds(place, LANES)] for place in places]
            part = part + jnp.concatenate(bias, axis=1)
        qkv[:, k * wide : (k + 1) * wide] = part.astype(BF)
    key = lax.broadcasted_iota(jnp.int32, (1, seq), 1)
    position = jnp.where(key < rows, key + core * rows, key - core * rows)
    allowed = position < valid
    factor = 1.0 / math.sqrt(HEAD)
    for b in range(wide // LANES):
        lanes = slice(b * LANES, (b + 1) * LANES)
        q = qkv[:, b * LANES : (b + 1) * LANES]
        k = qkv[:, wide + b * LANES : wide + (b + 1) * LANES]
        v = qkv[:, 2 * wide + b * LANES : 2 * wide + (b + 1) * LANES]
        total = None
        for h, (q_h, v_h) in enumerate(zip(lane_halves(q), lane_halves(v))):
            scores = jnp.where(allowed, dot_turned(q_h, k) * factor, NEG)
            expo = jnp.exp(scores - jnp.max(scores, axis=-1, keepdims=True))
            p = (expo / jnp.sum(expo, axis=-1, keepdims=True)).astype(BF)
            probs[2 * b + h] = p
            part = dot(p, v_h)
            total = part if total is None else total + part
        mixed[:, lanes] = total.astype(BF)
    out = dot_turned(mixed[...], weights.columns(scratch, "o"))
    mine[...] = out[:rows]
    theirs[...] = out[rows:].astype(BF)


def attention(weights, layer, scal, own, other, small, deps):
    rows, width = own.shape
    wide = width // 2
    seq = 2 * rows
    outs = [
        shape((rows, width), F32),
        shape((rows, width), BF),
        shape((seq, 3 * wide), BF),
        shape((wide // HEAD, seq, seq), BF),
        shape((seq, wide), BF),
    ]
    return call(
        functools.partial(attention_kernel, weights, layer),
        outs,
        [SMEM, VMEM, VMEM, VMEM] + [HBM] * 5,
        [scal, own, other, small, *weights.lines],
        weights.scratch(),
        out_specs=[VMEM, VMEM, WINDOW, WINDOW, WINDOW],
        deps=deps,
        cost=6.0,
    )


def attention_back_kernel(weights, scal, own, other, qkv, probs, *refs):
    pieces, refs = refs[:5], refs[5:]
    mine, theirs, grads = refs[:3]
    scratch = refs[3:]
    copies = weights.copies(scal[2], pieces, scratch, True)
    start(copies)
    rows = own.shape[0]
    wide = qkv.shape[1] // 3
    d = both_rows(own, other)
    finish(copies)
    factor = 1.0 / math.sqrt(HEAD)
    spread = dot(d, weights.columns(scratch, "o")).astype(BF)
    for b in range(wide // LANES):
        q = qkv[:, b * LANES : (b + 1) * LANES]
        k = qkv[:, wide + b * LANES : wide + (b + 1) * LANES]
        v = qkv[:, 2 * wide + b * LANES : 2 * wide + (b + 1) * LANES]
        do = spread[:, b * LANES : (b + 1) * LANES]
        dq = dk = dv = None
        parts = zip(lane_halves(q), lane_halves(k), lane_halves(do))
        for h, (q_h, k_h, do_h) in enumerate(parts):
            p = probs[2 * b + h]
            dv_h = outer(p, do_h)
            dp = dot_turned(do_h, v)
            wide_p = p.astype(F32)
            ds = wide_p * (dp - jnp.sum(wide_p * dp, axis=-1, keepdims=True))
            ds = ds.astype(BF)
            dq_h = dot(ds, k_h)
            dk_h = outer(ds, q_h)
            dq, dk, dv = (
                (dq_h, dk_h, dv_h) if dq is None else (dq + dq_h, dk + dk_h, dv + dv_h)
            )
        grads[:, b * LANES : (b + 1) * LANES] = (dq * factor).astype(BF)
        grads[:, wide + b * LANES : wide + (b + 1) * LANES] = (dk * factor).astype(BF)
        grads[:, 2 * wide + b * LANES : 2 * wide + (b + 1) * LANES] = dv.astype(BF)
    whole = jnp.concatenate([weights.columns(scratch, name) for name in "qkv"], axis=1)
    out = dot_turned(grads[...], whole)
    mine[...] = out[:rows]
    theirs[...] = out[rows:].astype(BF)


def attention_back(weights, scal, own, other, qkv, probs, deps=()):
    rows, width = own.shape
    seq, wide = qkv.shape[0], qkv.shape[1] // 3
    outs = [shape((rows, width), F32), shape((rows, width), BF), shape(qkv.shape, BF)]
    return call(
        functools.partial(attention_back_kernel, weights),
        outs,
        [SMEM, VMEM, VMEM, WINDOW, WINDOW] + [HBM] * 5,
        [scal, own, other, qkv, probs, *weights.lines],
        weights.scratch(),
        deps=deps,
        cost=7.0,
    )


def weight_grad_kernel(weights, jobs, lefts, rights, sums, scal, *refs):
    values = []
    for count in (*lefts, *rights):
        values.append(jnp.concatenate([r[...] for r in refs[:count]]) if count > 1 else refs[0])
        refs = refs[count:]
    pieces, refs = refs[:5], refs[5:]
    sum_refs, scratch = refs[: len(sums)], refs[len(sums) :]
    for name, left, right, first, wide in jobs:
        block = values[left].shape[1] // 4
        for x in range(4):
            grad = outer(
                values[left][:, x * block : (x + 1) * block],
                values[len(lefts) + right][:, first : first + wide],
            )
            weights.store(scratch, name, grad.astype(BF), x)
    copies = weights.copies(scal[2], pieces, scratch, False)
    start(copies)
    for ref, k in zip(sum_refs, sums):
        ref[...] = jnp.sum(values[len(lefts) + k][...].astype(F32), axis=0, keepdims=True)
    finish(copies)


def weight_grads(weights, scal, jobs, lefts, rights, kept, sums, deps=()):
    outs = weights.out_shapes() + [shape((1, rights[k][0].shape[1]), F32) for k in sums]
    arrays = [a for group in (*lefts, *rights) for a in group]
    rows = sum(a.shape[0] for a in lefts[0])
    return call(
        functools.partial(
            weight_grad_kernel,
            weights,
            jobs,
            [len(g) for g in lefts],
            [len(g) for g in rights],
            sums,
        ),
        outs,
        [SMEM]
        + [VMEM] * sum(len(g) for g in lefts)
        + [WINDOW if k in kept else VMEM for k, g in enumerate(rights) for _ in g],
        [scal, *arrays],
        weights.scratch(),
        out_specs=[HBM] * 5 + [VMEM] * len(sums),
        deps=deps,
        cost=5.0,
    )


def hidden_places(scal, layer, ylr):
    row = (scal[4] ^ ylr) * 2 + scal[5]
    mask = lax.broadcasted_iota(jnp.int32, (4, LANES), 0) == row
    return mask, [pl.multiple_of(((scal[2] * 4 + k) ^ scal[0]) * LANES, LANES) for k in range(4)]


def feed_kernel(weights, layer, scal, own, other, small, *refs):
    pieces, refs = refs[:5], refs[5:]
    mine, theirs, active, slope = refs[:4]
    scratch = refs[4:]
    copies = weights.copies(scal[2], pieces, scratch, True)
    start(copies)
    rows = own.shape[0]
    b = both_rows(own, other)
    finish(copies)
    wide = active.shape[1] // 2
    for k in range(2):
        cols = slice(k * wide, (k + 1) * wide)
        mask, places = hidden_places(scal, layer, k)
        at = layer * ROWS + 8
        bias = [jnp.where(mask, small[at : at + 4, pl.ds(p, LANES)], 0.0) for p in places]
        bias = jnp.sum(jnp.concatenate(bias, axis=1), axis=0, keepdims=True)
        u = dot(b, weights.columns(scratch, "u", (k,))) + bias
        below = 0.5 + 0.5 * lax.erf(u * math.sqrt(0.5))
        active[:, cols] = (u * below).astype(BF)
        bell = jnp.exp(u * u * -0.5) * (1.0 / math.sqrt(2.0 * math.pi))
        slope[:, cols] = (below + u * bell).astype(BF)
    out = dot_turned(active[...], weights.columns(scratch, "d"))
    mine[...] = out[:rows]
    theirs[...] = out[rows:].astype(BF)


def feed(weights, layer, scal, own, other, small, deps=()):
    rows, width = own.shape
    seq, wide = 2 * rows, width
    outs = [
        shape((rows, width), F32),
        shape((rows, width), BF),
        shape((seq, wide), BF),
        shape((seq, wide), BF),
    ]
    return call(
        functools.partial(feed_kernel, weights, layer),
        outs,
        [SMEM, VMEM, VMEM, VMEM] + [HBM] * 5,
        [scal, own, other, small, *weights.lines],
        weights.scratch(),
        out_specs=[VMEM, VMEM, WINDOW, WINDOW],
        deps=deps,
        cost=3.5,
    )


def feed_back_kernel(weights, scal, own, other, slope, *refs):
    pieces, refs = refs[:5], refs[5:]
    mine, theirs, grads = refs[:3]
    scratch = refs[3:]
    copies = weights.copies(scal[2], pieces, scratch, True)
    start(copies)
    rows = own.shape[0]
    g = both_rows(own, other)
    finish(copies)
    wide = slope.shape[1] // 2
    for k in range(2):
        cols = slice(k * wide, (k + 1) * wide)
        dz = dot(g, weights.columns(scratch, "d", (k,)))
        grads[:, cols] = (dz * slope[:, cols].astype(F32)).astype(BF)
    out = dot_turned(grads[...], weights.columns(scratch, "u"))
    mine[...] = out[:rows]
    theirs[...] = out[rows:].astype(BF)


def feed_back(weights, scal, own, other, slope, deps=()):
    rows, width = own.shape
    outs = [shape((rows, width), F32), shape((rows, width), BF), shape(slope.shape, BF)]
    return call(
        functools.partial(feed_back_kernel, weights),
        outs,
        [SMEM, VMEM, VMEM, WINDOW] + [HBM] * 5,
        [scal, own, other, slope, *weights.lines],
        weights.scratch(),
        deps=deps,
        cost=3.3,
    )


def in_order(ref, order):
    wide = ref.shape[1] // 8
    return jnp.concatenate(
        [ref[:, pl.ds(pl.multiple_of((k ^ order) * wide, wide), wide)] for k in range(8)], axis=1
    )


def normed(rows, gain, shift):
    centre = rows - jnp.mean(rows, axis=-1, keepdims=True)
    spread = jnp.mean(centre * centre, axis=-1, keepdims=True)
    return centre * lax.rsqrt(spread + EPS) * gain + shift


def first_kernel(scal, mine, moved, small, state, out):
    stays = scal[1] != 0
    order = scal[0]
    rows = jnp.where(stays, in_order(mine, order).astype(F32), in_order(moved, order).astype(F32))
    state[...] = rows
    out[...] = normed(rows, small[0:1], small[2:3]).astype(BF)


def first_rows(scal, mine, moved, small):
    outs = [shape(mine.shape, F32), shape(mine.shape, BF)]
    return call(
        first_kernel,
        outs,
        [SMEM] + [VMEM] * 3,
        [scal, mine, moved, small],
        out_specs=[WINDOW, VMEM],
    )


def grad_kernel(scal, mine, moved, state, out, sums):
    stays = scal[1] != 0
    order = scal[0]
    rows = jnp.where(stays, in_order(mine, order), in_order(moved, order))
    state[...] = rows
    out[...] = rows.astype(BF)
    sums[...] = jnp.sum(rows, axis=0, keepdims=True)


def grad_rows(scal, mine, moved):
    outs = [shape(mine.shape, F32), shape(mine.shape, BF), shape((1, mine.shape[1]), F32)]
    return call(grad_kernel, outs, [SMEM] + [VMEM] * 2, [scal, mine, moved])


def last_kernel(scal, mine, moved, out):
    stays = scal[1] != 0
    order = scal[0]
    out[...] = jnp.where(stays, in_order(mine, order), in_order(moved, order))


def last_rows(scal, mine):
    moved = sent_by(mine, CORE | ZL, zl_is_not_core)
    return call(
        last_kernel, [shape(mine.shape, F32)], [SMEM] + [VMEM] * 2, [scal, mine, moved]
    )[0]


def total_of(refs):
    total = refs[0][...].astype(F32)
    for ref in refs[1:]:
        total = total + ref[...].astype(F32)
    return total


def join_kernel(at, rows, small, *refs):
    *parts, state, out = refs
    bias, gain, shift = (small[k : k + 1] for k in at)
    total = rows[...] + (total_of(parts) + bias)
    state[...] = total
    out[...] = normed(total, gain, shift).astype(BF)


def joined(rows, parts, small, at, deps=()):
    outs = [shape(rows.shape, F32), shape(rows.shape, BF)]
    return call(
        functools.partial(join_kernel, at),
        outs,
        [WINDOW, VMEM] + [VMEM] * len(parts),
        [rows, small, *parts],
        out_specs=[WINDOW, VMEM],
        deps=deps,
        cost=2.0,
    )


def norm_back_kernel(at, above, rows, small, *refs):
    *parts, state, out, sums = refs
    dy = total_of(parts)
    centre = rows[...] - jnp.mean(rows[...], axis=-1, keepdims=True)
    scale = lax.rsqrt(jnp.mean(centre * centre, axis=-1, keepdims=True) + EPS)
    unit = centre * scale
    weighed = dy * small[at : at + 1]
    inner = weighed - jnp.mean(weighed, axis=-1, keepdims=True)
    inner = inner - unit * jnp.mean(weighed * unit, axis=-1, keepdims=True)
    total = above[...] + inner * scale
    state[...] = total
    out[...] = total.astype(BF)
    sums[0:1] = jnp.sum(dy * unit, axis=0, keepdims=True)
    sums[1:2] = jnp.sum(dy, axis=0, keepdims=True)
    sums[2:3] = jnp.sum(total, axis=0, keepdims=True)


def norm_back(above, rows, parts, small, at, deps=()):
    outs = [shape(rows.shape, F32), shape(rows.shape, BF), shape((3, rows.shape[1]), F32)]
    return call(
        functools.partial(norm_back_kernel, at),
        outs,
        [VMEM, WINDOW, VMEM] + [VMEM] * len(parts),
        [above, rows, small, *parts],
        deps=deps,
        cost=1.7,
    )


def fold_kernel(mine, theirs, out):
    out[...] = (mine[...] + theirs[...].astype(F32)).astype(BF)


def folded(mine, theirs):
    return call(
        fold_kernel, [shape(mine.shape, BF)], [VMEM] * 2, [mine, swapped(theirs, CORE)]
    )[0]


def from_far(mine, theirs):
    return swapped(folded(mine, theirs), Z_MASK)


def gathered_rows(own):
    far = swapped(own, Z_MASK)
    return own, swapped(own, CORE), far, swapped(far, CORE)


def gathered_small(small, lane):
    part = jnp.zeros((small.shape[0], LANES), F32)
    part = lax.dynamic_update_slice(part, small, (0, lane))
    steps = [part + swapped(part, YL)]
    for mask in (YH | YL, X_MASKS[0]):
        steps.append(jnp.concatenate([steps[-1], swapped(steps[-1], mask)], axis=1))
    half = steps[-1].shape[1] // 2
    moved = swapped(steps[-1], X_MASKS[2])
    steps.append(jnp.concatenate([steps[-1], moved[:, half:], moved[:, :half]], axis=1))
    for mask in (CORE, Z_MASK, ZL):
        steps.append(steps[-1] + swapped(steps[-1], mask))
    return steps


def summed_over(small, masks):
    for mask in masks:
        small = small + swapped(small, mask)
    return small


def reduced_small(small, lane, wide):
    steps = []
    half = small.shape[1] // 2
    quarter = half // 2
    send = jnp.concatenate([small[:, half + quarter :], small[:, half : half + quarter]], axis=1)
    steps.append(small[:, :half] + swapped(send, X_MASKS[2]))
    for mask in (X_MASKS[0], YH | YL):
        half = steps[-1].shape[1] // 2
        steps.append(steps[-1][:, :half] + swapped(steps[-1][:, half:], mask))
    small = summed_over(steps[-1], [YL])
    return steps, lax.dynamic_slice(small, (0, lane), (small.shape[0], wide))


def pack_kernel(layers, scal, *refs):
    out = refs[-1]
    out[...] = jnp.zeros(out.shape, F32)
    for layer in range(layers):
        one, two, above, heads, hidden = refs[5 * layer : 5 * layer + 5]
        at = layer * ROWS
        out[at : at + 1] = one[0:1]
        out[at + 1 : at + 2] = two[0:1]
        out[at + 2 : at + 3] = one[1:2]
        out[at + 3 : at + 4] = two[1:2]
        out[at + 4 : at + 5] = two[2:3]
        out[at + 5 : at + 6] = above[above.shape[0] - 1 : above.shape[0]]
        wide = heads.shape[1] // 3
        for k in range(4):
            block = (scal[4] ^ (k // 2)) * 4 + (scal[5] ^ (k % 2)) * 2 + scal[2]
            place = pl.multiple_of((block ^ scal[0]) * LANES, LANES)
            for row, first in ((6, 0), (7, 2 * wide)):
                first += k * LANES
                out[at + row : at + row + 1, pl.ds(place, LANES)] = heads[:, first : first + LANES]
        for ylr in range(2):
            mask, places = hidden_places(scal, layer, ylr)
            for k, place in enumerate(places):
                first = (4 * ylr + k) * LANES
                part = jnp.where(mask, hidden[:, first : first + LANES], 0.0)
                out[at + 8 : at + 12, pl.ds(place, LANES)] += part


def packed(scal, parts):
    arrays = [a for layer in parts for a in layer]
    out = shape((ROWS * len(parts), arrays[0].shape[1]), F32)
    return call(
        functools.partial(pack_kernel, len(parts)), [out], [SMEM] + [VMEM] * len(arrays), [scal, *arrays]
    )[0]


def per_device(tokens, kept, w_qkv, w_out, w_up, w_down, ln_gains, biases, grad_out):
    dp_place = lax.axis_index("dp")
    tensor_place = lax.axis_index("tensor")
    core = dp_place % 2
    order = dp_place // 2
    yl = tensor_place // 4
    zh = (tensor_place // 2) % 2
    zl = tensor_place % 2
    rows, width = tokens.shape
    layers = w_qkv.shape[0]
    head_wide = w_qkv.shape[3]
    hidden_wide = w_up.shape[2]

    both_kept = jnp.where(zl == core, kept, swapped(kept, CORE))
    valid = BUFFER + lax.dynamic_index_in_dim(both_kept, yl * 2 + zh, keepdims=False)
    scal = jnp.stack(
        [order, (zl == core).astype(jnp.int32), core, valid.astype(jnp.int32), yl, zh, zl]
    ).astype(jnp.int32)
    own_wide = ln_gains.shape[2]
    lane = (core * 8 + tensor_place) * own_wide

    h, f = head_wide, hidden_wide

    row_weights = [
        w_qkv.transpose(0, 2, 1, 3),
        w_out.transpose(0, 2, 1),
        w_up,
        w_down.transpose(0, 2, 1),
    ]

    shard = call(
        shard_kernel,
        [shape((w_up.shape[1], 8 * h + 4 * f), BF)],
        [WINDOW] * 4,
        row_weights,
    )[0]
    small = jnp.concatenate([ln_gains, biases], axis=1).reshape(layers * ROWS, own_wide)
    steps = gathered_small(tied(small, [shard]), lane)
    small = steps[-1]

    both = cores_joined(shard, scal, ())
    begin, later = begun(both, scal, 4 * h, [steps[2]])
    light = Light(begin, [steps[3]])
    line = light.line(0, [steps[4]])

    moved = sent_by(tokens, CORE | ZL, zl_is_not_core)
    state, a = first_rows(scal, tokens, moved, small)
    grad, g, sums_above = grad_rows(scal, grad_out, sent_by(grad_out, CORE | ZL, zl_is_not_core))

    wave = Heavy(line, [steps[5]])
    later = Light(tied(later, wave.halves))
    feed_places = {"u": (0, f), "d": (f, f)}
    attn_places = {n: (j * h, h) for j, n in enumerate("qkvo")}
    attn_weights, feed_weights = [], []

    saved = []
    for index in range(layers):
        attn_weights.append(Bundle(wave.lines(), 4, attn_places))
        line = light.line(1, [*wave.across, a])
        if index:
            g_rows = gathered_rows(g)
        a_other = swapped(a, CORE)
        mine, theirs, qkv, probs, mixed = attention(
            attn_weights[index], index, scal, a, a_other, small, [line] if index else [line, *later.halves]
        )
        middle, b = joined(
            state,
            [mine, swapped(theirs, CORE)],
            small,
            [index * ROWS + k for k in (4, 1, 3)],
            g_rows if index else [g],
        )
        b_rows = gathered_rows(b)
        wave = Heavy(line, [b])
        feed_weights.append(Bundle(wave.lines(), 2, feed_places))
        deps = () if index else later.across
        far = feed(feed_weights[index], index, scal, *b_rows[2:], small, deps)
        deps = far[1:2]
        if index == layers - 1:
            far_back = feed_back(feed_weights[index], scal, *g_rows[2:], far[3])
            deps = far_back[1:2]
        near = feed(feed_weights[index], index, scal, *b_rows[:2], small, deps)
        if index < layers - 1:
            light = later
            next_wave = Heavy(light.line(0, wave.across))
        active, slope = (near[2], far[2]), (near[3], far[3])
        saved.append((state, a, a_other, qkv, probs, mixed, middle, b_rows, active, slope))
        if index < layers - 1:
            wave = next_wave
            state, a = joined(
                middle,
                [near[0], swapped(near[1], CORE), from_far(far[0], far[1])],
                small,
                [index * ROWS + 5, (index + 1) * ROWS, (index + 1) * ROWS + 2],
            )
    last_near, last_far = near, far

    small_parts = [None] * layers
    feed_sums, attn_sums = [None] * layers, [None] * layers
    for index in reversed(range(layers)):
        state, a, a_other, qkv, probs, mixed, middle, b_rows, active, slope = saved[index]
        attn_w, feed_w = attn_weights[index], feed_weights[index]
        last = index == layers - 1
        if not last:
            g_rows = gathered_rows(g)
        near = feed_back(feed_w, scal, *g_rows[:2], slope[0])
        far = far_back if last else feed_back(feed_w, scal, *g_rows[2:], slope[1], near[1:2])
        fold = folded(far[0], far[1])
        *pieces, up_sum = weight_grads(
            feed_w,
            scal,
            [("d", 0, 0, 0, 2 * f), ("u", 1, 1, 0, 2 * f)],
            [g_rows, b_rows],
            [active, (near[2], far[2])],
            [0],
            [1],
            [fold] if last else [fold, *attn_sums[index + 1].a()],
        )
        feed_sums[index] = Reduction(pieces)
        deps = pieces[:1]
        if not last:
            deps = [*deps, *feed_sums[index + 1].b()]
        grad_mid, d, sums_two = norm_back(
            grad,
            middle,
            [near[0], swapped(near[1], CORE), swapped(fold, Z_MASK)],
            small,
            index * ROWS + 1,
            deps,
        )
        d_other = swapped(d, CORE)
        deps = () if last else [*feed_sums[index + 1].c(), *attn_sums[index + 1].b()]
        mine, theirs, triple = attention_back(attn_w, scal, d, d_other, qkv, probs, deps)
        moved = swapped(theirs, CORE)
        passed = feed_sums[index].a([moved])

        def chain(deps):
            return norm_back(grad_mid, state, [mine, moved], small, index * ROWS, deps)

        if last:
            grad, g, sums_one = chain(passed)
        *pieces, head_sum = weight_grads(
            attn_w,
            scal,
            [("q", 0, 0, 0, 4 * h), ("k", 0, 0, 4 * h, 4 * h), ("v", 0, 0, 8 * h, 4 * h)]
            + [("o", 1, 1, 0, 4 * h)],
            [(a, a_other), (d, d_other)],
            [(triple,), (mixed,)],
            [1],
            [0],
            [g] if last else [outcome, *feed_sums[index + 1].d()],
        )
        attn_sums[index] = Reduction(pieces)
        if last:
            outcome = joined(
                middle,
                [
                    last_near[0],
                    swapped(tied(last_near[1], [d]), CORE),
                    from_far(last_far[0], tied(last_far[1], [d])),
                ],
                small,
                [index * ROWS + 5, index * ROWS, index * ROWS + 2],
            )[0]
            activations = last_rows(scal, outcome)
        else:
            grad, g, sums_one = chain(pieces[:1])
        small_parts[index] = [sums_one, sums_two, sums_above, head_sum, up_sum]
        sums_above = sums_one
    input_grad = last_rows(scal, grad)
    small = summed_over(packed(scal, small_parts), [CORE])

    final, above = attn_sums
    final.a([*above.c(), *feed_sums[0].b(), grad])
    small = summed_over(tied(small, final.passed[:1]), [Z_MASK, ZL])
    final.b([input_grad, activations, small], True)
    feed_sums[0].c(final.parts[:1])
    moved = final.spread()
    steps, small = reduced_small(tied(small, moved[:1]), lane, own_wide)
    final.direct(moved, [*feed_sums[0].d(), *above.d(), steps[0]])
    ends = reduced_end(
        [a.total for a in attn_sums], [a.total for a in feed_sums], scal, steps[1:2], steps[2:3]
    )
    small = small.reshape(layers, ROWS, -1)
    qkv, out, up, down = call(
        result_kernel,
        [shape(w.shape, F32) for w in row_weights],
        [SMEM] + [VMEM] * 2,
        [scal, *ends],
        deps=[small],
    )
    return (
        activations,
        input_grad,
        qkv.transpose(0, 2, 1, 3),
        out.transpose(0, 2, 1),
        up,
        down.transpose(0, 2, 1),
        small[:, :2],
        small[:, 2:],
    )


def result_kernel(scal, mine, moved, qkv, out, up, down):
    grads = jnp.where(scal[1] != 0, mine[...], moved[...].astype(F32))
    wide, hidden = qkv.shape[3], up.shape[2]
    for layer in range(2):
        at = 4 * wide * layer
        for k in range(3):
            qkv[layer, k] = grads[:, at + k * wide : at + (k + 1) * wide]
        out[layer] = grads[:, at + 3 * wide : at + 4 * wide]
        at = 8 * wide + 2 * hidden * layer
        up[layer] = grads[:, at : at + hidden]
        down[layer] = grads[:, at + hidden : at + 2 * hidden]


def end_kernel(attns, *refs):
    *parts, near, far = refs
    at = 0
    for part in parts[:attns]:
        wide = part.shape[1] // 2
        near[:, at : at + wide] = part[:, :wide]
        far[:, at : at + wide] = part[:, wide:]
        at += wide
    for part in parts[attns:]:
        near[:, at : at + part.shape[1]] = part[...]
        at += part.shape[1]


def end_sum_kernel(scal, near, by_zl, by_zh, by_both, mine, theirs):
    rows = mine.shape[0]
    wide = by_zh.shape[1]
    for core, out in ((scal[2], mine), (1 - scal[2], theirs)):
        cut = pl.ds(pl.multiple_of(core * rows, rows), rows)
        total = near[cut, :].astype(F32) + by_zl[cut, :].astype(F32)
        attn = total[:, :wide] + (by_zh[cut, :].astype(F32) + by_both[cut, :].astype(F32))
        out[:, :wide] = attn.astype(out.dtype)
        out[:, wide:] = total[:, wide:].astype(out.dtype)


def reduced_end(attns, feeds, scal, deps=(), later=()):
    rows, wide = attns[0].shape[0], sum(a.shape[1] // 2 for a in attns)
    whole = wide + sum(f.shape[1] for f in feeds)
    near, far = call(
        functools.partial(end_kernel, len(attns)),
        [shape((rows, whole), BF), shape((rows, wide), BF)],
        [VMEM] * (len(attns) + len(feeds)),
        [*attns, *feeds],
        deps=deps,
    )
    mine, theirs = call(
        end_sum_kernel,
        [shape((rows // 2, whole), F32), shape((rows // 2, whole), BF)],
        [SMEM] + [VMEM] * 4,
        [
            scal,
            near,
            sent_by(near, ZL, zl_is_not_core),
            sent_by(far, ZH, zl_is_core),
            sent_by(far, Z_MASK, zl_is_not_core),
        ],
        deps=later,
    )
    return mine, sent_by(theirs, CORE, zl_is_core)


def solution(mesh):
    in_specs = (
        P(("dp", "tensor"), None),
        P("dp"),
        P(None, "dp", None, "tensor"),
        P(None, "tensor", "dp"),
        P(None, "dp", "tensor"),
        P(None, "tensor", "dp"),
        P(None, None, ("dp", "tensor")),
        P(None, None, ("dp", "tensor")),
        P(("dp", "tensor"), None),
    )
    out_specs = (
        P(("dp", "tensor"), None),
        P(("dp", "tensor"), None),
        P(None, "dp", None, "tensor"),
        P(None, "tensor", "dp"),
        P(None, "dp", "tensor"),
        P(None, "tensor", "dp"),
        P(None, None, ("dp", "tensor")),
        P(None, None, ("dp", "tensor")),
    )
    return jax.shard_map(
        per_device, mesh=mesh, in_specs=in_specs, out_specs=out_specs, check_vma=False
    )
```

time: 1310 us -> 375 us (0.29)
  blocking collectives: 468 us -> 0 us
  waiting for transfers between devices: 501 us -> 122 us
  matrix products: 120 us -> 0 us
  Pallas kernels: 0 us -> 105 us
  local copies, waits for them, and re-layouts: 103 us -> 4.19 us
  starting transfers between devices: 47.2 us -> 134 us
  other arithmetic: 41.6 us -> 0.39 us
    all_gather x1 -> x0, blocking collectives: 323 us -> none  [gather_turned(): whole = lax.all_gather(both, axis, axis=0, tiled=True)]
    reduce_scatter x6 -> x0, waiting for transfers between devices: 204 us -> none  [the longest x4 127 us: forward_sum(): lax.psum_scatter(jnp.dot(left, right, preferred_element_type=jnp.float32)...]
    all_to_all x4 -> x0, blocking collectives: 145 us -> none  [the longest x2 75.9 us: sent_and_summed(): parts = lax.all_to_all(split_up(array, dim, peers), axis, 0, 0, tiled=True)]
    unnamed x10 -> x0, waiting for transfers between devices: 139 us -> none
    ppermute x0 -> x109, starting transfers between devices: none -> 134 us  [the longest x48 55.3 us: swapped(): return lax.ppermute(array, PLACES, [(i, i ^ mask) for i in range(DEVICES)])]
    ppermute x0 -> x109, waiting for transfers between devices: none -> 122 us  [the longest x49 64.9 us: along(): return lax.ppermute(array, PLACES, pairs)]
    dot_general x36 -> x0, matrix products: 120 us -> none  [the longest x2 20 us: per_device(): hidden = jnp.dot(second, w_u, preferred_element_type=jnp.float32) + bias_up]
    all_to_all x8 -> x0, waiting for transfers between devices: 112 us -> none  [the longest x6 105 us: sent_to_all(): return lax.all_to_all(copies, axis, split_axis=0, concat_axis=0, tiled=True)]
  transfers between devices with their start and end apart: 17 -> 109, of which waited for: 13 -> 52; matrix products, arithmetic and copies ran while one was open for 11% -> 1% of each run, Pallas kernels for 0% -> 27%
where the time goes in v1:
time: 375 us; the launch traced here: 368 us
  starting transfers between devices  134 us (36%)
  waiting for transfers between devices  122 us (33%)
  Pallas kernels  105 us (28%)
  local copies, waits for them, and re-layouts  4.19 us (1%)
    pallas_call x71, Pallas kernels, call(): pl.pallas_call(kernel, grid=(1,) if windowed else (), out_shape=tuple(out...  105 us
    ppermute x49, waiting for transfers between devices, along(): return lax.ppermute(array, PLACES, pairs)  64.9 us
    ppermute x48, starting transfers between devices, swapped(): return lax.ppermute(array, PLACES, [(i, i ^ mask) for i in range(DEVICES)])  55.3 us
    ppermute x49, starting transfers between devices, along(): return lax.ppermute(array, PLACES, pairs)  54.3 us
    ppermute x48, waiting for transfers between devices, swapped(): return lax.ppermute(array, PLACES, [(i, i ^ mask) for i in range(DEVICES)])  51.8 us
    ppermute x12, starting transfers between devices, sent_by(): lax.ppermute(array, PLACES, [(i, i ^ mask) for i in range(DEVICES) if sen...  24.1 us
  transfers between devices with their start and end apart: 109, of which 52 were waited for; matrix products, arithmetic and copies ran while one was open for 1% of the time, Pallas kernels for 27%

profile of v1, /device:TPU:0, one launch (start us, length us, event | category | flops | bytes accessed | tf_op | source)
XLA Modules:
  0.0 367.7 jit_solution(9843220476194285034)
XLA Ops:
  7.1 3.3 collective-permute-start.3
  11.1 3.8 %collective-permute-start.11 = (bf16[128,1536]{1,0:T(8,128)(2,1)S(1)}, bf16[128,1536]{1,0:T(8,128)(2,1)S(1)}, u32[]{:S(2)}, u32[]{:S(2)}) collective-permute-start(bf16[128,1536]{1,0:T(8,128)(2,1)S(1)} %pad_maximum_fusion), channel_id=1, source_target_pairs={{0,1},{2,3},{4,5},{6,7},{9,8},{11,10},{13,12},{15,14},{16,17},{18,... | collective-permute-start | bytes 1179656 | tf_op jit(solution)/shard_map/ppermute | solution.py:40
  14.9 5.5 %collective-permute-start.12 = (bf16[128,1024]{1,0:T(8,128)(2,1)S(1)}, bf16[128,1024]{1,0:T(8,128)(2,1)S(1)}, u32[]{:S(2)}, u32[]{:S(2)}) collective-permute-start(bf16[128,1024]{1,0:T(8,128)(2,1)S(1)} %get-tuple-element.297), channel_id=1, source_target_pairs={{0,2},{2,0},{4,6},{6,4},{9,11},{11,9},{13,15},{15,13},{16,18},{18,... | collective-permute-start | bytes 786440 | tf_op jit(solution)/shard_map/ppermute | solution.py:40
  23.3 2.3 collective-permute-done.4
  25.7 2.8 collective-permute-start.5
  31.6 6.7 %collective-permute-done.14.refs_0_.refs_1_ = bf16[128,2048]{1,0:T(8,128)(2,1)S(1)} collective-permute-done((bf16[128,2048]{1,0:T(8,128)(2,1)S(1)}, bf16[128,2048]{1,0:T(8,128)(2,1)S(1)}, u32[]{:S(2)}, u32[]{:S(2)}) %collective-permute-start.14) | collective-permute-done | bytes 524320 | tf_op jit(solution)/shard_map/ppermute | solution.py:126
  42.2 6.1 %collective-permute-done.16.refs_2_ = bf16[128,1024]{1,0:T(8,128)(2,1)S(1)} collective-permute-done((bf16[128,1024]{1,0:T(8,128)(2,1)S(1)}, bf16[128,1024]{1,0:T(8,128)(2,1)S(1)}, u32[]{:S(2)}, u32[]{:S(2)}) %collective-permute-start.16) | collective-permute-done | bytes 262176 | tf_op jit(solution)/shard_map/ppermute | solution.py:126
  50.7 2.2 collective-permute-start.22
  53.5 2.7 collective-permute-start.7
  56.2 4.0 %collective-permute-done.7 = f32[24,1024]{1,0:T(8,128)S(1)} collective-permute-done((f32[24,1024]{1,0:T(8,128)S(1)}, f32[24,1024]{1,0:T(8,128)S(1)}, u32[]{:S(2)}, u32[]{:S(2)}) %collective-permute-start.7) | collective-permute-done | bytes 98336 | tf_op jit(solution)/shard_map/ppermute | solution.py:36
  66.9 2.1 collective-permute-start.23
  70.7 2.5 collective-permute-done.21.refs_2_
  73.2 5.8 %collective-permute-done.19.refs_4_.refs_6_.refs_7_ = bf16[2,128,1024]{2,1,0:T(8,128)(2,1)S(1)} collective-permute-done((bf16[2,128,1024]{2,1,0:T(8,128)(2,1)S(1)}, bf16[2,128,1024]{2,1,0:T(8,128)(2,1)S(1)}, u32[]{:S(2)}, u32[]{:S(2)}) %collective-permute-start.19) | collective-permute-done | bytes 524320 | tf_op jit(solution)/shard_map/ppermute | solution.py:126
  81.6 6.1 %shard_map.164 = (f32[160,1024]{1,0:T(8,128)S(1)}, bf16[160,1024]{1,0:T(8,128)(2,1)S(1)}, bf16[320,1536]{1,0:T(8,128)(2,1)}, bf16[8,320,320]{2,1,0:T(8,128)(2,1)}, bf16[320,512]{1,0:T(8,128)(2,1)}) custom-call(s32[7]{0:T(128)S(1)} %stack.32.refs_0_, bf16[160,1024]{1,0:T(8,128)(2,1)S(1)} %get-tuple-element.144.refs_6_.refs_1_, ...), custom_call_target="tpu_custom_call" | custom-call | flops 6899999744 | bytes 1 | tf_op jit(solution)/shard_map/pallas_call | solution.py:79
  87.7 2.2 collective-permute-start.25
  93.2 4.2 %collective-permute-start.32 = (bf16[160,1024]{1,0:T(8,128)(2,1)S(1)}, bf16[160,1024]{1,0:T(8,128)(2,1)S(1)}, u32[]{:S(2)}, u32[]{:S(2)}) collective-permute-start(bf16[160,1024]{1,0:T(8,128)(2,1)S(1)} %get-tuple-element.155.refs_2_.refs_1_.refs_5_), channel_id=1, source_target_pairs={{0,3},{1,2},{2,1},{3,0},{4,7},{5,6},{6,5},{7,4},{8,11},{9,10},{10,... | collective-permute-start | bytes 983048 | tf_op jit(solution)/shard_map/ppermute | solution.py:36
  99.4 5.7 %collective-permute-done.32.refs_1_.refs_7_ = bf16[160,1024]{1,0:T(8,128)(2,1)S(1)} collective-permute-done((bf16[160,1024]{1,0:T(8,128)(2,1)S(1)}, bf16[160,1024]{1,0:T(8,128)(2,1)S(1)}, u32[]{:S(2)}, u32[]{:S(2)}) %collective-permute-start.32) | collective-permute-done | bytes 327712 | tf_op jit(solution)/shard_map/ppermute | solution.py:36
  105.1 2.2 collective-permute-start.34
  107.7 4.9 %collective-permute-done.34.refs_9_.refs_2_ = bf16[128,1024]{1,0:T(8,128)(2,1)S(1)} collective-permute-done((bf16[128,1024]{1,0:T(8,128)(2,1)S(1)}, bf16[128,1024]{1,0:T(8,128)(2,1)S(1)}, u32[]{:S(2)}, u32[]{:S(2)}) %collective-permute-start.34) | collective-permute-done | bytes 262176 | tf_op jit(solution)/shard_map/ppermute | solution.py:126
  115.5 3.7 shard_map.168
  119.7 3.5 shard_map.169
  123.6 3.0 collective-permute-start.38
  127.6 2.5 collective-permute-done.41.refs_1_.refs_8_.refs_9_
  131.6 3.0 collective-permute-start.46
  135.4 2.1 shard_map.171
  138.1 4.0 %collective-permute-done.46.refs_6_.refs_1_.refs_3_ = bf16[160,1024]{1,0:T(8,128)(2,1)S(1)} collective-permute-done((bf16[160,1024]{1,0:T(8,128)(2,1)S(1)}, bf16[160,1024]{1,0:T(8,128)(2,1)S(1)}, u32[]{:S(2)}, u32[]{:S(2)}) %collective-permute-start.46) | collective-permute-done | bytes 327712 | tf_op jit(solution)/shard_map/ppermute | solution.py:36
  144.2 6.1 %shard_map.175 = (f32[160,1024]{1,0:T(8,128)S(1)}, bf16[160,1024]{1,0:T(8,128)(2,1)S(1)}, bf16[320,1536]{1,0:T(8,128)(2,1)}, bf16[8,320,320]{2,1,0:T(8,128)(2,1)}, bf16[320,512]{1,0:T(8,128)(2,1)}) custom-call(s32[7]{0:T(128)S(1)} %stack.32.refs_0_, bf16[160,1024]{1,0:T(8,128)(2,1)S(1)} %get-tuple-element.163.refs_6_.refs_1_, ...), custom_call_target="tpu_custom_call" | custom-call | flops 6899999744 | bytes 1 | tf_op jit(solution)/shard_map/pallas_call | solution.py:79
  154.1 3.0 collective-permute-start.53
  160.5 4.6 %collective-permute-done.53.refs_1_.refs_7_ = bf16[160,1024]{1,0:T(8,128)(2,1)S(1)} collective-permute-done((bf16[160,1024]{1,0:T(8,128)(2,1)S(1)}, bf16[160,1024]{1,0:T(8,128)(2,1)S(1)}, u32[]{:S(2)}, u32[]{:S(2)}) %collective-permute-start.53) | collective-permute-done | bytes 327712 | tf_op jit(solution)/shard_map/ppermute | solution.py:36
  166.7 2.2 collective-permute-done.51.refs_6_
  169.6 3.6 shard_map.178
  173.2 3.3 shard_map.179
  176.6 3.6 shard_map.180
  180.1 3.3 shard_map.181
  184.0 3.5 collective-permute-start.57
  187.5 5.5 %shard_map.183 = (bf16[4,128,1024]{2,1,0:T(8,128)(2,1)S(1)}, bf16[4,128,1024]{2,1,0:T(8,128)(2,1)S(1)}, bf16[2,128,1024]{2,1,0:T(8,128)(2,1)S(1)}, bf16[2,128,10...) custom-call(s32[7]{0:T(128)S(1)} %stack.32.refs_0_, ...), custom_call_target="tpu_custom_call" | custom-call | flops 5750000128 | bytes 1 | tf_op jit(solution)/shard_map/pallas_call | solution.py:79
  193.0 2.4 collective-permute-done.57.refs_5_
  198.9 7.2 %shard_map.190 = (f32[160,1024]{1,0:T(8,128)S(1)}, bf16[160,1024]{1,0:T(8,128)(2,1)S(1)}, bf16[320,1536]{1,0:T(8,128)(2,1)S(1)}) custom-call(s32[7]{0:T(128)S(1)} %stack.32.refs_0_, bf16[160,1024]{1,0:T(8,128)(2,1)S(1)} %get-tuple-element.186.refs_1_.refs_3_, bf16[160,1024]{1,0:T(8,128)(2,1)S(1)} %collective-permute-done.62.refs_2_.refs_4_, ...), custom_call_target="tpu_custom_call" | custom-call | flops 8049999872 | bytes 1 | tf_op jit(solution)/shard_map/pallas_call | solution.py:79
  211.7 2.6 collective-permute-start.68
  216.3 4.1 %shard_map.196 = (bf16[4,128,1024]{2,1,0:T(8,128)(2,1)S(1)}, bf16[4,128,1024]{2,1,0:T(8,128)(2,1)S(1)}, bf16[2,128,1024]{2,1,0:T(8,128)(2,1)S(1)}, bf16[2,128,10...) custom-call(s32[7]{0:T(128)S(1)} %stack.32.refs_0_, ...), custom_call_target="tpu_custom_call" | custom-call | flops 5750000128 | bytes 1 | tf_op jit(solution)/shard_map/pallas_call | solution.py:79
  222.6 3.2 shard_map.193
  225.8 3.3 shard_map.194
  229.8 6.2 %collective-permute-done.73.refs_3_ = bf16[2,128,1024]{2,1,0:T(8,128)(2,1)S(1)} collective-permute-done((bf16[2,128,1024]{2,1,0:T(8,128)(2,1)S(1)}, bf16[2,128,1024]{2,1,0:T(8,128)(2,1)S(1)}, u32[]{:S(2)}, u32[]{:S(2)}) %collective-permute-start.73) | collective-permute-done | bytes 524320 | tf_op jit(solution)/shard_map/ppermute | solution.py:126
  239.2 2.5 collective-permute-start.77
  241.8 5.5 %shard_map.198 = (bf16[4,128,1024]{2,1,0:T(8,128)(2,1)S(1)}, bf16[4,128,1024]{2,1,0:T(8,128)(2,1)S(1)}, bf16[2,128,1024]{2,1,0:T(8,128)(2,1)S(1)}, bf16[2,128,10...) custom-call(s32[7]{0:T(128)S(1)} %stack.32.refs_0_, ...), custom_call_target="tpu_custom_call" | custom-call | flops 5750000128 | bytes 1 | tf_op jit(solution)/shard_map/pallas_call | solution.py:79
  250.0 5.6 %collective-permute-done.77.refs_1_ = bf16[2,128,1024]{2,1,0:T(8,128)(2,1)S(1)} collective-permute-done((bf16[2,128,1024]{2,1,0:T(8,128)(2,1)S(1)}, bf16[2,128,1024]{2,1,0:T(8,128)(2,1)S(1)}, u32[]{:S(2)}, u32[]{:S(2)}) %collective-permute-start.77) | collective-permute-done | bytes 524320 | tf_op jit(solution)/shard_map/ppermute | solution.py:126
  260.4 7.2 %shard_map.203 = (f32[160,1024]{1,0:T(8,128)S(1)}, bf16[160,1024]{1,0:T(8,128)(2,1)S(1)}, bf16[320,1536]{1,0:T(8,128)(2,1)S(1)}) custom-call(s32[7]{0:T(128)S(1)} %stack.32.refs_0_, bf16[160,1024]{1,0:T(8,128)(2,1)S(1)} %get-tuple-element.223.refs_1_.refs_3_, bf16[160,1024]{1,0:T(8,128)(2,1)S(1)} %collective-permute-done.76.refs_2_.refs_4_, ...), custom_call_target="tpu_custom_call" | custom-call | flops 8049999872 | bytes 1 | tf_op jit(solution)/shard_map/pallas_call | solution.py:79
  268.3 2.3 shard_map.188
  274.8 4.1 %shard_map.205 = (bf16[4,128,1024]{2,1,0:T(8,128)(2,1)S(1)}, bf16[4,128,1024]{2,1,0:T(8,128)(2,1)S(1)}, bf16[2,128,1024]{2,1,0:T(8,128)(2,1)S(1)}, bf16[2,128,10...) custom-call(s32[7]{0:T(128)S(1)} %stack.32.refs_0_, ...), custom_call_target="tpu_custom_call" | custom-call | flops 5750000128 | bytes 1 | tf_op jit(solution)/shard_map/pallas_call | solution.py:79
  281.6 2.4 shard_map.206
  284.0 2.2 collective-permute-done.85.refs_1_
  287.4 4.0 %collective-permute-done.89.refs_2_ = bf16[4,128,1024]{2,1,0:T(8,128)(2,1)S(1)} collective-permute-done((bf16[4,128,1024]{2,1,0:T(8,128)(2,1)S(1)}, bf16[4,128,1024]{2,1,0:T(8,128)(2,1)S(1)}, u32[]{:S(2)}, u32[]{:S(2)}) %collective-permute-start.89) | collective-permute-done | bytes 1048608 | tf_op jit(solution)/shard_map/ppermute | solution.py:126
  293.1 4.0 %collective-permute-done.84.refs_3_ = bf16[2,128,1024]{2,1,0:T(8,128)(2,1)S(1)} collective-permute-done((bf16[2,128,1024]{2,1,0:T(8,128)(2,1)S(1)}, bf16[2,128,1024]{2,1,0:T(8,128)(2,1)S(1)}, u32[]{:S(2)}, u32[]{:S(2)}) %collective-permute-start.84) | collective-permute-done | bytes 524320 | tf_op jit(solution)/shard_map/ppermute | solution.py:126
  301.3 4.5 %collective-permute-start.92 = (f32[24,1024]{1,0:T(8,128)S(1)}, f32[24,1024]{1,0:T(8,128)S(1)}, u32[]{:S(2)}, u32[]{:S(2)}) collective-permute-start(f32[24,1024]{1,0:T(8,128)S(1)} %shard_map.212), channel_id=1, source_target_pairs={{0,8},{1,9},{2,10},{3,11},{4,12},{5,13},{6,14},{7,15},{8,0},{9,1},... | collective-permute-start | bytes 294920 | tf_op jit(solution)/shard_map/ppermute | solution.py:36
  306.8 2.5 collective-permute-start.93
  309.3 3.8 %collective-permute-done.93 = f32[24,1024]{1,0:T(8,128)S(1)} collective-permute-done((f32[24,1024]{1,0:T(8,128)S(1)}, f32[24,1024]{1,0:T(8,128)S(1)}, u32[]{:S(2)}, u32[]{:S(2)}) %collective-permute-start.93) | collective-permute-done | bytes 98336 | tf_op jit(solution)/shard_map/ppermute | solution.py:36
  315.4 2.9 collective-permute-start.94
  325.4 2.2 collective-permute-start.96
  332.3 5.1 %collective-permute-done.101 = f32[24,512]{1,0:T(8,128)S(1)} collective-permute-done((f32[24,512]{1,0:T(8,128)S(1)}, f32[24,512]{1,0:T(8,128)S(1)}, u32[]{:S(2)}, u32[]{:S(2)}) %collective-permute-start.101) | collective-permute-done | bytes 49184 | tf_op jit(solution)/shard_map/ppermute | solution.py:36
  338.2 3.2 collective-permute-done.102
  342.8 4.7 %collective-permute-start.104 = (bf16[128,1024]{1,0:T(8,128)(2,1)S(1)}, bf16[128,1024]{1,0:T(8,128)(2,1)S(1)}, u32[]{:S(2)}, u32[]{:S(2)}) collective-permute-start(bf16[128,1024]{1,0:T(8,128)(2,1)S(1)} %get-tuple-element.271), channel_id=1, source_target_pairs={{0,2},{2,0},{4,6},{6,4},{9,11},{11,9},{13,15},{15,13},{16,18},{18,... | collective-permute-start | bytes 786440 | tf_op jit(solution)/shard_map/ppermute | solution.py:40
  350.2 3.5 collective-permute-done.106
  355.4 2.2 collective-permute-done.105.refs_4_
  360.4 3.7 %collective-permute-done.108 = f32[24,128]{1,0:T(8,128)S(1)} collective-permute-done((f32[24,128]{1,0:T(8,128)S(1)}, f32[24,128]{1,0:T(8,128)S(1)}, u32[]{:S(2)}, u32[]{:S(2)}) %collective-permute-start.108) | collective-permute-done | bytes 12320 | tf_op jit(solution)/shard_map/ppermute | solution.py:36
  (284 shorter events, 122.5 us)
Async XLA Ops:
  7.1 14.7 %collective-permute-start.3 = (f32[24,128]{1,0:T(8,128)S(1)}, f32[24,128]{1,0:T(8,128)S(1)}, u32[]{:S(2)}, u32[]{:S(2)}) collective-permute-start(f32[24,128]{1,0:T(8,128)S(1)} %add.68), channel_id=1, source_target_pairs={{0,20},{1,21},{2,22},{3,23},{4,16},{5,17},{6,18},{7,19},{8,28},{9,... | collective-permute-start | bytes 36872 | tf_op jit(solution)/shard_map/ppermute | solution.py:36
  11.1 17.4 %collective-permute-start.11 = (bf16[128,1536]{1,0:T(8,128)(2,1)S(1)}, bf16[128,1536]{1,0:T(8,128)(2,1)S(1)}, u32[]{:S(2)}, u32[]{:S(2)}) collective-permute-start(bf16[128,1536]{1,0:T(8,128)(2,1)S(1)} %pad_maximum_fusion), channel_id=1, source_target_pairs={{0,1},{2,3},{4,5},{6,7},{9,8},{11,10},{13,12},{15,14},{16,17},{18,... | collective-permute-start | bytes 1179656 | tf_op jit(solution)/shard_map/ppermute | solution.py:40
  14.9 13.5 %collective-permute-start.12 = (bf16[128,1024]{1,0:T(8,128)(2,1)S(1)}, bf16[128,1024]{1,0:T(8,128)(2,1)S(1)}, u32[]{:S(2)}, u32[]{:S(2)}) collective-permute-start(bf16[128,1024]{1,0:T(8,128)(2,1)S(1)} %get-tuple-element.297), channel_id=1, source_target_pairs={{0,2},{2,0},{4,6},{6,4},{9,11},{11,9},{13,15},{15,13},{16,18},{18,... | collective-permute-start | bytes 786440 | tf_op jit(solution)/shard_map/ppermute | solution.py:40
  29.3 10.4 %collective-permute-start.15 = (bf16[128,2048]{1,0:T(8,128)(2,1)S(1)}, bf16[128,2048]{1,0:T(8,128)(2,1)S(1)}, u32[]{:S(2)}, u32[]{:S(2)}) collective-permute-start(bf16[128,2048]{1,0:T(8,128)(2,1)S(1)} %shard_map.156.refs_0_), channel_id=1, source_target_pairs={{0,20},{1,21},{2,22},{3,23},{4,16},{5,17},{6,18},{7,19},{8,104},{9... | collective-permute-start | bytes 1572872 | tf_op jit(solution)/shard_map/ppermute | solution.py:126
  48.4 14.9 %collective-permute-start.17 = (bf16[4,128,1024]{2,1,0:T(8,128)(2,1)S(1)}, bf16[4,128,1024]{2,1,0:T(8,128)(2,1)S(1)}, u32[]{:S(2)}, u32[]{:S(2)}) collective-permute-start(bf16[4,128,1024]{2,1,0:T(8,128)(2,1)S(1)} %shard_map.158.refs_4_.refs_5_), channel_id=1, source_target_pairs={{0,32},{1,33},{2,34},{3,35},{4,36},{5,37},{6,38},{7,39},{8,12},{9,... | collective-permute-start | bytes 3145736 | tf_op jit(solution)/shard_map/ppermute | solution.py:126
  48.7 16.0 %collective-permute-start.18 = (bf16[4,128,1024]{2,1,0:T(8,128)(2,1)S(1)}, bf16[4,128,1024]{2,1,0:T(8,128)(2,1)S(1)}, u32[]{:S(2)}, u32[]{:S(2)}) collective-permute-start(bf16[4,128,1024]{2,1,0:T(8,128)(2,1)S(1)} %shard_map.158.refs_4_.refs_5_), channel_id=1, source_target_pairs={{0,96},{1,97},{2,98},{3,99},{4,100},{5,101},{6,102},{7,103},{8,28}... | collective-permute-start | bytes 3145736 | tf_op jit(solution)/shard_map/ppermute | solution.py:126
  50.7 10.9 %collective-permute-start.22 = (bf16[128,1536]{1,0:T(8,128)(2,1)S(1)}, bf16[128,1536]{1,0:T(8,128)(2,1)S(1)}, u32[]{:S(2)}, u32[]{:S(2)}) collective-permute-start(bf16[128,1536]{1,0:T(8,128)(2,1)S(1)} %pad_maximum_fusion.1), channel_id=1, source_target_pairs={{0,1},{2,3},{4,5},{6,7},{9,8},{11,10},{13,12},{15,14},{16,17},{18,... | collective-permute-start | bytes 1179656 | tf_op jit(solution)/shard_map/ppermute | solution.py:40
  52.8 14.0 %collective-permute-start.1 = (bf16[160,1024]{1,0:T(8,128)(2,1)S(1)}, bf16[160,1024]{1,0:T(8,128)(2,1)S(1)}, u32[]{:S(2)}, u32[]{:S(2)}) collective-permute-start(bf16[160,1024]{1,0:T(8,128)(2,1)S(1)} %copy-done.4), channel_id=1, source_target_pairs={{1,8},{3,10},{5,12},{7,14},{8,1},{10,3},{12,5},{14,7},{17,24},{19,... | collective-permute-start | bytes 983048 | tf_op jit(solution)/shard_map/ppermute | solution.py:40
  64.8 14.2 %collective-permute-start.19 = (bf16[2,128,1024]{2,1,0:T(8,128)(2,1)S(1)}, bf16[2,128,1024]{2,1,0:T(8,128)(2,1)S(1)}, u32[]{:S(2)}, u32[]{:S(2)}) collective-permute-start(bf16[2,128,1024]{2,1,0:T(8,128)(2,1)S(1)} %get-tuple-element.146.refs_1_), channel_id=1, source_target_pairs={{0,96},{1,97},{2,98},{3,99},{4,100},{5,101},{6,102},{7,103},{8,28}... | collective-permute-start | bytes 1572872 | tf_op jit(solution)/shard_map/ppermute | solution.py:126
  66.8 12.9 %collective-permute-start.20 = (bf16[2,128,1024]{2,1,0:T(8,128)(2,1)S(1)}, bf16[2,128,1024]{2,1,0:T(8,128)(2,1)S(1)}, u32[]{:S(2)}, u32[]{:S(2)}) collective-permute-start(bf16[2,128,1024]{2,1,0:T(8,128)(2,1)S(1)} %get-tuple-element.147.refs_2_), channel_id=1, source_target_pairs={{0,32},{1,33},{2,34},{3,35},{4,36},{5,37},{6,38},{7,39},{8,12},{9,... | collective-permute-start | bytes 1572872 | tf_op jit(solution)/shard_map/ppermute | solution.py:126
  66.9 13.0 %collective-permute-start.23 = (bf16[128,2048]{1,0:T(8,128)(2,1)S(1)}, bf16[128,2048]{1,0:T(8,128)(2,1)S(1)}, u32[]{:S(2)}, u32[]{:S(2)}) collective-permute-start(bf16[128,2048]{1,0:T(8,128)(2,1)S(1)} %shard_map.162.refs_0_), channel_id=1, source_target_pairs={{0,4},{1,5},{2,6},{3,7},{4,0},{5,1},{6,2},{7,3},{8,40},{9,41},{10,... | collective-permute-start | bytes 1572872 | tf_op jit(solution)/shard_map/ppermute | solution.py:126
  68.9 12.6 %collective-permute-start.24 = (bf16[128,2048]{1,0:T(8,128)(2,1)S(1)}, bf16[128,2048]{1,0:T(8,128)(2,1)S(1)}, u32[]{:S(2)}, u32[]{:S(2)}) collective-permute-start(bf16[128,2048]{1,0:T(8,128)(2,1)S(1)} %shard_map.162.refs_0_), channel_id=1, source_target_pairs={{0,20},{1,21},{2,22},{3,23},{4,16},{5,17},{6,18},{7,19},{8,104},{9... | collective-permute-start | bytes 1572872 | tf_op jit(solution)/shard_map/ppermute | solution.py:126
  79.0 10.9 %collective-permute-start.26 = (f32[160,1024]{1,0:T(8,128)S(1)}, f32[160,1024]{1,0:T(8,128)S(1)}, u32[]{:S(2)}, u32[]{:S(2)}) collective-permute-start(f32[160,1024]{1,0:T(8,128)S(1)} %copy-done.2), channel_id=1, source_target_pairs={{1,8},{3,10},{5,12},{7,14},{8,1},{10,3},{12,5},{14,7},{17,24},{19,... | collective-permute-start | bytes 1966088 | tf_op jit(solution)/shard_map/ppermute | solution.py:40
  79.8 17.6 %collective-permute-start.28 = (bf16[4,128,1024]{2,1,0:T(8,128)(2,1)S(1)}, bf16[4,128,1024]{2,1,0:T(8,128)(2,1)S(1)}, u32[]{:S(2)}, u32[]{:S(2)}) collective-permute-start(bf16[4,128,1024]{2,1,0:T(8,128)(2,1)S(1)} %shard_map.160.refs_9_.refs_4_), channel_id=1, source_target_pairs={{0,32},{1,33},{2,34},{3,35},{4,36},{5,37},{6,38},{7,39},{8,12},{9,... | collective-permute-start | bytes 3145736 | tf_op jit(solution)/shard_map/ppermute | solution.py:126
  79.9 17.5 %collective-permute-start.29 = (bf16[4,128,1024]{2,1,0:T(8,128)(2,1)S(1)}, bf16[4,128,1024]{2,1,0:T(8,128)(2,1)S(1)}, u32[]{:S(2)}, u32[]{:S(2)}) collective-permute-start(bf16[4,128,1024]{2,1,0:T(8,128)(2,1)S(1)} %shard_map.160.refs_9_.refs_4_), channel_id=1, source_target_pairs={{0,96},{1,97},{2,98},{3,99},{4,100},{5,101},{6,102},{7,103},{8,28}... | collective-permute-start | bytes 3145736 | tf_op jit(solution)/shard_map/ppermute | solution.py:126
  93.2 11.9 %collective-permute-start.32 = (bf16[160,1024]{1,0:T(8,128)(2,1)S(1)}, bf16[160,1024]{1,0:T(8,128)(2,1)S(1)}, u32[]{:S(2)}, u32[]{:S(2)}) collective-permute-start(bf16[160,1024]{1,0:T(8,128)(2,1)S(1)} %get-tuple-element.155.refs_2_.refs_1_.refs_5_), channel_id=1, source_target_pairs={{0,3},{1,2},{2,1},{3,0},{4,7},{5,6},{6,5},{7,4},{8,11},{9,10},{10,... | collective-permute-start | bytes 983048 | tf_op jit(solution)/shard_map/ppermute | solution.py:36
  97.4 15.2 %collective-permute-start.30 = (bf16[2,128,1024]{2,1,0:T(8,128)(2,1)S(1)}, bf16[2,128,1024]{2,1,0:T(8,128)(2,1)S(1)}, u32[]{:S(2)}, u32[]{:S(2)}) collective-permute-start(bf16[2,128,1024]{2,1,0:T(8,128)(2,1)S(1)} %get-tuple-element.156), channel_id=1, source_target_pairs={{0,96},{1,97},{2,98},{3,99},{4,100},{5,101},{6,102},{7,103},{8,28}... | collective-permute-start | bytes 1572872 | tf_op jit(solution)/shard_map/ppermute | solution.py:126
  99.4 13.3 %collective-permute-start.31 = (bf16[2,128,1024]{2,1,0:T(8,128)(2,1)S(1)}, bf16[2,128,1024]{2,1,0:T(8,128)(2,1)S(1)}, u32[]{:S(2)}, u32[]{:S(2)}) collective-permute-start(bf16[2,128,1024]{2,1,0:T(8,128)(2,1)S(1)} %get-tuple-element.157), channel_id=1, source_target_pairs={{0,32},{1,33},{2,34},{3,35},{4,36},{5,37},{6,38},{7,39},{8,12},{9,... | collective-permute-start | bytes 1572872 | tf_op jit(solution)/shard_map/ppermute | solution.py:126
  105.1 10.4 %collective-permute-start.33 = (bf16[160,1024]{1,0:T(8,128)(2,1)S(1)}, bf16[160,1024]{1,0:T(8,128)(2,1)S(1)}, u32[]{:S(2)}, u32[]{:S(2)}) collective-permute-start(bf16[160,1024]{1,0:T(8,128)(2,1)S(1)} %collective-permute-done.32.refs_1_.refs_7_), channel_id=1, source_target_pairs={{0,8},{1,9},{2,10},{3,11},{4,12},{5,13},{6,14},{7,15},{8,0},{9,1},... | collective-permute-start | bytes 983048 | tf_op jit(solution)/shard_map/ppermute | solution.py:36
  112.7 14.9 %collective-permute-start.40 = (bf16[4,128,1024]{2,1,0:T(8,128)(2,1)S(1)}, bf16[4,128,1024]{2,1,0:T(8,128)(2,1)S(1)}, u32[]{:S(2)}, u32[]{:S(2)}) collective-permute-start(bf16[4,128,1024]{2,1,0:T(8,128)(2,1)S(1)} %shard_map.172.refs_4_.refs_5_), channel_id=1, source_target_pairs={{0,32},{1,33},{2,34},{3,35},{4,36},{5,37},{6,38},{7,39},{8,12},{9,... | collective-permute-start | bytes 3145736 | tf_op jit(solution)/shard_map/ppermute | solution.py:126
  114.1 16.0 %collective-permute-start.41 = (bf16[4,128,1024]{2,1,0:T(8,128)(2,1)S(1)}, bf16[4,128,1024]{2,1,0:T(8,128)(2,1)S(1)}, u32[]{:S(2)}, u32[]{:S(2)}) collective-permute-start(bf16[4,128,1024]{2,1,0:T(8,128)(2,1)S(1)} %shard_map.172.refs_4_.refs_5_), channel_id=1, source_target_pairs={{0,96},{1,97},{2,98},{3,99},{4,100},{5,101},{6,102},{7,103},{8,28}... | collective-permute-start | bytes 3145736 | tf_op jit(solution)/shard_map/ppermute | solution.py:126
  123.3 11.3 %collective-permute-start.36 = (bf16[160,1024]{1,0:T(8,128)(2,1)S(1)}, bf16[160,1024]{1,0:T(8,128)(2,1)S(1)}, u32[]{:S(2)}, u32[]{:S(2)}) collective-permute-start(bf16[160,1024]{1,0:T(8,128)(2,1)S(1)} %get-tuple-element.160), channel_id=1, source_target_pairs={{0,8},{1,9},{2,10},{3,11},{4,12},{5,13},{6,14},{7,15},{8,0},{9,1},... | collective-permute-start | bytes 983048 | tf_op jit(solution)/shard_map/ppermute | solution.py:36
  123.6 11.8 %collective-permute-start.38 = (bf16[160,1024]{1,0:T(8,128)(2,1)S(1)}, bf16[160,1024]{1,0:T(8,128)(2,1)S(1)}, u32[]{:S(2)}, u32[]{:S(2)}) collective-permute-start(bf16[160,1024]{1,0:T(8,128)(2,1)S(1)} %shard_map.170), channel_id=1, source_target_pairs={{0,3},{1,2},{2,1},{3,0},{4,7},{5,6},{6,5},{7,4},{8,11},{9,10},{10,... | collective-permute-start | bytes 983048 | tf_op jit(solution)/shard_map/ppermute | solution.py:36
  130.2 11.9 %collective-permute-start.42 = (bf16[2,128,1024]{2,1,0:T(8,128)(2,1)S(1)}, bf16[2,128,1024]{2,1,0:T(8,128)(2,1)S(1)}, u32[]{:S(2)}, u32[]{:S(2)}) collective-permute-start(bf16[2,128,1024]{2,1,0:T(8,128)(2,1)S(1)} %get-tuple-element.164), channel_id=1, source_target_pairs={{0,96},{1,97},{2,98},{3,99},{4,100},{5,101},{6,102},{7,103},{8,28}... | collective-permute-start | bytes 1572872 | tf_op jit(solution)/shard_map/ppermute | solution.py:126
  131.6 10.4 %collective-permute-start.43 = (bf16[2,128,1024]{2,1,0:T(8,128)(2,1)S(1)}, bf16[2,128,1024]{2,1,0:T(8,128)(2,1)S(1)}, u32[]{:S(2)}, u32[]{:S(2)}) collective-permute-start(bf16[2,128,1024]{2,1,0:T(8,128)(2,1)S(1)} %get-tuple-element.165), channel_id=1, source_target_pairs={{0,32},{1,33},{2,34},{3,35},{4,36},{5,37},{6,38},{7,39},{8,12},{9,... | collective-permute-start | bytes 1572872 | tf_op jit(solution)/shard_map/ppermute | solution.py:126
  131.6 10.4 %collective-permute-start.46 = (bf16[160,1024]{1,0:T(8,128)(2,1)S(1)}, bf16[160,1024]{1,0:T(8,128)(2,1)S(1)}, u32[]{:S(2)}, u32[]{:S(2)}) collective-permute-start(bf16[160,1024]{1,0:T(8,128)(2,1)S(1)} %get-tuple-element.153.refs_4_.refs_1_), channel_id=1, source_target_pairs={{0,3},{1,2},{2,1},{3,0},{4,7},{5,6},{6,5},{7,4},{8,11},{9,10},{10,... | collective-permute-start | bytes 983048 | tf_op jit(solution)/shard_map/ppermute | solution.py:36
  137.6 12.8 %collective-permute-start.45 = (bf16[160,1024]{1,0:T(8,128)(2,1)S(1)}, bf16[160,1024]{1,0:T(8,128)(2,1)S(1)}, u32[]{:S(2)}, u32[]{:S(2)}) collective-permute-start(bf16[160,1024]{1,0:T(8,128)(2,1)S(1)} %get-tuple-element.153.refs_4_.refs_1_), channel_id=1, source_target_pairs={{0,8},{1,9},{2,10},{3,11},{4,12},{5,13},{6,14},{7,15},{8,0},{9,1},... | collective-permute-start | bytes 983048 | tf_op jit(solution)/shard_map/ppermute | solution.py:36
  142.1 14.9 %collective-permute-start.49 = (bf16[4,128,1024]{2,1,0:T(8,128)(2,1)S(1)}, bf16[4,128,1024]{2,1,0:T(8,128)(2,1)S(1)}, u32[]{:S(2)}, u32[]{:S(2)}) collective-permute-start(bf16[4,128,1024]{2,1,0:T(8,128)(2,1)S(1)} %shard_map.174.refs_9_.refs_4_), channel_id=1, source_target_pairs={{0,32},{1,33},{2,34},{3,35},{4,36},{5,37},{6,38},{7,39},{8,12},{9,... | collective-permute-start | bytes 3145736 | tf_op jit(solution)/shard_map/ppermute | solution.py:126
  142.3 16.0 %collective-permute-start.50 = (bf16[4,128,1024]{2,1,0:T(8,128)(2,1)S(1)}, bf16[4,128,1024]{2,1,0:T(8,128)(2,1)S(1)}, u32[]{:S(2)}, u32[]{:S(2)}) collective-permute-start(bf16[4,128,1024]{2,1,0:T(8,128)(2,1)S(1)} %shard_map.174.refs_9_.refs_4_), channel_id=1, source_target_pairs={{0,96},{1,97},{2,98},{3,99},{4,100},{5,101},{6,102},{7,103},{8,28}... | collective-permute-start | bytes 3145736 | tf_op jit(solution)/shard_map/ppermute | solution.py:126
  154.1 11.0 %collective-permute-start.53 = (bf16[160,1024]{1,0:T(8,128)(2,1)S(1)}, bf16[160,1024]{1,0:T(8,128)(2,1)S(1)}, u32[]{:S(2)}, u32[]{:S(2)}) collective-permute-start(bf16[160,1024]{1,0:T(8,128)(2,1)S(1)} %get-tuple-element.169.refs_2_.refs_1_.refs_5_), channel_id=1, source_target_pairs={{0,3},{1,2},{2,1},{3,0},{4,7},{5,6},{6,5},{7,4},{8,11},{9,10},{10,... | collective-permute-start | bytes 983048 | tf_op jit(solution)/shard_map/ppermute | solution.py:36
  158.4 10.5 %collective-permute-start.51 = (bf16[2,128,1024]{2,1,0:T(8,128)(2,1)S(1)}, bf16[2,128,1024]{2,1,0:T(8,128)(2,1)S(1)}, u32[]{:S(2)}, u32[]{:S(2)}) collective-permute-start(bf16[2,128,1024]{2,1,0:T(8,128)(2,1)S(1)} %get-tuple-element.170), channel_id=1, source_target_pairs={{0,96},{1,97},{2,98},{3,99},{4,100},{5,101},{6,102},{7,103},{8,28}... | collective-permute-start | bytes 1572872 | tf_op jit(solution)/shard_map/ppermute | solution.py:126
  165.0 11.5 %collective-permute-start.48 = (bf16[160,1024]{1,0:T(8,128)(2,1)S(1)}, bf16[160,1024]{1,0:T(8,128)(2,1)S(1)}, u32[]{:S(2)}, u32[]{:S(2)}) collective-permute-start(bf16[160,1024]{1,0:T(8,128)(2,1)S(1)} %get-tuple-element.169.refs_2_.refs_1_.refs_5_), channel_id=1, source_target_pairs={{0,8},{1,9},{2,10},{3,11},{4,12},{5,13},{6,14},{7,15},{8,0},{9,1},... | collective-permute-start | bytes 983048 | tf_op jit(solution)/shard_map/ppermute | solution.py:36
  183.4 9.6 %collective-permute-start.55 = (bf16[160,1024]{1,0:T(8,128)(2,1)S(1)}, bf16[160,1024]{1,0:T(8,128)(2,1)S(1)}, u32[]{:S(2)}, u32[]{:S(2)}) collective-permute-start(bf16[160,1024]{1,0:T(8,128)(2,1)S(1)} %get-tuple-element.179), channel_id=1, source_target_pairs={{0,8},{1,9},{2,10},{3,11},{4,12},{5,13},{6,14},{7,15},{8,0},{9,1},... | collective-permute-start | bytes 983048 | tf_op jit(solution)/shard_map/ppermute | solution.py:36
  184.0 11.4 %collective-permute-start.57 = (bf16[160,1024]{1,0:T(8,128)(2,1)S(1)}, bf16[160,1024]{1,0:T(8,128)(2,1)S(1)}, u32[]{:S(2)}, u32[]{:S(2)}) collective-permute-start(bf16[160,1024]{1,0:T(8,128)(2,1)S(1)} %shard_map.182.refs_13_), channel_id=1, source_target_pairs={{0,3},{1,2},{2,1},{3,0},{4,7},{5,6},{6,5},{7,4},{8,11},{9,10},{10,... | collective-permute-start | bytes 983048 | tf_op jit(solution)/shard_map/ppermute | solution.py:36
  197.2 9.8 %collective-permute-start.64 = (bf16[2,128,1024]{2,1,0:T(8,128)(2,1)S(1)}, bf16[2,128,1024]{2,1,0:T(8,128)(2,1)S(1)}, u32[]{:S(2)}, u32[]{:S(2)}) collective-permute-start(bf16[2,128,1024]{2,1,0:T(8,128)(2,1)S(1)} %get-tuple-element.197), channel_id=1, source_target_pairs={{0,32},{1,33},{2,34},{3,35},{4,36},{5,37},{6,38},{7,39},{8,12},{9,... | collective-permute-start | bytes 1572872 | tf_op jit(solution)/shard_map/ppermute | solution.py:126
  197.4 10.4 %collective-permute-start.65 = (bf16[2,128,1024]{2,1,0:T(8,128)(2,1)S(1)}, bf16[2,128,1024]{2,1,0:T(8,128)(2,1)S(1)}, u32[]{:S(2)}, u32[]{:S(2)}) collective-permute-start(bf16[2,128,1024]{2,1,0:T(8,128)(2,1)S(1)} %get-tuple-element.198), channel_id=1, source_target_pairs={{0,96},{1,97},{2,98},{3,99},{4,100},{5,101},{6,102},{7,103},{8,28}... | collective-permute-start | bytes 1572872 | tf_op jit(solution)/shard_map/ppermute | solution.py:126
  208.6 29.9 %collective-permute-start.74 = (bf16[4,128,1024]{2,1,0:T(8,128)(2,1)S(1)}, bf16[4,128,1024]{2,1,0:T(8,128)(2,1)S(1)}, u32[]{:S(2)}, u32[]{:S(2)}) collective-permute-start(bf16[4,128,1024]{2,1,0:T(8,128)(2,1)S(1)} %get-tuple-element.199.refs_5_), channel_id=1, source_target_pairs={{0,32},{1,33},{2,34},{3,35},{4,36},{5,37},{6,38},{7,39},{8,12},{9,... | collective-permute-start | bytes 3145736 | tf_op jit(solution)/shard_map/ppermute | solution.py:126
  211.7 10.9 %collective-permute-start.68 = (bf16[160,1024]{1,0:T(8,128)(2,1)S(1)}, bf16[160,1024]{1,0:T(8,128)(2,1)S(1)}, u32[]{:S(2)}, u32[]{:S(2)}) collective-permute-start(bf16[160,1024]{1,0:T(8,128)(2,1)S(1)} %get-tuple-element.201.refs_1_.refs_7_), channel_id=1, source_target_pairs={{0,3},{1,2},{2,1},{3,0},{4,7},{5,6},{6,5},{7,4},{8,11},{9,10},{10,... | collective-permute-start | bytes 983048 | tf_op jit(solution)/shard_map/ppermute | solution.py:36
  214.3 24.6 %collective-permute-start.75 = (bf16[4,128,1024]{2,1,0:T(8,128)(2,1)S(1)}, bf16[4,128,1024]{2,1,0:T(8,128)(2,1)S(1)}, u32[]{:S(2)}, u32[]{:S(2)}) collective-permute-start(bf16[4,128,1024]{2,1,0:T(8,128)(2,1)S(1)} %get-tuple-element.220), channel_id=1, source_target_pairs={{0,96},{1,97},{2,98},{3,99},{4,100},{5,101},{6,102},{7,103},{8,28}... | collective-permute-start | bytes 3145736 | tf_op jit(solution)/shard_map/ppermute | solution.py:126
  220.6 15.5 %collective-permute-start.73 = (bf16[2,128,1024]{2,1,0:T(8,128)(2,1)S(1)}, bf16[2,128,1024]{2,1,0:T(8,128)(2,1)S(1)}, u32[]{:S(2)}, u32[]{:S(2)}) collective-permute-start(bf16[2,128,1024]{2,1,0:T(8,128)(2,1)S(1)} %get-tuple-element.217), channel_id=1, source_target_pairs={{0,96},{1,97},{2,98},{3,99},{4,100},{5,101},{6,102},{7,103},{8,28}... | collective-permute-start | bytes 1572872 | tf_op jit(solution)/shard_map/ppermute | solution.py:126
  229.7 17.5 %collective-permute-start.67 = (bf16[160,1024]{1,0:T(8,128)(2,1)S(1)}, bf16[160,1024]{1,0:T(8,128)(2,1)S(1)}, u32[]{:S(2)}, u32[]{:S(2)}) collective-permute-start(bf16[160,1024]{1,0:T(8,128)(2,1)S(1)} %get-tuple-element.204.refs_9_), channel_id=1, source_target_pairs={{0,8},{1,9},{2,10},{3,11},{4,12},{5,13},{6,14},{7,15},{8,0},{9,1},... | collective-permute-start | bytes 983048 | tf_op jit(solution)/shard_map/ppermute | solution.py:36
  236.4 20.6 %collective-permute-start.78 = (bf16[4,128,1024]{2,1,0:T(8,128)(2,1)S(1)}, bf16[4,128,1024]{2,1,0:T(8,128)(2,1)S(1)}, u32[]{:S(2)}, u32[]{:S(2)}) collective-permute-start(bf16[4,128,1024]{2,1,0:T(8,128)(2,1)S(1)} %get-tuple-element.218.refs_14_), channel_id=1, source_target_pairs={{0,32},{1,33},{2,34},{3,35},{4,36},{5,37},{6,38},{7,39},{8,12},{9,... | collective-permute-start | bytes 3145736 | tf_op jit(solution)/shard_map/ppermute | solution.py:126
  236.5 21.7 %collective-permute-start.79 = (bf16[4,128,1024]{2,1,0:T(8,128)(2,1)S(1)}, bf16[4,128,1024]{2,1,0:T(8,128)(2,1)S(1)}, u32[]{:S(2)}, u32[]{:S(2)}) collective-permute-start(bf16[4,128,1024]{2,1,0:T(8,128)(2,1)S(1)} %get-tuple-element.229), channel_id=1, source_target_pairs={{0,96},{1,97},{2,98},{3,99},{4,100},{5,101},{6,102},{7,103},{8,28}... | collective-permute-start | bytes 3145736 | tf_op jit(solution)/shard_map/ppermute | solution.py:126
  239.2 16.4 %collective-permute-start.77 = (bf16[2,128,1024]{2,1,0:T(8,128)(2,1)S(1)}, bf16[2,128,1024]{2,1,0:T(8,128)(2,1)S(1)}, u32[]{:S(2)}, u32[]{:S(2)}) collective-permute-start(bf16[2,128,1024]{2,1,0:T(8,128)(2,1)S(1)} %get-tuple-element.226), channel_id=1, source_target_pairs={{0,20},{1,21},{2,22},{3,23},{4,16},{5,17},{6,18},{7,19},{8,104},{9... | collective-permute-start | bytes 1572872 | tf_op jit(solution)/shard_map/ppermute | solution.py:126
  249.3 11.1 %collective-permute-start.76 = (bf16[160,1024]{1,0:T(8,128)(2,1)S(1)}, bf16[160,1024]{1,0:T(8,128)(2,1)S(1)}, u32[]{:S(2)}, u32[]{:S(2)}) collective-permute-start(bf16[160,1024]{1,0:T(8,128)(2,1)S(1)} %get-tuple-element.223.refs_1_.refs_3_), channel_id=1, source_target_pairs={{0,8},{1,9},{2,10},{3,11},{4,12},{5,13},{6,14},{7,15},{8,0},{9,1},... | collective-permute-start | bytes 983048 | tf_op jit(solution)/shard_map/ppermute | solution.py:36
  249.7 18.0 %collective-permute-start.58 = (bf16[160,1024]{1,0:T(8,128)(2,1)S(1)}, bf16[160,1024]{1,0:T(8,128)(2,1)S(1)}, u32[]{:S(2)}, u32[]{:S(2)}) collective-permute-start(bf16[160,1024]{1,0:T(8,128)(2,1)S(1)} %shard_map.185), channel_id=1, source_target_pairs={{0,8},{1,9},{2,10},{3,11},{4,12},{5,13},{6,14},{7,15},{8,0},{9,1},... | collective-permute-start | bytes 983048 | tf_op jit(solution)/shard_map/ppermute | solution.py:36
  255.6 12.7 %collective-permute-start.60 = (bf16[160,1024]{1,0:T(8,128)(2,1)S(1)}, bf16[160,1024]{1,0:T(8,128)(2,1)S(1)}, u32[]{:S(2)}, u32[]{:S(2)}) collective-permute-start(bf16[160,1024]{1,0:T(8,128)(2,1)S(1)} %shard_map.187), channel_id=1, source_target_pairs={{0,3},{1,2},{2,1},{3,0},{4,7},{5,6},{6,5},{7,4},{8,11},{9,10},{10,... | collective-permute-start | bytes 983048 | tf_op jit(solution)/shard_map/ppermute | solution.py:36
  256.9 15.3 %collective-permute-start.86 = (bf16[2,128,1024]{2,1,0:T(8,128)(2,1)S(1)}, bf16[2,128,1024]{2,1,0:T(8,128)(2,1)S(1)}, u32[]{:S(2)}, u32[]{:S(2)}) collective-permute-start(bf16[2,128,1024]{2,1,0:T(8,128)(2,1)S(1)} %get-tuple-element.246), channel_id=1, source_target_pairs={{0,32},{1,33},{2,34},{3,35},{4,36},{5,37},{6,38},{7,39},{8,12},{9,... | collective-permute-start | bytes 1572872 | tf_op jit(solution)/shard_map/ppermute | solution.py:126
  258.2 14.1 %collective-permute-start.87 = (bf16[2,128,1024]{2,1,0:T(8,128)(2,1)S(1)}, bf16[2,128,1024]{2,1,0:T(8,128)(2,1)S(1)}, u32[]{:S(2)}, u32[]{:S(2)}) collective-permute-start(bf16[2,128,1024]{2,1,0:T(8,128)(2,1)S(1)} %get-tuple-element.247), channel_id=1, source_target_pairs={{0,96},{1,97},{2,98},{3,99},{4,100},{5,101},{6,102},{7,103},{8,28}... | collective-permute-start | bytes 1572872 | tf_op jit(solution)/shard_map/ppermute | solution.py:126
  270.6 15.6 %collective-permute-start.85 = (bf16[2,128,1024]{2,1,0:T(8,128)(2,1)S(1)}, bf16[2,128,1024]{2,1,0:T(8,128)(2,1)S(1)}, u32[]{:S(2)}, u32[]{:S(2)}) collective-permute-start(bf16[2,128,1024]{2,1,0:T(8,128)(2,1)S(1)} %get-tuple-element.242), channel_id=1, source_target_pairs={{0,20},{1,21},{2,22},{3,23},{4,16},{5,17},{6,18},{7,19},{8,104},{9... | collective-permute-start | bytes 1572872 | tf_op jit(solution)/shard_map/ppermute | solution.py:126
  272.6 14.9 %collective-permute-start.88 = (bf16[4,128,1024]{2,1,0:T(8,128)(2,1)S(1)}, bf16[4,128,1024]{2,1,0:T(8,128)(2,1)S(1)}, u32[]{:S(2)}, u32[]{:S(2)}) collective-permute-start(bf16[4,128,1024]{2,1,0:T(8,128)(2,1)S(1)} %get-tuple-element.248), channel_id=1, source_target_pairs={{0,32},{1,33},{2,34},{3,35},{4,36},{5,37},{6,38},{7,39},{8,12},{9,... | collective-permute-start | bytes 3145736 | tf_op jit(solution)/shard_map/ppermute | solution.py:126
  273.3 18.1 %collective-permute-start.89 = (bf16[4,128,1024]{2,1,0:T(8,128)(2,1)S(1)}, bf16[4,128,1024]{2,1,0:T(8,128)(2,1)S(1)}, u32[]{:S(2)}, u32[]{:S(2)}) collective-permute-start(bf16[4,128,1024]{2,1,0:T(8,128)(2,1)S(1)} %get-tuple-element.249), channel_id=1, source_target_pairs={{0,96},{1,97},{2,98},{3,99},{4,100},{5,101},{6,102},{7,103},{8,28}... | collective-permute-start | bytes 3145736 | tf_op jit(solution)/shard_map/ppermute | solution.py:126
  278.9 14.2 %collective-permute-start.83 = (bf16[2,128,1024]{2,1,0:T(8,128)(2,1)S(1)}, bf16[2,128,1024]{2,1,0:T(8,128)(2,1)S(1)}, u32[]{:S(2)}, u32[]{:S(2)}) collective-permute-start(bf16[2,128,1024]{2,1,0:T(8,128)(2,1)S(1)} %get-tuple-element.240), channel_id=1, source_target_pairs={{0,32},{1,33},{2,34},{3,35},{4,36},{5,37},{6,38},{7,39},{8,12},{9,... | collective-permute-start | bytes 1572872 | tf_op jit(solution)/shard_map/ppermute | solution.py:126
  280.0 17.0 %collective-permute-start.84 = (bf16[2,128,1024]{2,1,0:T(8,128)(2,1)S(1)}, bf16[2,128,1024]{2,1,0:T(8,128)(2,1)S(1)}, u32[]{:S(2)}, u32[]{:S(2)}) collective-permute-start(bf16[2,128,1024]{2,1,0:T(8,128)(2,1)S(1)} %get-tuple-element.241), channel_id=1, source_target_pairs={{0,96},{1,97},{2,98},{3,99},{4,100},{5,101},{6,102},{7,103},{8,28}... | collective-permute-start | bytes 1572872 | tf_op jit(solution)/shard_map/ppermute | solution.py:126
  297.3 24.2 %collective-permute-start.90 = (bf16[4,128,1024]{2,1,0:T(8,128)(2,1)S(1)}, bf16[4,128,1024]{2,1,0:T(8,128)(2,1)S(1)}, u32[]{:S(2)}, u32[]{:S(2)}) collective-permute-start(bf16[4,128,1024]{2,1,0:T(8,128)(2,1)S(1)} %get-tuple-element.251.refs_1_), channel_id=1, source_target_pairs={{0,32},{1,33},{2,34},{3,35},{4,36},{5,37},{6,38},{7,39},{8,12},{9,... | collective-permute-start | bytes 3145736 | tf_op jit(solution)/shard_map/ppermute | solution.py:126
  297.9 23.6 %collective-permute-start.91 = (bf16[4,128,1024]{2,1,0:T(8,128)(2,1)S(1)}, bf16[4,128,1024]{2,1,0:T(8,128)(2,1)S(1)}, u32[]{:S(2)}, u32[]{:S(2)}) collective-permute-start(bf16[4,128,1024]{2,1,0:T(8,128)(2,1)S(1)} %get-tuple-element.252), channel_id=1, source_target_pairs={{0,96},{1,97},{2,98},{3,99},{4,100},{5,101},{6,102},{7,103},{8,28}... | collective-permute-start | bytes 3145736 | tf_op jit(solution)/shard_map/ppermute | solution.py:126
  299.3 15.6 %collective-permute-start.61 = (f32[160,1024]{1,0:T(8,128)S(1)}, f32[160,1024]{1,0:T(8,128)S(1)}, u32[]{:S(2)}, u32[]{:S(2)}) collective-permute-start(f32[160,1024]{1,0:T(8,128)S(1)} %copy-done.3), channel_id=1, source_target_pairs={{1,8},{3,10},{5,12},{7,14},{8,1},{10,3},{12,5},{14,7},{17,24},{19,... | collective-permute-start | bytes 1966088 | tf_op jit(solution)/shard_map/ppermute | solution.py:40
  300.0 15.4 %collective-permute-start.82 = (f32[160,1024]{1,0:T(8,128)S(1)}, f32[160,1024]{1,0:T(8,128)S(1)}, u32[]{:S(2)}, u32[]{:S(2)}) collective-permute-start(f32[160,1024]{1,0:T(8,128)S(1)} %get-tuple-element.237.refs_1_.refs_6_), channel_id=1, source_target_pairs={{1,8},{3,10},{5,12},{7,14},{8,1},{10,3},{12,5},{14,7},{17,24},{19,... | collective-permute-start | bytes 1966088 | tf_op jit(solution)/shard_map/ppermute | solution.py:40
  313.1 11.1 %collective-permute-start.98 = (bf16[2,128,1024]{2,1,0:T(8,128)(2,1)S(1)}, bf16[2,128,1024]{2,1,0:T(8,128)(2,1)S(1)}, u32[]{:S(2)}, u32[]{:S(2)}) collective-permute-start(bf16[2,128,1024]{2,1,0:T(8,128)(2,1)S(1)} %get-tuple-element.266), channel_id=1, source_target_pairs={{0,20},{1,21},{2,22},{3,23},{4,16},{5,17},{6,18},{7,19},{8,104},{9... | collective-permute-start | bytes 1572872 | tf_op jit(solution)/shard_map/ppermute | solution.py:126
  325.4 12.2 %collective-permute-start.96 = (bf16[128,1024]{1,0:T(8,128)(2,1)S(1)}, bf16[128,1024]{1,0:T(8,128)(2,1)S(1)}, u32[]{:S(2)}, u32[]{:S(2)}) collective-permute-start(bf16[128,1024]{1,0:T(8,128)(2,1)S(1)} %get-tuple-element.264), channel_id=1, source_target_pairs={{0,16},{1,17},{2,18},{3,19},{4,20},{5,21},{6,22},{7,23},{8,72},{9,... | collective-permute-start | bytes 786440 | tf_op jit(solution)/shard_map/ppermute | solution.py:126
  327.7 10.4 %collective-permute-start.97 = (bf16[128,1024]{1,0:T(8,128)(2,1)S(1)}, bf16[128,1024]{1,0:T(8,128)(2,1)S(1)}, u32[]{:S(2)}, u32[]{:S(2)}) collective-permute-start(bf16[128,1024]{1,0:T(8,128)(2,1)S(1)} %get-tuple-element.265), channel_id=1, source_target_pairs={{0,20},{1,21},{2,22},{3,23},{4,16},{5,17},{6,18},{7,19},{8,104},{9... | collective-permute-start | bytes 786440 | tf_op jit(solution)/shard_map/ppermute | solution.py:126
  341.5 16.7 %collective-permute-start.103 = (bf16[128,3072]{1,0:T(8,128)(2,1)S(1)}, bf16[128,3072]{1,0:T(8,128)(2,1)S(1)}, u32[]{:S(2)}, u32[]{:S(2)}) collective-permute-start(bf16[128,3072]{1,0:T(8,128)(2,1)S(1)} %get-tuple-element.270.refs_1_), channel_id=1, source_target_pairs={{1,0},{3,2},{5,4},{7,6},{8,9},{10,11},{12,13},{14,15},{17,16},{19,... | collective-permute-start | bytes 2359304 | tf_op jit(solution)/shard_map/ppermute | solution.py:40
  342.8 12.6 %collective-permute-start.104 = (bf16[128,1024]{1,0:T(8,128)(2,1)S(1)}, bf16[128,1024]{1,0:T(8,128)(2,1)S(1)}, u32[]{:S(2)}, u32[]{:S(2)}) collective-permute-start(bf16[128,1024]{1,0:T(8,128)(2,1)S(1)} %get-tuple-element.271), channel_id=1, source_target_pairs={{0,2},{2,0},{4,6},{6,4},{9,11},{11,9},{13,15},{15,13},{16,18},{18,... | collective-permute-start | bytes 786440 | tf_op jit(solution)/shard_map/ppermute | solution.py:40
  347.4 10.1 %collective-permute-start.105 = (bf16[128,1024]{1,0:T(8,128)(2,1)S(1)}, bf16[128,1024]{1,0:T(8,128)(2,1)S(1)}, u32[]{:S(2)}, u32[]{:S(2)}) collective-permute-start(bf16[128,1024]{1,0:T(8,128)(2,1)S(1)} %get-tuple-element.271), channel_id=1, source_target_pairs={{1,2},{3,0},{5,6},{7,4},{8,11},{10,9},{12,15},{14,13},{17,18},{19,... | collective-permute-start | bytes 786440 | tf_op jit(solution)/shard_map/ppermute | solution.py:40
  (53 other events, 309.9 us)

commit v2 on v1

--- a/solution.py
+++ b/solution.py
@@ -781,10 +781,9 @@
     out[...] = (mine[...] + theirs[...].astype(F32)).astype(BF)
 
 
-def folded(mine, theirs):
-    return call(
-        fold_kernel, [shape(mine.shape, BF)], [VMEM] * 2, [mine, swapped(theirs, CORE)]
-    )[0]
+def folded(mine, theirs, deps=()):
+    moved = swapped(theirs, CORE)
+    return call(fold_kernel, [shape(mine.shape, BF)], [VMEM] * 2, [mine, moved], deps=deps)[0]
 
 
 def from_far(mine, theirs):
@@ -971,7 +970,7 @@
             g_rows = gathered_rows(g)
         near = feed_back(feed_w, scal, *g_rows[:2], slope[0])
         far = far_back if last else feed_back(feed_w, scal, *g_rows[2:], slope[1], near[1:2])
-        fold = folded(far[0], far[1])
+        fold = folded(far[0], far[1], () if last else feed_sums[index + 1].b())
         *pieces, up_sum = weight_grads(
             feed_w,
             scal,
@@ -980,12 +979,10 @@
             [active, (near[2], far[2])],
             [0],
             [1],
-            [fold] if last else [fold, *attn_sums[index + 1].a()],
+            [fold] if last else [fold, *attn_sums[index + 1].a([fold])],
         )
         feed_sums[index] = Reduction(pieces)
         deps = pieces[:1]
-        if not last:
-            deps = [*deps, *feed_sums[index + 1].b()]
         grad_mid, d, sums_two = norm_back(
             grad,
             middle,
@@ -995,7 +992,7 @@
             deps,
         )
         d_other = swapped(d, CORE)
-        deps = () if last else [*feed_sums[index + 1].c(), *attn_sums[index + 1].b()]
+        deps = () if last else [*attn_sums[index + 1].b(), last_fold]
         mine, theirs, triple = attention_back(attn_w, scal, d, d_other, qkv, probs, deps)
         moved = swapped(theirs, CORE)
         passed = feed_sums[index].a([moved])
@@ -1014,16 +1011,17 @@
             [(triple,), (mixed,)],
             [1],
             [0],
-            [g] if last else [outcome, *feed_sums[index + 1].d()],
+            [g] if last else feed_sums[index + 1].c(),
         )
         attn_sums[index] = Reduction(pieces)
         if last:
+            last_fold = folded(last_far[0], tied(last_far[1], [d]))
             outcome = joined(
                 middle,
                 [
                     last_near[0],
                     swapped(tied(last_near[1], [d]), CORE),
-                    from_far(last_far[0], tied(last_far[1], [d])),
+                    swapped(last_fold, Z_MASK),
                 ],
                 small,
                 [index * ROWS + 5, index * ROWS, index * ROWS + 2],
@@ -1037,16 +1035,17 @@
     small = summed_over(packed(scal, small_parts), [CORE])
 
     final, above = attn_sums
-    final.a([*above.c(), *feed_sums[0].b(), grad])
-    small = summed_over(tied(small, final.passed[:1]), [Z_MASK, ZL])
-    final.b([input_grad, activations, small], True)
+    final.a([*above.c(), *feed_sums[0].b(), grad, outcome])
+    final.b([activations, input_grad, small], True)
     feed_sums[0].c(final.parts[:1])
     moved = final.spread()
-    steps, small = reduced_small(tied(small, moved[:1]), lane, own_wide)
-    final.direct(moved, [*feed_sums[0].d(), *above.d(), steps[0]])
+    small = summed_over(tied(small, moved[:1]), [Z_MASK, ZL])
+    final.direct(moved, [*feed_sums[0].d(), *above.d(), *feed_sums[1].d()])
+    steps, small_sums = reduced_small(small, lane, own_wide)
     ends = reduced_end(
-        [a.total for a in attn_sums], [a.total for a in feed_sums], scal, steps[1:2], steps[2:3]
-    )
+        [a.total for a in attn_sums], [a.total for a in feed_sums], scal, [small], steps[2:3]
+    )
+    small = small_sums
     small = small.reshape(layers, ROWS, -1)
     qkv, out, up, down = call(
         result_kernel,

time: 375 us -> 376 us (level)
  the two profiles are of different devices: /device:TPU:0 before, /device:TPU:2 now
where the time goes in v2:
time: 376 us; the launch traced here: 369 us
  starting transfers between devices  138 us (37%)
  waiting for transfers between devices  119 us (32%)
  Pallas kernels  105 us (28%)
  local copies, waits for them, and re-layouts  4.2 us (1%)
    pallas_call x70, Pallas kernels, call(): pl.pallas_call(kernel, grid=(1,) if windowed else (), out_shape=tuple(out...  105 us
    ppermute x49, waiting for transfers between devices, along(): return lax.ppermute(array, PLACES, pairs)  66.2 us
    ppermute x49, starting transfers between devices, along(): return lax.ppermute(array, PLACES, pairs)  61 us
    ppermute x48, starting transfers between devices, swapped(): return lax.ppermute(array, PLACES, [(i, i ^ mask) for i in range(DEVICES)])  55 us
    ppermute x48, waiting for transfers between devices, swapped(): return lax.ppermute(array, PLACES, [(i, i ^ mask) for i in range(DEVICES)])  48.8 us
    ppermute x12, starting transfers between devices, sent_by(): lax.ppermute(array, PLACES, [(i, i ^ mask) for i in range(DEVICES) if sen...  21.6 us
  transfers between devices with their start and end apart: 109, of which 49 were waited for; matrix products, arithmetic and copies ran while one was open for 1% of the time, Pallas kernels for 27%

profile of v2, /device:TPU:2, one launch (start us, length us, event | category | flops | bytes accessed | tf_op | source)
XLA Modules:
  0.0 368.5 jit_solution(5174560331793533459)
XLA Ops:
  7.1 3.2 collective-permute-start.3
  11.0 3.8 %collective-permute-start.11 = (bf16[128,1536]{1,0:T(8,128)(2,1)S(1)}, bf16[128,1536]{1,0:T(8,128)(2,1)S(1)}, u32[]{:S(2)}, u32[]{:S(2)}) collective-permute-start(bf16[128,1536]{1,0:T(8,128)(2,1)S(1)} %pad_maximum_fusion), channel_id=1, source_target_pairs={{0,1},{2,3},{4,5},{6,7},{9,8},{11,10},{13,12},{15,14},{16,17},{18,... | collective-permute-start | bytes 1179656 | tf_op jit(solution)/shard_map/ppermute | solution.py:40
  14.9 5.5 %collective-permute-start.12 = (bf16[128,1024]{1,0:T(8,128)(2,1)S(1)}, bf16[128,1024]{1,0:T(8,128)(2,1)S(1)}, u32[]{:S(2)}, u32[]{:S(2)}) collective-permute-start(bf16[128,1024]{1,0:T(8,128)(2,1)S(1)} %get-tuple-element.297), channel_id=1, source_target_pairs={{0,2},{2,0},{4,6},{6,4},{9,11},{11,9},{13,15},{15,13},{16,18},{18,... | collective-permute-start | bytes 786440 | tf_op jit(solution)/shard_map/ppermute | solution.py:40
  22.3 3.3 collective-permute-done.4
  30.3 6.7 %collective-permute-done.14.refs_0_.refs_1_ = bf16[128,2048]{1,0:T(8,128)(2,1)S(1)} collective-permute-done((bf16[128,2048]{1,0:T(8,128)(2,1)S(1)}, bf16[128,2048]{1,0:T(8,128)(2,1)S(1)}, u32[]{:S(2)}, u32[]{:S(2)}) %collective-permute-start.14) | collective-permute-done | bytes 524320 | tf_op jit(solution)/shard_map/ppermute | solution.py:126
  40.8 6.1 %collective-permute-done.16.refs_2_ = bf16[128,1024]{1,0:T(8,128)(2,1)S(1)} collective-permute-done((bf16[128,1024]{1,0:T(8,128)(2,1)S(1)}, bf16[128,1024]{1,0:T(8,128)(2,1)S(1)}, u32[]{:S(2)}, u32[]{:S(2)}) %collective-permute-start.16) | collective-permute-done | bytes 262176 | tf_op jit(solution)/shard_map/ppermute | solution.py:126
  52.0 3.3 collective-permute-start.7
  55.3 3.4 collective-permute-done.7
  64.6 2.6 collective-permute-start.20
  67.3 2.1 collective-permute-start.23
  72.7 3.5 collective-permute-done.19.refs_4_.refs_6_.refs_7_
  77.3 3.0 collective-permute-start.28
  81.3 6.1 %shard_map.164 = (f32[160,1024]{1,0:T(8,128)S(1)}, bf16[160,1024]{1,0:T(8,128)(2,1)S(1)}, bf16[320,1536]{1,0:T(8,128)(2,1)}, bf16[8,320,320]{2,1,0:T(8,128)(2,1)}, bf16[320,512]{1,0:T(8,128)(2,1)}) custom-call(s32[7]{0:T(128)S(1)} %stack.32.refs_0_, bf16[160,1024]{1,0:T(8,128)(2,1)S(1)} %get-tuple-element.144.refs_6_.refs_1_, ...), custom_call_target="tpu_custom_call" | custom-call | flops 6899999744 | bytes 1 | tf_op jit(solution)/shard_map/pallas_call | solution.py:79
  89.1 2.0 shard_map.166
  91.1 5.6 %collective-permute-start.32 = (bf16[160,1024]{1,0:T(8,128)(2,1)S(1)}, bf16[160,1024]{1,0:T(8,128)(2,1)S(1)}, u32[]{:S(2)}, u32[]{:S(2)}) collective-permute-start(bf16[160,1024]{1,0:T(8,128)(2,1)S(1)} %get-tuple-element.155.refs_2_.refs_1_.refs_5_), channel_id=1, source_target_pairs={{0,3},{1,2},{2,1},{3,0},{4,7},{5,6},{6,5},{7,4},{8,11},{9,10},{10,... | collective-permute-start | bytes 983048 | tf_op jit(solution)/shard_map/ppermute | solution.py:36
  97.7 2.1 collective-permute-start.31
  99.8 5.0 %collective-permute-done.32.refs_1_.refs_7_ = bf16[160,1024]{1,0:T(8,128)(2,1)S(1)} collective-permute-done((bf16[160,1024]{1,0:T(8,128)(2,1)S(1)}, bf16[160,1024]{1,0:T(8,128)(2,1)S(1)}, u32[]{:S(2)}, u32[]{:S(2)}) %collective-permute-start.32) | collective-permute-done | bytes 327712 | tf_op jit(solution)/shard_map/ppermute | solution.py:36
  104.9 7.4 %collective-permute-done.34.refs_9_.refs_2_ = bf16[128,1024]{1,0:T(8,128)(2,1)S(1)} collective-permute-done((bf16[128,1024]{1,0:T(8,128)(2,1)S(1)}, bf16[128,1024]{1,0:T(8,128)(2,1)S(1)}, u32[]{:S(2)}, u32[]{:S(2)}) %collective-permute-start.34) | collective-permute-done | bytes 262176 | tf_op jit(solution)/shard_map/ppermute | solution.py:126
  114.0 3.7 shard_map.168
  118.3 3.5 shard_map.169
  122.2 3.0 collective-permute-start.38
  125.2 2.1 collective-permute-done.40.refs_0_.refs_5_.refs_6_
  129.0 3.1 collective-permute-start.43
  132.1 3.0 collective-permute-start.46
  135.0 2.1 shard_map.171
  137.7 2.9 collective-permute-done.46.refs_6_.refs_1_.refs_3_
  143.9 6.1 %shard_map.175 = (f32[160,1024]{1,0:T(8,128)S(1)}, bf16[160,1024]{1,0:T(8,128)(2,1)S(1)}, bf16[320,1536]{1,0:T(8,128)(2,1)}, bf16[8,320,320]{2,1,0:T(8,128)(2,1)}, bf16[320,512]{1,0:T(8,128)(2,1)}) custom-call(s32[7]{0:T(128)S(1)} %stack.32.refs_0_, bf16[160,1024]{1,0:T(8,128)(2,1)S(1)} %get-tuple-element.163.refs_6_.refs_1_, ...), custom_call_target="tpu_custom_call" | custom-call | flops 6899999744 | bytes 1 | tf_op jit(solution)/shard_map/pallas_call | solution.py:79
  151.7 2.1 shard_map.176
  153.8 3.0 collective-permute-start.53
  160.8 3.9 %collective-permute-done.53.refs_1_.refs_7_ = bf16[160,1024]{1,0:T(8,128)(2,1)S(1)} collective-permute-done((bf16[160,1024]{1,0:T(8,128)(2,1)S(1)}, bf16[160,1024]{1,0:T(8,128)(2,1)S(1)}, u32[]{:S(2)}, u32[]{:S(2)}) %collective-permute-start.53) | collective-permute-done | bytes 327712 | tf_op jit(solution)/shard_map/ppermute | solution.py:36
  168.1 3.6 shard_map.178
  171.7 3.3 shard_map.179
  175.1 3.6 shard_map.180
  178.7 3.3 shard_map.181
  182.6 3.5 collective-permute-start.57
  186.0 5.5 %shard_map.183 = (bf16[4,128,1024]{2,1,0:T(8,128)(2,1)S(1)}, bf16[4,128,1024]{2,1,0:T(8,128)(2,1)S(1)}, bf16[2,128,1024]{2,1,0:T(8,128)(2,1)S(1)}, bf16[2,128,10...) custom-call(s32[7]{0:T(128)S(1)} %stack.32.refs_0_, ...), custom_call_target="tpu_custom_call" | custom-call | flops 5750000128 | bytes 1 | tf_op jit(solution)/shard_map/pallas_call | solution.py:79
  191.5 2.4 collective-permute-done.57.refs_5_
  198.5 7.2 %shard_map.190 = (f32[160,1024]{1,0:T(8,128)S(1)}, bf16[160,1024]{1,0:T(8,128)(2,1)S(1)}, bf16[320,1536]{1,0:T(8,128)(2,1)S(1)}) custom-call(s32[7]{0:T(128)S(1)} %stack.32.refs_0_, bf16[160,1024]{1,0:T(8,128)(2,1)S(1)} %get-tuple-element.186.refs_1_.refs_3_, bf16[160,1024]{1,0:T(8,128)(2,1)S(1)} %collective-permute-done.62.refs_2_.refs_4_, ...), custom_call_target="tpu_custom_call" | custom-call | flops 8049999872 | bytes 1 | tf_op jit(solution)/shard_map/pallas_call | solution.py:79
  210.9 2.6 collective-permute-start.68
  214.8 4.1 %shard_map.197 = (bf16[4,128,1024]{2,1,0:T(8,128)(2,1)S(1)}, bf16[4,128,1024]{2,1,0:T(8,128)(2,1)S(1)}, bf16[2,128,1024]{2,1,0:T(8,128)(2,1)S(1)}, bf16[2,128,10...) custom-call(s32[7]{0:T(128)S(1)} %stack.32.refs_0_, ...), custom_call_target="tpu_custom_call" | custom-call | flops 5750000128 | bytes 1 | tf_op jit(solution)/shard_map/pallas_call | solution.py:79
  222.2 3.3 shard_map.193
  225.5 3.3 shard_map.194
  230.7 3.3 collective-permute-done.75.refs_3_
  234.3 2.5 collective-permute-start.77
  239.2 5.5 %shard_map.199 = (bf16[4,128,1024]{2,1,0:T(8,128)(2,1)S(1)}, bf16[4,128,1024]{2,1,0:T(8,128)(2,1)S(1)}, bf16[2,128,1024]{2,1,0:T(8,128)(2,1)S(1)}, bf16[2,128,10...) custom-call(s32[7]{0:T(128)S(1)} %stack.32.refs_0_, ...), custom_call_target="tpu_custom_call" | custom-call | flops 5750000128 | bytes 1 | tf_op jit(solution)/shard_map/pallas_call | solution.py:79
  244.7 5.1 %collective-permute-done.73.refs_5_ = bf16[160,1024]{1,0:T(8,128)(2,1)S(1)} collective-permute-done((bf16[160,1024]{1,0:T(8,128)(2,1)S(1)}, bf16[160,1024]{1,0:T(8,128)(2,1)S(1)}, u32[]{:S(2)}, u32[]{:S(2)}) %collective-permute-start.73) | collective-permute-done | bytes 327712 | tf_op jit(solution)/shard_map/ppermute | solution.py:36
  255.0 7.2 %shard_map.202 = (f32[160,1024]{1,0:T(8,128)S(1)}, bf16[160,1024]{1,0:T(8,128)(2,1)S(1)}, bf16[320,1536]{1,0:T(8,128)(2,1)S(1)}) custom-call(s32[7]{0:T(128)S(1)} %stack.32.refs_0_, bf16[160,1024]{1,0:T(8,128)(2,1)S(1)} %get-tuple-element.223.refs_1_.refs_3_, bf16[160,1024]{1,0:T(8,128)(2,1)S(1)} %collective-permute-done.76.refs_2_.refs_4_, ...), custom_call_target="tpu_custom_call" | custom-call | flops 8049999872 | bytes 1 | tf_op jit(solution)/shard_map/pallas_call | solution.py:79
  264.0 2.1 collective-permute-done.86.refs_3_
  271.0 4.1 %shard_map.204 = (bf16[4,128,1024]{2,1,0:T(8,128)(2,1)S(1)}, bf16[4,128,1024]{2,1,0:T(8,128)(2,1)S(1)}, bf16[2,128,1024]{2,1,0:T(8,128)(2,1)S(1)}, bf16[2,128,10...) custom-call(s32[7]{0:T(128)S(1)} %stack.32.refs_0_, ...), custom_call_target="tpu_custom_call" | custom-call | flops 5750000128 | bytes 1 | tf_op jit(solution)/shard_map/pallas_call | solution.py:79
  276.6 2.3 shard_map.188
  278.9 2.4 shard_map.205
  281.4 4.4 %collective-permute-done.84.refs_1_ = bf16[2,128,1024]{2,1,0:T(8,128)(2,1)S(1)} collective-permute-done((bf16[2,128,1024]{2,1,0:T(8,128)(2,1)S(1)}, bf16[2,128,1024]{2,1,0:T(8,128)(2,1)S(1)}, u32[]{:S(2)}, u32[]{:S(2)}) %collective-permute-start.84) | collective-permute-done | bytes 524320 | tf_op jit(solution)/shard_map/ppermute | solution.py:126
  285.9 2.8 collective-permute-done.88.refs_2_
  289.0 5.2 %collective-permute-done.83.refs_3_ = bf16[2,128,1024]{2,1,0:T(8,128)(2,1)S(1)} collective-permute-done((bf16[2,128,1024]{2,1,0:T(8,128)(2,1)S(1)}, bf16[2,128,1024]{2,1,0:T(8,128)(2,1)S(1)}, u32[]{:S(2)}, u32[]{:S(2)}) %collective-permute-start.83) | collective-permute-done | bytes 524320 | tf_op jit(solution)/shard_map/ppermute | solution.py:126
  300.6 7.8 %collective-permute-start.91 = (f32[24,1024]{1,0:T(8,128)S(1)}, f32[24,1024]{1,0:T(8,128)S(1)}, u32[]{:S(2)}, u32[]{:S(2)}) collective-permute-start(f32[24,1024]{1,0:T(8,128)S(1)} %shard_map.211), channel_id=1, source_target_pairs={{0,8},{1,9},{2,10},{3,11},{4,12},{5,13},{6,14},{7,15},{8,0},{9,1},... | collective-permute-start | bytes 294920 | tf_op jit(solution)/shard_map/ppermute | solution.py:36
  311.5 5.3 %collective-permute-done.90.refs_2_ = bf16[4,128,1024]{2,1,0:T(8,128)(2,1)S(1)} collective-permute-done((bf16[4,128,1024]{2,1,0:T(8,128)(2,1)S(1)}, bf16[4,128,1024]{2,1,0:T(8,128)(2,1)S(1)}, u32[]{:S(2)}, u32[]{:S(2)}) %collective-permute-start.90) | collective-permute-done | bytes 1048608 | tf_op jit(solution)/shard_map/ppermute | solution.py:126
  330.4 3.0 collective-permute-done.99
  333.6 2.5 collective-permute-done.93.refs_2_
  340.4 3.3 collective-permute-done.104
  343.7 2.7 collective-permute-start.105
  346.5 2.6 collective-permute-start.102
  352.3 3.1 collective-permute-done.106
  356.3 2.8 collective-permute-done.103.refs_4_
  362.2 2.8 collective-permute-done.108
  (283 shorter events, 124.3 us)
Async XLA Ops:
  7.1 14.6 %collective-permute-start.3 = (f32[24,128]{1,0:T(8,128)S(1)}, f32[24,128]{1,0:T(8,128)S(1)}, u32[]{:S(2)}, u32[]{:S(2)}) collective-permute-start(f32[24,128]{1,0:T(8,128)S(1)} %add.68), channel_id=1, source_target_pairs={{0,20},{1,21},{2,22},{3,23},{4,16},{5,17},{6,18},{7,19},{8,28},{9,... | collective-permute-start | bytes 36872 | tf_op jit(solution)/shard_map/ppermute | solution.py:36
  11.0 16.1 %collective-permute-start.11 = (bf16[128,1536]{1,0:T(8,128)(2,1)S(1)}, bf16[128,1536]{1,0:T(8,128)(2,1)S(1)}, u32[]{:S(2)}, u32[]{:S(2)}) collective-permute-start(bf16[128,1536]{1,0:T(8,128)(2,1)S(1)} %pad_maximum_fusion), channel_id=1, source_target_pairs={{0,1},{2,3},{4,5},{6,7},{9,8},{11,10},{13,12},{15,14},{16,17},{18,... | collective-permute-start | bytes 1179656 | tf_op jit(solution)/shard_map/ppermute | solution.py:40
  14.9 12.2 %collective-permute-start.12 = (bf16[128,1024]{1,0:T(8,128)(2,1)S(1)}, bf16[128,1024]{1,0:T(8,128)(2,1)S(1)}, u32[]{:S(2)}, u32[]{:S(2)}) collective-permute-start(bf16[128,1024]{1,0:T(8,128)(2,1)S(1)} %get-tuple-element.297), channel_id=1, source_target_pairs={{0,2},{2,0},{4,6},{6,4},{9,11},{11,9},{13,15},{15,13},{16,18},{18,... | collective-permute-start | bytes 786440 | tf_op jit(solution)/shard_map/ppermute | solution.py:40
  27.9 10.4 %collective-permute-start.15 = (bf16[128,2048]{1,0:T(8,128)(2,1)S(1)}, bf16[128,2048]{1,0:T(8,128)(2,1)S(1)}, u32[]{:S(2)}, u32[]{:S(2)}) collective-permute-start(bf16[128,2048]{1,0:T(8,128)(2,1)S(1)} %shard_map.156.refs_0_), channel_id=1, source_target_pairs={{0,20},{1,21},{2,22},{3,23},{4,16},{5,17},{6,18},{7,19},{8,104},{9... | collective-permute-start | bytes 1572872 | tf_op jit(solution)/shard_map/ppermute | solution.py:126
  47.0 14.9 %collective-permute-start.17 = (bf16[4,128,1024]{2,1,0:T(8,128)(2,1)S(1)}, bf16[4,128,1024]{2,1,0:T(8,128)(2,1)S(1)}, u32[]{:S(2)}, u32[]{:S(2)}) collective-permute-start(bf16[4,128,1024]{2,1,0:T(8,128)(2,1)S(1)} %shard_map.158.refs_4_.refs_5_), channel_id=1, source_target_pairs={{0,32},{1,33},{2,34},{3,35},{4,36},{5,37},{6,38},{7,39},{8,12},{9,... | collective-permute-start | bytes 3145736 | tf_op jit(solution)/shard_map/ppermute | solution.py:126
  48.9 14.8 %collective-permute-start.18 = (bf16[4,128,1024]{2,1,0:T(8,128)(2,1)S(1)}, bf16[4,128,1024]{2,1,0:T(8,128)(2,1)S(1)}, u32[]{:S(2)}, u32[]{:S(2)}) collective-permute-start(bf16[4,128,1024]{2,1,0:T(8,128)(2,1)S(1)} %shard_map.158.refs_4_.refs_5_), channel_id=1, source_target_pairs={{0,96},{1,97},{2,98},{3,99},{4,100},{5,101},{6,102},{7,103},{8,28}... | collective-permute-start | bytes 3145736 | tf_op jit(solution)/shard_map/ppermute | solution.py:126
  49.7 10.4 %collective-permute-start.22 = (bf16[128,1536]{1,0:T(8,128)(2,1)S(1)}, bf16[128,1536]{1,0:T(8,128)(2,1)S(1)}, u32[]{:S(2)}, u32[]{:S(2)}) collective-permute-start(bf16[128,1536]{1,0:T(8,128)(2,1)S(1)} %pad_maximum_fusion.1), channel_id=1, source_target_pairs={{0,1},{2,3},{4,5},{6,7},{9,8},{11,10},{13,12},{15,14},{16,17},{18,... | collective-permute-start | bytes 1179656 | tf_op jit(solution)/shard_map/ppermute | solution.py:40
  51.3 16.0 %collective-permute-start.1 = (bf16[160,1024]{1,0:T(8,128)(2,1)S(1)}, bf16[160,1024]{1,0:T(8,128)(2,1)S(1)}, u32[]{:S(2)}, u32[]{:S(2)}) collective-permute-start(bf16[160,1024]{1,0:T(8,128)(2,1)S(1)} %copy-done.4), channel_id=1, source_target_pairs={{1,8},{3,10},{5,12},{7,14},{8,1},{10,3},{12,5},{14,7},{17,24},{19,... | collective-permute-start | bytes 983048 | tf_op jit(solution)/shard_map/ppermute | solution.py:40
  58.7 10.7 %collective-permute-start.8 = (f32[24,1024]{1,0:T(8,128)S(1)}, f32[24,1024]{1,0:T(8,128)S(1)}, u32[]{:S(2)}, u32[]{:S(2)}) collective-permute-start(f32[24,1024]{1,0:T(8,128)S(1)} %add.70.refs_2_), channel_id=1, source_target_pairs={{0,1},{1,0},{2,3},{3,2},{4,5},{5,4},{6,7},{7,6},{8,9},{9,8},{10,11... | collective-permute-start | bytes 294920 | tf_op jit(solution)/shard_map/ppermute | solution.py:36
  63.8 12.4 %collective-permute-start.19 = (bf16[2,128,1024]{2,1,0:T(8,128)(2,1)S(1)}, bf16[2,128,1024]{2,1,0:T(8,128)(2,1)S(1)}, u32[]{:S(2)}, u32[]{:S(2)}) collective-permute-start(bf16[2,128,1024]{2,1,0:T(8,128)(2,1)S(1)} %get-tuple-element.146.refs_1_), channel_id=1, source_target_pairs={{0,96},{1,97},{2,98},{3,99},{4,100},{5,101},{6,102},{7,103},{8,28}... | collective-permute-start | bytes 1572872 | tf_op jit(solution)/shard_map/ppermute | solution.py:126
  64.6 12.6 %collective-permute-start.20 = (bf16[2,128,1024]{2,1,0:T(8,128)(2,1)S(1)}, bf16[2,128,1024]{2,1,0:T(8,128)(2,1)S(1)}, u32[]{:S(2)}, u32[]{:S(2)}) collective-permute-start(bf16[2,128,1024]{2,1,0:T(8,128)(2,1)S(1)} %get-tuple-element.147.refs_2_), channel_id=1, source_target_pairs={{0,32},{1,33},{2,34},{3,35},{4,36},{5,37},{6,38},{7,39},{8,12},{9,... | collective-permute-start | bytes 1572872 | tf_op jit(solution)/shard_map/ppermute | solution.py:126
  67.3 13.0 %collective-permute-start.23 = (bf16[128,2048]{1,0:T(8,128)(2,1)S(1)}, bf16[128,2048]{1,0:T(8,128)(2,1)S(1)}, u32[]{:S(2)}, u32[]{:S(2)}) collective-permute-start(bf16[128,2048]{1,0:T(8,128)(2,1)S(1)} %shard_map.162.refs_0_), channel_id=1, source_target_pairs={{0,4},{1,5},{2,6},{3,7},{4,0},{5,1},{6,2},{7,3},{8,40},{9,41},{10,... | collective-permute-start | bytes 1572872 | tf_op jit(solution)/shard_map/ppermute | solution.py:126
  69.4 11.9 %collective-permute-start.24 = (bf16[128,2048]{1,0:T(8,128)(2,1)S(1)}, bf16[128,2048]{1,0:T(8,128)(2,1)S(1)}, u32[]{:S(2)}, u32[]{:S(2)}) collective-permute-start(bf16[128,2048]{1,0:T(8,128)(2,1)S(1)} %shard_map.162.refs_0_), channel_id=1, source_target_pairs={{0,20},{1,21},{2,22},{3,23},{4,16},{5,17},{6,18},{7,19},{8,104},{9... | collective-permute-start | bytes 1572872 | tf_op jit(solution)/shard_map/ppermute | solution.py:126
  76.2 11.3 %collective-permute-start.26 = (f32[160,1024]{1,0:T(8,128)S(1)}, f32[160,1024]{1,0:T(8,128)S(1)}, u32[]{:S(2)}, u32[]{:S(2)}) collective-permute-start(f32[160,1024]{1,0:T(8,128)S(1)} %copy-done.3), channel_id=1, source_target_pairs={{1,8},{3,10},{5,12},{7,14},{8,1},{10,3},{12,5},{14,7},{17,24},{19,... | collective-permute-start | bytes 1966088 | tf_op jit(solution)/shard_map/ppermute | solution.py:40
  77.3 19.5 %collective-permute-start.28 = (bf16[4,128,1024]{2,1,0:T(8,128)(2,1)S(1)}, bf16[4,128,1024]{2,1,0:T(8,128)(2,1)S(1)}, u32[]{:S(2)}, u32[]{:S(2)}) collective-permute-start(bf16[4,128,1024]{2,1,0:T(8,128)(2,1)S(1)} %shard_map.160.refs_9_.refs_4_), channel_id=1, source_target_pairs={{0,32},{1,33},{2,34},{3,35},{4,36},{5,37},{6,38},{7,39},{8,12},{9,... | collective-permute-start | bytes 3145736 | tf_op jit(solution)/shard_map/ppermute | solution.py:126
  80.3 16.5 %collective-permute-start.29 = (bf16[4,128,1024]{2,1,0:T(8,128)(2,1)S(1)}, bf16[4,128,1024]{2,1,0:T(8,128)(2,1)S(1)}, u32[]{:S(2)}, u32[]{:S(2)}) collective-permute-start(bf16[4,128,1024]{2,1,0:T(8,128)(2,1)S(1)} %shard_map.160.refs_9_.refs_4_), channel_id=1, source_target_pairs={{0,96},{1,97},{2,98},{3,99},{4,100},{5,101},{6,102},{7,103},{8,28}... | collective-permute-start | bytes 3145736 | tf_op jit(solution)/shard_map/ppermute | solution.py:126
  91.1 13.6 %collective-permute-start.32 = (bf16[160,1024]{1,0:T(8,128)(2,1)S(1)}, bf16[160,1024]{1,0:T(8,128)(2,1)S(1)}, u32[]{:S(2)}, u32[]{:S(2)}) collective-permute-start(bf16[160,1024]{1,0:T(8,128)(2,1)S(1)} %get-tuple-element.155.refs_2_.refs_1_.refs_5_), channel_id=1, source_target_pairs={{0,3},{1,2},{2,1},{3,0},{4,7},{5,6},{6,5},{7,4},{8,11},{9,10},{10,... | collective-permute-start | bytes 983048 | tf_op jit(solution)/shard_map/ppermute | solution.py:36
  96.8 15.5 %collective-permute-start.30 = (bf16[2,128,1024]{2,1,0:T(8,128)(2,1)S(1)}, bf16[2,128,1024]{2,1,0:T(8,128)(2,1)S(1)}, u32[]{:S(2)}, u32[]{:S(2)}) collective-permute-start(bf16[2,128,1024]{2,1,0:T(8,128)(2,1)S(1)} %get-tuple-element.156), channel_id=1, source_target_pairs={{0,96},{1,97},{2,98},{3,99},{4,100},{5,101},{6,102},{7,103},{8,28}... | collective-permute-start | bytes 1572872 | tf_op jit(solution)/shard_map/ppermute | solution.py:126
  97.7 14.7 %collective-permute-start.31 = (bf16[2,128,1024]{2,1,0:T(8,128)(2,1)S(1)}, bf16[2,128,1024]{2,1,0:T(8,128)(2,1)S(1)}, u32[]{:S(2)}, u32[]{:S(2)}) collective-permute-start(bf16[2,128,1024]{2,1,0:T(8,128)(2,1)S(1)} %get-tuple-element.157), channel_id=1, source_target_pairs={{0,32},{1,33},{2,34},{3,35},{4,36},{5,37},{6,38},{7,39},{8,12},{9,... | collective-permute-start | bytes 1572872 | tf_op jit(solution)/shard_map/ppermute | solution.py:126
  112.4 14.9 %collective-permute-start.40 = (bf16[4,128,1024]{2,1,0:T(8,128)(2,1)S(1)}, bf16[4,128,1024]{2,1,0:T(8,128)(2,1)S(1)}, u32[]{:S(2)}, u32[]{:S(2)}) collective-permute-start(bf16[4,128,1024]{2,1,0:T(8,128)(2,1)S(1)} %shard_map.172.refs_4_.refs_5_), channel_id=1, source_target_pairs={{0,32},{1,33},{2,34},{3,35},{4,36},{5,37},{6,38},{7,39},{8,12},{9,... | collective-permute-start | bytes 3145736 | tf_op jit(solution)/shard_map/ppermute | solution.py:126
  113.3 14.8 %collective-permute-start.41 = (bf16[4,128,1024]{2,1,0:T(8,128)(2,1)S(1)}, bf16[4,128,1024]{2,1,0:T(8,128)(2,1)S(1)}, u32[]{:S(2)}, u32[]{:S(2)}) collective-permute-start(bf16[4,128,1024]{2,1,0:T(8,128)(2,1)S(1)} %shard_map.172.refs_4_.refs_5_), channel_id=1, source_target_pairs={{0,96},{1,97},{2,98},{3,99},{4,100},{5,101},{6,102},{7,103},{8,28}... | collective-permute-start | bytes 3145736 | tf_op jit(solution)/shard_map/ppermute | solution.py:126
  121.8 13.2 %collective-permute-start.36 = (bf16[160,1024]{1,0:T(8,128)(2,1)S(1)}, bf16[160,1024]{1,0:T(8,128)(2,1)S(1)}, u32[]{:S(2)}, u32[]{:S(2)}) collective-permute-start(bf16[160,1024]{1,0:T(8,128)(2,1)S(1)} %get-tuple-element.160), channel_id=1, source_target_pairs={{0,8},{1,9},{2,10},{3,11},{4,12},{5,13},{6,14},{7,15},{8,0},{9,1},... | collective-permute-start | bytes 983048 | tf_op jit(solution)/shard_map/ppermute | solution.py:36
  122.2 12.8 %collective-permute-start.38 = (bf16[160,1024]{1,0:T(8,128)(2,1)S(1)}, bf16[160,1024]{1,0:T(8,128)(2,1)S(1)}, u32[]{:S(2)}, u32[]{:S(2)}) collective-permute-start(bf16[160,1024]{1,0:T(8,128)(2,1)S(1)} %shard_map.170), channel_id=1, source_target_pairs={{0,3},{1,2},{2,1},{3,0},{4,7},{5,6},{6,5},{7,4},{8,11},{9,10},{10,... | collective-permute-start | bytes 983048 | tf_op jit(solution)/shard_map/ppermute | solution.py:36
  128.1 12.5 %collective-permute-start.42 = (bf16[2,128,1024]{2,1,0:T(8,128)(2,1)S(1)}, bf16[2,128,1024]{2,1,0:T(8,128)(2,1)S(1)}, u32[]{:S(2)}, u32[]{:S(2)}) collective-permute-start(bf16[2,128,1024]{2,1,0:T(8,128)(2,1)S(1)} %get-tuple-element.164), channel_id=1, source_target_pairs={{0,96},{1,97},{2,98},{3,99},{4,100},{5,101},{6,102},{7,103},{8,28}... | collective-permute-start | bytes 1572872 | tf_op jit(solution)/shard_map/ppermute | solution.py:126
  129.0 11.6 %collective-permute-start.43 = (bf16[2,128,1024]{2,1,0:T(8,128)(2,1)S(1)}, bf16[2,128,1024]{2,1,0:T(8,128)(2,1)S(1)}, u32[]{:S(2)}, u32[]{:S(2)}) collective-permute-start(bf16[2,128,1024]{2,1,0:T(8,128)(2,1)S(1)} %get-tuple-element.165), channel_id=1, source_target_pairs={{0,32},{1,33},{2,34},{3,35},{4,36},{5,37},{6,38},{7,39},{8,12},{9,... | collective-permute-start | bytes 1572872 | tf_op jit(solution)/shard_map/ppermute | solution.py:126
  137.2 13.0 %collective-permute-start.45 = (bf16[160,1024]{1,0:T(8,128)(2,1)S(1)}, bf16[160,1024]{1,0:T(8,128)(2,1)S(1)}, u32[]{:S(2)}, u32[]{:S(2)}) collective-permute-start(bf16[160,1024]{1,0:T(8,128)(2,1)S(1)} %get-tuple-element.153.refs_4_.refs_1_), channel_id=1, source_target_pairs={{0,8},{1,9},{2,10},{3,11},{4,12},{5,13},{6,14},{7,15},{8,0},{9,1},... | collective-permute-start | bytes 983048 | tf_op jit(solution)/shard_map/ppermute | solution.py:36
  140.7 16.1 %collective-permute-start.49 = (bf16[4,128,1024]{2,1,0:T(8,128)(2,1)S(1)}, bf16[4,128,1024]{2,1,0:T(8,128)(2,1)S(1)}, u32[]{:S(2)}, u32[]{:S(2)}) collective-permute-start(bf16[4,128,1024]{2,1,0:T(8,128)(2,1)S(1)} %shard_map.174.refs_9_.refs_4_), channel_id=1, source_target_pairs={{0,32},{1,33},{2,34},{3,35},{4,36},{5,37},{6,38},{7,39},{8,12},{9,... | collective-permute-start | bytes 3145736 | tf_op jit(solution)/shard_map/ppermute | solution.py:126
  142.7 14.8 %collective-permute-start.50 = (bf16[4,128,1024]{2,1,0:T(8,128)(2,1)S(1)}, bf16[4,128,1024]{2,1,0:T(8,128)(2,1)S(1)}, u32[]{:S(2)}, u32[]{:S(2)}) collective-permute-start(bf16[4,128,1024]{2,1,0:T(8,128)(2,1)S(1)} %shard_map.174.refs_9_.refs_4_), channel_id=1, source_target_pairs={{0,96},{1,97},{2,98},{3,99},{4,100},{5,101},{6,102},{7,103},{8,28}... | collective-permute-start | bytes 3145736 | tf_op jit(solution)/shard_map/ppermute | solution.py:126
  153.8 11.0 %collective-permute-start.53 = (bf16[160,1024]{1,0:T(8,128)(2,1)S(1)}, bf16[160,1024]{1,0:T(8,128)(2,1)S(1)}, u32[]{:S(2)}, u32[]{:S(2)}) collective-permute-start(bf16[160,1024]{1,0:T(8,128)(2,1)S(1)} %get-tuple-element.169.refs_2_.refs_1_.refs_5_), channel_id=1, source_target_pairs={{0,3},{1,2},{2,1},{3,0},{4,7},{5,6},{6,5},{7,4},{8,11},{9,10},{10,... | collective-permute-start | bytes 983048 | tf_op jit(solution)/shard_map/ppermute | solution.py:36
  164.8 10.3 %collective-permute-start.48 = (bf16[160,1024]{1,0:T(8,128)(2,1)S(1)}, bf16[160,1024]{1,0:T(8,128)(2,1)S(1)}, u32[]{:S(2)}, u32[]{:S(2)}) collective-permute-start(bf16[160,1024]{1,0:T(8,128)(2,1)S(1)} %get-tuple-element.169.refs_2_.refs_1_.refs_5_), channel_id=1, source_target_pairs={{0,8},{1,9},{2,10},{3,11},{4,12},{5,13},{6,14},{7,15},{8,0},{9,1},... | collective-permute-start | bytes 983048 | tf_op jit(solution)/shard_map/ppermute | solution.py:36
  181.9 9.6 %collective-permute-start.55 = (bf16[160,1024]{1,0:T(8,128)(2,1)S(1)}, bf16[160,1024]{1,0:T(8,128)(2,1)S(1)}, u32[]{:S(2)}, u32[]{:S(2)}) collective-permute-start(bf16[160,1024]{1,0:T(8,128)(2,1)S(1)} %get-tuple-element.179), channel_id=1, source_target_pairs={{0,8},{1,9},{2,10},{3,11},{4,12},{5,13},{6,14},{7,15},{8,0},{9,1},... | collective-permute-start | bytes 983048 | tf_op jit(solution)/shard_map/ppermute | solution.py:36
  182.6 11.4 %collective-permute-start.57 = (bf16[160,1024]{1,0:T(8,128)(2,1)S(1)}, bf16[160,1024]{1,0:T(8,128)(2,1)S(1)}, u32[]{:S(2)}, u32[]{:S(2)}) collective-permute-start(bf16[160,1024]{1,0:T(8,128)(2,1)S(1)} %shard_map.182.refs_13_), channel_id=1, source_target_pairs={{0,3},{1,2},{2,1},{3,0},{4,7},{5,6},{6,5},{7,4},{8,11},{9,10},{10,... | collective-permute-start | bytes 983048 | tf_op jit(solution)/shard_map/ppermute | solution.py:36
  195.7 10.1 %collective-permute-start.64 = (bf16[2,128,1024]{2,1,0:T(8,128)(2,1)S(1)}, bf16[2,128,1024]{2,1,0:T(8,128)(2,1)S(1)}, u32[]{:S(2)}, u32[]{:S(2)}) collective-permute-start(bf16[2,128,1024]{2,1,0:T(8,128)(2,1)S(1)} %get-tuple-element.197), channel_id=1, source_target_pairs={{0,32},{1,33},{2,34},{3,35},{4,36},{5,37},{6,38},{7,39},{8,12},{9,... | collective-permute-start | bytes 1572872 | tf_op jit(solution)/shard_map/ppermute | solution.py:126
  207.8 21.6 %collective-permute-start.71 = (bf16[4,128,1024]{2,1,0:T(8,128)(2,1)S(1)}, bf16[4,128,1024]{2,1,0:T(8,128)(2,1)S(1)}, u32[]{:S(2)}, u32[]{:S(2)}) collective-permute-start(bf16[4,128,1024]{2,1,0:T(8,128)(2,1)S(1)} %get-tuple-element.199.refs_5_), channel_id=1, source_target_pairs={{0,32},{1,33},{2,34},{3,35},{4,36},{5,37},{6,38},{7,39},{8,12},{9,... | collective-permute-start | bytes 3145736 | tf_op jit(solution)/shard_map/ppermute | solution.py:126
  210.8 10.1 %collective-permute-start.66 = (bf16[160,1024]{1,0:T(8,128)(2,1)S(1)}, bf16[160,1024]{1,0:T(8,128)(2,1)S(1)}, u32[]{:S(2)}, u32[]{:S(2)}) collective-permute-start(bf16[160,1024]{1,0:T(8,128)(2,1)S(1)} %get-tuple-element.201.refs_1_.refs_7_), channel_id=1, source_target_pairs={{0,8},{1,9},{2,10},{3,11},{4,12},{5,13},{6,14},{7,15},{8,0},{9,1},... | collective-permute-start | bytes 983048 | tf_op jit(solution)/shard_map/ppermute | solution.py:36
  210.9 11.3 %collective-permute-start.68 = (bf16[160,1024]{1,0:T(8,128)(2,1)S(1)}, bf16[160,1024]{1,0:T(8,128)(2,1)S(1)}, u32[]{:S(2)}, u32[]{:S(2)}) collective-permute-start(bf16[160,1024]{1,0:T(8,128)(2,1)S(1)} %get-tuple-element.201.refs_1_.refs_7_), channel_id=1, source_target_pairs={{0,3},{1,2},{2,1},{3,0},{4,7},{5,6},{6,5},{7,4},{8,11},{9,10},{10,... | collective-permute-start | bytes 983048 | tf_op jit(solution)/shard_map/ppermute | solution.py:36
  213.4 15.9 %collective-permute-start.72 = (bf16[4,128,1024]{2,1,0:T(8,128)(2,1)S(1)}, bf16[4,128,1024]{2,1,0:T(8,128)(2,1)S(1)}, u32[]{:S(2)}, u32[]{:S(2)}) collective-permute-start(bf16[4,128,1024]{2,1,0:T(8,128)(2,1)S(1)} %get-tuple-element.208), channel_id=1, source_target_pairs={{0,96},{1,97},{2,98},{3,99},{4,100},{5,101},{6,102},{7,103},{8,28}... | collective-permute-start | bytes 3145736 | tf_op jit(solution)/shard_map/ppermute | solution.py:126
  218.9 11.8 %collective-permute-start.74 = (bf16[2,128,1024]{2,1,0:T(8,128)(2,1)S(1)}, bf16[2,128,1024]{2,1,0:T(8,128)(2,1)S(1)}, u32[]{:S(2)}, u32[]{:S(2)}) collective-permute-start(bf16[2,128,1024]{2,1,0:T(8,128)(2,1)S(1)} %get-tuple-element.218), channel_id=1, source_target_pairs={{0,32},{1,33},{2,34},{3,35},{4,36},{5,37},{6,38},{7,39},{8,12},{9,... | collective-permute-start | bytes 1572872 | tf_op jit(solution)/shard_map/ppermute | solution.py:126
  220.9 13.1 %collective-permute-start.75 = (bf16[2,128,1024]{2,1,0:T(8,128)(2,1)S(1)}, bf16[2,128,1024]{2,1,0:T(8,128)(2,1)S(1)}, u32[]{:S(2)}, u32[]{:S(2)}) collective-permute-start(bf16[2,128,1024]{2,1,0:T(8,128)(2,1)S(1)} %get-tuple-element.219), channel_id=1, source_target_pairs={{0,96},{1,97},{2,98},{3,99},{4,100},{5,101},{6,102},{7,103},{8,28}... | collective-permute-start | bytes 1572872 | tf_op jit(solution)/shard_map/ppermute | solution.py:126
  234.3 19.1 %collective-permute-start.77 = (bf16[4,128,1024]{2,1,0:T(8,128)(2,1)S(1)}, bf16[4,128,1024]{2,1,0:T(8,128)(2,1)S(1)}, u32[]{:S(2)}, u32[]{:S(2)}) collective-permute-start(bf16[4,128,1024]{2,1,0:T(8,128)(2,1)S(1)} %get-tuple-element.220.refs_14_), channel_id=1, source_target_pairs={{0,32},{1,33},{2,34},{3,35},{4,36},{5,37},{6,38},{7,39},{8,12},{9,... | collective-permute-start | bytes 3145736 | tf_op jit(solution)/shard_map/ppermute | solution.py:126
  236.9 17.8 %collective-permute-start.78 = (bf16[4,128,1024]{2,1,0:T(8,128)(2,1)S(1)}, bf16[4,128,1024]{2,1,0:T(8,128)(2,1)S(1)}, u32[]{:S(2)}, u32[]{:S(2)}) collective-permute-start(bf16[4,128,1024]{2,1,0:T(8,128)(2,1)S(1)} %get-tuple-element.227), channel_id=1, source_target_pairs={{0,96},{1,97},{2,98},{3,99},{4,100},{5,101},{6,102},{7,103},{8,28}... | collective-permute-start | bytes 3145736 | tf_op jit(solution)/shard_map/ppermute | solution.py:126
  238.1 13.5 %collective-permute-start.59 = (bf16[160,1024]{1,0:T(8,128)(2,1)S(1)}, bf16[160,1024]{1,0:T(8,128)(2,1)S(1)}, u32[]{:S(2)}, u32[]{:S(2)}) collective-permute-start(bf16[160,1024]{1,0:T(8,128)(2,1)S(1)} %shard_map.186), channel_id=1, source_target_pairs={{0,8},{1,9},{2,10},{3,11},{4,12},{5,13},{6,14},{7,15},{8,0},{9,1},... | collective-permute-start | bytes 983048 | tf_op jit(solution)/shard_map/ppermute | solution.py:36
  238.7 11.1 %collective-permute-start.73 = (bf16[160,1024]{1,0:T(8,128)(2,1)S(1)}, bf16[160,1024]{1,0:T(8,128)(2,1)S(1)}, u32[]{:S(2)}, u32[]{:S(2)}) collective-permute-start(bf16[160,1024]{1,0:T(8,128)(2,1)S(1)} %shard_map.196.refs_4_.refs_13_), channel_id=1, source_target_pairs={{0,3},{1,2},{2,1},{3,0},{4,7},{5,6},{6,5},{7,4},{8,11},{9,10},{10,... | collective-permute-start | bytes 983048 | tf_op jit(solution)/shard_map/ppermute | solution.py:36
  251.7 17.7 %collective-permute-start.80 = (bf16[2,128,1024]{2,1,0:T(8,128)(2,1)S(1)}, bf16[2,128,1024]{2,1,0:T(8,128)(2,1)S(1)}, u32[]{:S(2)}, u32[]{:S(2)}) collective-permute-start(bf16[2,128,1024]{2,1,0:T(8,128)(2,1)S(1)} %get-tuple-element.233), channel_id=1, source_target_pairs={{0,20},{1,21},{2,22},{3,23},{4,16},{5,17},{6,18},{7,19},{8,104},{9... | collective-permute-start | bytes 1572872 | tf_op jit(solution)/shard_map/ppermute | solution.py:126
  252.7 10.3 %collective-permute-start.85 = (bf16[2,128,1024]{2,1,0:T(8,128)(2,1)S(1)}, bf16[2,128,1024]{2,1,0:T(8,128)(2,1)S(1)}, u32[]{:S(2)}, u32[]{:S(2)}) collective-permute-start(bf16[2,128,1024]{2,1,0:T(8,128)(2,1)S(1)} %get-tuple-element.245), channel_id=1, source_target_pairs={{0,32},{1,33},{2,34},{3,35},{4,36},{5,37},{6,38},{7,39},{8,12},{9,... | collective-permute-start | bytes 1572872 | tf_op jit(solution)/shard_map/ppermute | solution.py:126
  253.4 12.7 %collective-permute-start.86 = (bf16[2,128,1024]{2,1,0:T(8,128)(2,1)S(1)}, bf16[2,128,1024]{2,1,0:T(8,128)(2,1)S(1)}, u32[]{:S(2)}, u32[]{:S(2)}) collective-permute-start(bf16[2,128,1024]{2,1,0:T(8,128)(2,1)S(1)} %get-tuple-element.246), channel_id=1, source_target_pairs={{0,96},{1,97},{2,98},{3,99},{4,100},{5,101},{6,102},{7,103},{8,28}... | collective-permute-start | bytes 1572872 | tf_op jit(solution)/shard_map/ppermute | solution.py:126
  262.4 12.7 %collective-permute-start.58 = (bf16[160,1024]{1,0:T(8,128)(2,1)S(1)}, bf16[160,1024]{1,0:T(8,128)(2,1)S(1)}, u32[]{:S(2)}, u32[]{:S(2)}) collective-permute-start(bf16[160,1024]{1,0:T(8,128)(2,1)S(1)} %shard_map.185), channel_id=1, source_target_pairs={{0,8},{1,9},{2,10},{3,11},{4,12},{5,13},{6,14},{7,15},{8,0},{9,1},... | collective-permute-start | bytes 983048 | tf_op jit(solution)/shard_map/ppermute | solution.py:36
  263.0 12.9 %collective-permute-start.60 = (bf16[160,1024]{1,0:T(8,128)(2,1)S(1)}, bf16[160,1024]{1,0:T(8,128)(2,1)S(1)}, u32[]{:S(2)}, u32[]{:S(2)}) collective-permute-start(bf16[160,1024]{1,0:T(8,128)(2,1)S(1)} %shard_map.187.refs_11_), channel_id=1, source_target_pairs={{0,3},{1,2},{2,1},{3,0},{4,7},{5,6},{6,5},{7,4},{8,11},{9,10},{10,... | collective-permute-start | bytes 983048 | tf_op jit(solution)/shard_map/ppermute | solution.py:36
  266.4 19.4 %collective-permute-start.87 = (bf16[4,128,1024]{2,1,0:T(8,128)(2,1)S(1)}, bf16[4,128,1024]{2,1,0:T(8,128)(2,1)S(1)}, u32[]{:S(2)}, u32[]{:S(2)}) collective-permute-start(bf16[4,128,1024]{2,1,0:T(8,128)(2,1)S(1)} %get-tuple-element.247), channel_id=1, source_target_pairs={{0,32},{1,33},{2,34},{3,35},{4,36},{5,37},{6,38},{7,39},{8,12},{9,... | collective-permute-start | bytes 3145736 | tf_op jit(solution)/shard_map/ppermute | solution.py:126
  268.4 20.2 %collective-permute-start.88 = (bf16[4,128,1024]{2,1,0:T(8,128)(2,1)S(1)}, bf16[4,128,1024]{2,1,0:T(8,128)(2,1)S(1)}, u32[]{:S(2)}, u32[]{:S(2)}) collective-permute-start(bf16[4,128,1024]{2,1,0:T(8,128)(2,1)S(1)} %get-tuple-element.248), channel_id=1, source_target_pairs={{0,96},{1,97},{2,98},{3,99},{4,100},{5,101},{6,102},{7,103},{8,28}... | collective-permute-start | bytes 3145736 | tf_op jit(solution)/shard_map/ppermute | solution.py:126
  269.6 16.1 %collective-permute-start.84 = (bf16[2,128,1024]{2,1,0:T(8,128)(2,1)S(1)}, bf16[2,128,1024]{2,1,0:T(8,128)(2,1)S(1)}, u32[]{:S(2)}, u32[]{:S(2)}) collective-permute-start(bf16[2,128,1024]{2,1,0:T(8,128)(2,1)S(1)} %get-tuple-element.241), channel_id=1, source_target_pairs={{0,20},{1,21},{2,22},{3,23},{4,16},{5,17},{6,18},{7,19},{8,104},{9... | collective-permute-start | bytes 1572872 | tf_op jit(solution)/shard_map/ppermute | solution.py:126
  275.1 13.9 %collective-permute-start.82 = (bf16[2,128,1024]{2,1,0:T(8,128)(2,1)S(1)}, bf16[2,128,1024]{2,1,0:T(8,128)(2,1)S(1)}, u32[]{:S(2)}, u32[]{:S(2)}) collective-permute-start(bf16[2,128,1024]{2,1,0:T(8,128)(2,1)S(1)} %get-tuple-element.239), channel_id=1, source_target_pairs={{0,32},{1,33},{2,34},{3,35},{4,36},{5,37},{6,38},{7,39},{8,12},{9,... | collective-permute-start | bytes 1572872 | tf_op jit(solution)/shard_map/ppermute | solution.py:126
  275.9 18.4 %collective-permute-start.83 = (bf16[2,128,1024]{2,1,0:T(8,128)(2,1)S(1)}, bf16[2,128,1024]{2,1,0:T(8,128)(2,1)S(1)}, u32[]{:S(2)}, u32[]{:S(2)}) collective-permute-start(bf16[2,128,1024]{2,1,0:T(8,128)(2,1)S(1)} %get-tuple-element.240), channel_id=1, source_target_pairs={{0,96},{1,97},{2,98},{3,99},{4,100},{5,101},{6,102},{7,103},{8,28}... | collective-permute-start | bytes 1572872 | tf_op jit(solution)/shard_map/ppermute | solution.py:126
  294.5 17.0 %collective-permute-start.89 = (bf16[4,128,1024]{2,1,0:T(8,128)(2,1)S(1)}, bf16[4,128,1024]{2,1,0:T(8,128)(2,1)S(1)}, u32[]{:S(2)}, u32[]{:S(2)}) collective-permute-start(bf16[4,128,1024]{2,1,0:T(8,128)(2,1)S(1)} %get-tuple-element.250), channel_id=1, source_target_pairs={{0,32},{1,33},{2,34},{3,35},{4,36},{5,37},{6,38},{7,39},{8,12},{9,... | collective-permute-start | bytes 3145736 | tf_op jit(solution)/shard_map/ppermute | solution.py:126
  296.4 20.4 %collective-permute-start.90 = (bf16[4,128,1024]{2,1,0:T(8,128)(2,1)S(1)}, bf16[4,128,1024]{2,1,0:T(8,128)(2,1)S(1)}, u32[]{:S(2)}, u32[]{:S(2)}) collective-permute-start(bf16[4,128,1024]{2,1,0:T(8,128)(2,1)S(1)} %get-tuple-element.251), channel_id=1, source_target_pairs={{0,96},{1,97},{2,98},{3,99},{4,100},{5,101},{6,102},{7,103},{8,28}... | collective-permute-start | bytes 3145736 | tf_op jit(solution)/shard_map/ppermute | solution.py:126
  297.9 12.1 %collective-permute-start.81 = (f32[160,1024]{1,0:T(8,128)S(1)}, f32[160,1024]{1,0:T(8,128)S(1)}, u32[]{:S(2)}, u32[]{:S(2)}) collective-permute-start(f32[160,1024]{1,0:T(8,128)S(1)} %get-tuple-element.236.refs_1_.refs_6_), channel_id=1, source_target_pairs={{1,8},{3,10},{5,12},{7,14},{8,1},{10,3},{12,5},{14,7},{17,24},{19,... | collective-permute-start | bytes 1966088 | tf_op jit(solution)/shard_map/ppermute | solution.py:40
  298.6 22.3 %collective-permute-start.95 = (bf16[2,128,1024]{2,1,0:T(8,128)(2,1)S(1)}, bf16[2,128,1024]{2,1,0:T(8,128)(2,1)S(1)}, u32[]{:S(2)}, u32[]{:S(2)}) collective-permute-start(bf16[2,128,1024]{2,1,0:T(8,128)(2,1)S(1)} %get-tuple-element.265), channel_id=1, source_target_pairs={{0,20},{1,21},{2,22},{3,23},{4,16},{5,17},{6,18},{7,19},{8,104},{9... | collective-permute-start | bytes 1572872 | tf_op jit(solution)/shard_map/ppermute | solution.py:126
  320.4 10.0 %collective-permute-start.97 = (bf16[128,1024]{1,0:T(8,128)(2,1)S(1)}, bf16[128,1024]{1,0:T(8,128)(2,1)S(1)}, u32[]{:S(2)}, u32[]{:S(2)}) collective-permute-start(bf16[128,1024]{1,0:T(8,128)(2,1)S(1)} %get-tuple-element.268), channel_id=1, source_target_pairs={{0,4},{1,5},{2,6},{3,7},{4,0},{5,1},{6,2},{7,3},{8,40},{9,41},{10,... | collective-permute-start | bytes 786440 | tf_op jit(solution)/shard_map/ppermute | solution.py:126
  321.0 12.5 %collective-permute-start.96 = (bf16[128,1024]{1,0:T(8,128)(2,1)S(1)}, bf16[128,1024]{1,0:T(8,128)(2,1)S(1)}, u32[]{:S(2)}, u32[]{:S(2)}) collective-permute-start(bf16[128,1024]{1,0:T(8,128)(2,1)S(1)} %get-tuple-element.267), channel_id=1, source_target_pairs={{0,4},{1,5},{2,6},{3,7},{4,0},{5,1},{6,2},{7,3},{8,40},{9,41},{10,... | collective-permute-start | bytes 786440 | tf_op jit(solution)/shard_map/ppermute | solution.py:126
  322.6 13.4 %collective-permute-start.93 = (bf16[128,1024]{1,0:T(8,128)(2,1)S(1)}, bf16[128,1024]{1,0:T(8,128)(2,1)S(1)}, u32[]{:S(2)}, u32[]{:S(2)}) collective-permute-start(bf16[128,1024]{1,0:T(8,128)(2,1)S(1)} %get-tuple-element.263), channel_id=1, source_target_pairs={{0,16},{1,17},{2,18},{3,19},{4,20},{5,21},{6,22},{7,23},{8,72},{9,... | collective-permute-start | bytes 786440 | tf_op jit(solution)/shard_map/ppermute | solution.py:126
  324.7 11.3 %collective-permute-start.94 = (bf16[128,1024]{1,0:T(8,128)(2,1)S(1)}, bf16[128,1024]{1,0:T(8,128)(2,1)S(1)}, u32[]{:S(2)}, u32[]{:S(2)}) collective-permute-start(bf16[128,1024]{1,0:T(8,128)(2,1)S(1)} %get-tuple-element.264), channel_id=1, source_target_pairs={{0,20},{1,21},{2,22},{3,23},{4,16},{5,17},{6,18},{7,19},{8,104},{9... | collective-permute-start | bytes 786440 | tf_op jit(solution)/shard_map/ppermute | solution.py:126
  338.2 20.8 %collective-permute-start.101 = (bf16[128,3072]{1,0:T(8,128)(2,1)S(1)}, bf16[128,3072]{1,0:T(8,128)(2,1)S(1)}, u32[]{:S(2)}, u32[]{:S(2)}) collective-permute-start(bf16[128,3072]{1,0:T(8,128)(2,1)S(1)} %get-tuple-element.270.refs_1_), channel_id=1, source_target_pairs={{1,0},{3,2},{5,4},{7,6},{8,9},{10,11},{12,13},{14,15},{17,16},{19,... | collective-permute-start | bytes 2359304 | tf_op jit(solution)/shard_map/ppermute | solution.py:40
  346.5 9.8 %collective-permute-start.102 = (bf16[128,1024]{1,0:T(8,128)(2,1)S(1)}, bf16[128,1024]{1,0:T(8,128)(2,1)S(1)}, u32[]{:S(2)}, u32[]{:S(2)}) collective-permute-start(bf16[128,1024]{1,0:T(8,128)(2,1)S(1)} %get-tuple-element.271), channel_id=1, source_target_pairs={{0,2},{2,0},{4,6},{6,4},{9,11},{11,9},{13,15},{15,13},{16,18},{18,... | collective-permute-start | bytes 786440 | tf_op jit(solution)/shard_map/ppermute | solution.py:40
  349.1 9.9 %collective-permute-start.103 = (bf16[128,1024]{1,0:T(8,128)(2,1)S(1)}, bf16[128,1024]{1,0:T(8,128)(2,1)S(1)}, u32[]{:S(2)}, u32[]{:S(2)}) collective-permute-start(bf16[128,1024]{1,0:T(8,128)(2,1)S(1)} %get-tuple-element.271), channel_id=1, source_target_pairs={{1,2},{3,0},{5,6},{7,4},{8,11},{10,9},{12,15},{14,13},{17,18},{19,... | collective-permute-start | bytes 786440 | tf_op jit(solution)/shard_map/ppermute | solution.py:40
  (53 other events, 310.7 us)
